TPU v7x, 32 devices: a whole 2x2x4 slice. The times are simulated.
32 devices in a mesh: grp: 8 (over z, x), blk: 4 (over y, core).
Axes of the slice: x: 2, y: 2, z: 4, core: 2. Of those that a mesh axis runs over, the one named last changes fastest.
Arguments:
- embeddings: bfloat16 [49152, 768], P(('grp', 'blk')), may hold values from -6 to 6
- route: int32 [49152], P(('grp', 'blk')), may hold values from 0 to 49151, as said below
- cluster: int32 [8, 6144], P('grp', 'blk'), may hold values from 0 to 3, never falling along the last dimension, each value on 1 to 3072 neighbouring positions
Outputs:
- best_cosine: float32 [49152], P(('grp', 'blk'))
Inputs may be any that keep to these rules, and one draw needn't show every extreme that they name: route is a permutation of all slots; the 1536 rows of each device are sent to every device's 1536 slots in exactly 48 cases, and which rows and which slots is drawn from the seed. Within each family the cluster numbers never fall along the slots, every cluster number occurs, and one cluster has exactly 3072 slots.
All inputs are finite; a program needn't handle non-finite values.
Results may differ from a plain program's by a relative error of at most 0.0014.
Values may be sent and summed in bfloat16 or wider, within the bound.
No kernel may reach another device: no remote copies, remote signals or barrier semaphores. Data moves between devices by JAX's collectives and lax.ppermute only.
A program may use at most 64 MiB of HBM per device.

v0:
```python
import jax
import jax.numpy as jnp
from jax import lax
from jax.sharding import PartitionSpec as P


def passed_along(shard, axis, by):
    size = lax.axis_size(axis)
    return lax.ppermute(shard, axis, [(i, (i + by) % size) for i in range(size)])


def fold_tile(best_score, mine, other):
    unit_rows, index_rows, cluster_rows = mine
    unit_other, index_other, cluster_other = other
    row_count = unit_rows.shape[0]
    block_rows = min(512, row_count)
    block_count = row_count // block_rows

    def one_block(packed):
        unit_part, index_part, cluster_part, best_part = packed
        scores = lax.dot_general(
            unit_part, unit_other, (((1,), (1,)), ((), ())), preferred_element_type=jnp.float32
        )
        matches = (cluster_part[:, None] == cluster_other[None, :]) & (
            index_other[None, :] < index_part[:, None]
        )
        return jnp.maximum(best_part, jnp.max(jnp.where(matches, scores, -1.0), axis=1))

    result = lax.map(
        one_block,
        (
            unit_rows.reshape(block_count, block_rows, -1),
            index_rows.reshape(block_count, block_rows),
            cluster_rows.reshape(block_count, block_rows),
            best_score.reshape(block_count, block_rows),
        ),
    )
    return result.reshape(row_count)


def on_device(embeddings, route, cluster):
    row_count, width = embeddings.shape
    device_count = lax.axis_size(("grp", "blk"))
    cycle_size = lax.axis_size("blk")
    pair_rows = row_count // device_count
    here = lax.axis_index(("grp", "blk"))
    data_index = here * row_count + jnp.arange(row_count, dtype=jnp.int32)
    values = embeddings.astype(jnp.float32)
    unit_rows = (
        values * lax.rsqrt(jnp.sum(values * values, axis=1, keepdims=True) + 1e-06)
    ).astype(jnp.bfloat16)
    ordering = jnp.argsort(route)
    sent_unit = jnp.take(unit_rows, ordering, axis=0)
    sent_slot = jnp.take(route % row_count, ordering)
    sent_index = jnp.take(data_index, ordering)
    arrived = (
        lax.all_to_all(
            sent_unit.reshape(device_count, pair_rows, width),
            ("grp", "blk"),
            split_axis=0,
            concat_axis=0,
            tiled=True,
        ),
        lax.all_to_all(
            sent_slot.reshape(device_count, pair_rows),
            ("grp", "blk"),
            split_axis=0,
            concat_axis=0,
            tiled=True,
        ),
        lax.all_to_all(
            sent_index.reshape(device_count, pair_rows),
            ("grp", "blk"),
            split_axis=0,
            concat_axis=0,
            tiled=True,
        ),
    )
    slot_pos = arrived[1].reshape(-1)
    block_unit = (
        jnp.zeros((row_count, width), jnp.bfloat16).at[slot_pos].set(arrived[0].reshape(-1, width))
    )
    block_index = jnp.zeros((row_count,), jnp.int32).at[slot_pos].set(arrived[2].reshape(-1))
    block_cluster = cluster.reshape(-1)
    mine = (block_unit, block_index, block_cluster)
    best_score = jnp.full((row_count,), -1.0, jnp.float32)
    best_score = fold_tile(best_score, mine, mine)
    current = mine
    for stepping in range(cycle_size - 1):
        current = passed_along((current[0], current[1], current[2]), "blk", 1)
        best_score = fold_tile(best_score, mine, current)
    ordering_back = jnp.argsort(block_index)
    home_score = jnp.take(best_score, ordering_back)
    home_pos = jnp.take(block_index % row_count, ordering_back)
    returned = (
        lax.all_to_all(
            home_score.reshape(device_count, pair_rows),
            ("grp", "blk"),
            split_axis=0,
            concat_axis=0,
            tiled=True,
        ),
        lax.all_to_all(
            home_pos.reshape(device_count, pair_rows),
            ("grp", "blk"),
            split_axis=0,
            concat_axis=0,
            tiled=True,
        ),
    )
    return (
        jnp.zeros((row_count,), jnp.float32)
        .at[returned[1].reshape(-1)]
        .set(returned[0].reshape(-1))
    )


def solution(mesh):
    in_specs = (P(("grp", "blk"), None), P(("grp", "blk")), P("grp", "blk"))
    out_specs = P(("grp", "blk"))
    return jax.shard_map(
        on_device, mesh=mesh, in_specs=in_specs, out_specs=out_specs, check_vma=False
    )
```

profile of v0, /device:TPU:0, one launch (start us, length us, event | category | flops | bytes accessed | tf_op | source)
XLA Modules:
  0.0 258.7 jit_solution(14870827692256221043)
XLA Ops:
  0.7 5.7 %sort.31 = (s32[1536]{0:T(1024)}, s32[1536]{0:T(1024)S(1)}) sort(s32[1536]{0:T(1024)} %param.14, s32[1536]{0:T(1024)S(1)} %iota.10), dimensions={0}, to_apply=%region_0.0 | sort | flops 16896 | bytes 24576 | tf_op jit(solution)/shard_map/jit(argsort)/sort | solution.py:52
  6.5 8.4 %gather_fusion.3 = s32[1536]{0:T(1024)S(1)} fusion(s32[1536]{0:T(1024)S(1)} %iota_add_fusion, s32[2048]{0:T(1024)S(1)} %pad_clamp_fusion.1), kind=kCustom, calls=%fused_computation.1.clone | custom fusion | bytes 18432 | tf_op jit(solution)/shard_map/jit(_take)/gather | solution.py:55
  14.9 8.4 %gather_fusion.2 = s32[1536]{0:T(1024)S(1)} fusion(s32[1536]{0:T(1024)S(1)} %add_select_fusion.1, s32[2048]{0:T(1024)S(1)} %pad_clamp_fusion.1), kind=kCustom, calls=%fused_computation.clone | custom fusion | bytes 18432 | tf_op jit(solution)/shard_map/jit(_take)/gather | solution.py:54
  24.0 7.3 %all-to-all-start = ((s32[32,1,48]{2,1,0:T(1,128)}), s32[32,1,48]{2,1,0:T(1,128)S(1)}, u32[]{:S(2)}, u32[]{:S(2)}) async-start(s32[32,1,48]{2,1,0:T(1,128)} %all_to_all.25), calls=%async_computation | async-start | bytes 32768 | tf_op jit(solution)/shard_map/all_to_all | solution.py:64
  33.5 5.6 %gather_fusion = bf16[1536,768]{1,0:T(8,128)(2,1)} fusion(bf16[1536,768]{1,0:T(8,128)(2,1)S(1)} %fusion.17, s32[2048]{0:T(1024)S(1)} %pad_clamp_fusion.1), kind=kCustom, calls=%fused_computation.3 | custom fusion | bytes 4724736 | tf_op jit(solution)/shard_map/jit(_take)/gather | solution.py:53
  39.1 3.4 %broadcast_select_fusion = bf16[32,48,768]{2,1,0:T(8,128)(2,1)} fusion(bf16[32,48,768]{2,1,0:T(8,128)(2,1)} %bitcast.71, pred[32,48]{1,0:T(8,128)(4,1)S(1)} %broadcast_in_dim.73), kind=kLoop, calls=%fused_computation.44 | loop fusion | flops 1179648 | bytes 4720128 | tf_op jit(solution)/shard_map/jit(_take)/select_n | solution.py:53
  42.5 5.9 %all-to-all-start.3 = ((bf16[32,48,768]{2,1,0:T(8,128)(2,1)}), bf16[32,48,768]{2,1,0:T(8,128)(2,1)}, u32[]{:S(2)}, u32[]{:S(2)}) async-start(bf16[32,48,768]{2,1,0:T(8,128)(2,1)} %broadcast_select_fusion), calls=%async_computation.3 | async-start | bytes 4718592 | tf_op jit(solution)/shard_map/all_to_all | solution.py:57
  49.7 53.1 %all-to-all-done.3 = bf16[32,48,768]{2,1,0:T(8,128)(2,1)} async-done(((bf16[32,48,768]{2,1,0:T(8,128)(2,1)}), bf16[32,48,768]{2,1,0:T(8,128)(2,1)}, u32[]{:S(2)}, u32[]{:S(2)}) %all-to-all-start.3) | async-done | bytes 2359328 | tf_op jit(solution)/shard_map/all_to_all | solution.py:57
  102.9 8.7 %scatter_custom_fusion.1 = bf16[1536,768]{1,0:T(8,128)(2,1)S(1)} fusion(s32[1536]{0:T(1024)S(1)} %fusion.20, bf16[1536,768]{1,0:T(8,128)(2,1)} %bitcast.17, bf16[]{:T(256)} %constant.131.clone.1), kind=kCustom, calls=%fused_computation.45 | custom fusion | bytes 2359808 | tf_op jit(solution)/shard_map/scatter | solution.py:81
  112.4 4.5 %all-to-all-start.1 = ((s32[32,1,48]{2,1,0:T(1,128)}), s32[32,1,48]{2,1,0:T(1,128)S(1)}, u32[]{:S(2)}, u32[]{:S(2)}) async-start(s32[32,1,48]{2,1,0:T(1,128)} %all_to_all.27), calls=%async_computation.1 | async-start | bytes 32768 | tf_op jit(solution)/shard_map/all_to_all | solution.py:71
  117.3 22.9 %collective-permute-done = s32[1536]{0:T(1024)S(1)} collective-permute-done((s32[1536]{0:T(1024)S(1)}, s32[1536]{0:T(1024)S(1)}, u32[]{:S(2)}, u32[]{:S(2)}) %collective-permute-start) | collective-permute-done | bytes 6176 | tf_op jit(solution)/shard_map/ppermute | solution.py:9
  140.9 6.2 %scatter_custom_fusion = s32[1536]{0:T(1024)S(1)} fusion(s32[1536]{0:T(1024)S(1)} %fusion.20, s32[1536]{0:T(1024)S(1)} %reshape.246, s32[]{:T(128)} %constant.124.clone.1), kind=kCustom, calls=%fused_computation.65 | custom fusion | bytes 6148 | tf_op jit(solution)/shard_map/scatter | solution.py:83
  148.7 5.0 %sort.32 = (s32[1536]{0:T(1024)}, s32[1536]{0:T(1024)S(1)}) sort(s32[1536]{0:T(1024)S(1)} %scatter_custom_fusion, s32[1536]{0:T(1024)S(1)} %iota.12), dimensions={0}, to_apply=%region_2.4 | sort | flops 16896 | bytes 24576 | tf_op jit(solution)/shard_map/jit(argsort)/sort | solution.py:92
  154.5 8.4 %gather_fusion.4 = s32[1536]{0:T(1024)S(1)} fusion(s32[1536]{0:T(1024)S(1)} %add_select_fusion, s32[2048]{0:T(1024)S(1)} %pad_clamp_fusion), kind=kCustom, calls=%fused_computation.2.clone | custom fusion | bytes 18432 | tf_op jit(solution)/shard_map/jit(_take)/gather | solution.py:94
  164.5 5.3 %while.40 = (s32[]{:T(128)}, f32[3,512]{1,0:T(4,128)S(1)}, s32[3,512]{1,0:T(4,128)S(1)}, s32[1,1536]{1,0:T(1,128)S(1)}, s32[1536]{0:T(1024)S(1)}, /*index=5*/s32...) while((s32[]{:T(128)}, f32[3,512]{1,0:T(4,128)S(1)}, ...), condition=%wide.region_7.9_spmd, body=%wide.region_5.8_spmd.sunk | while | flops 1211891712 | bytes 3197045 | solution.py:29
  169.8 12.7 %collective-permute-done.5 = bf16[1536,768]{1,0:T(8,128)(2,1)} collective-permute-done((bf16[1536,768]{1,0:T(8,128)(2,1)}, bf16[1536,768]{1,0:T(8,128)(2,1)}, u32[]{:S(2)}, u32[]{:S(2)}) %collective-permute-start.5) | collective-permute-done | bytes 2359328 | tf_op jit(solution)/shard_map/ppermute | solution.py:9
  182.4 10.2 %while.41 = (s32[]{:T(128)}, f32[3,512]{1,0:T(4,128)S(1)}, f32[3,512]{1,0:T(4,128)S(1)}, s32[3,512]{1,0:T(4,128)S(1)}, s32[1536]{0:T(1024)S(1)}, /*index=5*/s32[...) while((s32[]{:T(128)}, f32[3,512]{1,0:T(4,128)S(1)}, ...), condition=%wide.region_10.12_spmd, body=%wide.region_8.11_spmd.sunk | while | flops 1211891712 | bytes 3186813 | solution.py:29
  185.9 3.3 %fusion.47 = f32[512]{0:T(512)S(1)} fusion(bf16[1536,768]{1,0:T(8,128)(2,1)} %get-tuple-element.569, s32[512]{0:T(512)S(1)} %bitcast.79, s32[1536]{0:T(1024)S(1)} %get-tuple-element.566, s32[1536]{0:T(1024)S(1)} %get-tuple-element.565, s32[512]{0:T(512)S(1)} %bitcast.80, bf16[3,512,768]{2,1,0:T(8,128)(2,1)S(1)} %get-tuple-element.568, ...), kind=kOutput, calls=%fused_computation.9.clone.1 | convolution fusion | flops 1211891200 | bytes 3168260 | tf_op jit(solution)/shard_map/while/body/eval_jaxpr/dot_general | solution.py:21
  189.3 3.3 %fusion.47 = f32[512]{0:T(512)S(1)} fusion(bf16[1536,768]{1,0:T(8,128)(2,1)} %get-tuple-element.569, s32[512]{0:T(512)S(1)} %bitcast.79, s32[1536]{0:T(1024)S(1)} %get-tuple-element.566, s32[1536]{0:T(1024)S(1)} %get-tuple-element.565, s32[512]{0:T(512)S(1)} %bitcast.80, bf16[3,512,768]{2,1,0:T(8,128)(2,1)S(1)} %get-tuple-element.568, ...), kind=kOutput, calls=%fused_computation.9.clone.1 | convolution fusion | flops 1211891200 | bytes 3168260 | tf_op jit(solution)/shard_map/while/body/eval_jaxpr/dot_general | solution.py:21
  192.6 10.3 %while.42 = (s32[]{:T(128)}, f32[3,512]{1,0:T(4,128)S(1)}, f32[3,512]{1,0:T(4,128)S(1)}, s32[3,512]{1,0:T(4,128)S(1)}, s32[1536]{0:T(1024)}, /*index=5*/s32[1536...) while((s32[]{:T(128)}, f32[3,512]{1,0:T(4,128)S(1)}, ...), condition=%wide.region_13.15_spmd, body=%wide.region_11.14_spmd.sunk | while | flops 1211891712 | bytes 3182717 | solution.py:29
  192.7 3.3 %fusion.50 = f32[512]{0:T(512)S(1)} fusion(bf16[1536,768]{1,0:T(8,128)(2,1)} %get-tuple-element.602, s32[512]{0:T(512)S(1)} %bitcast.81, s32[1536]{0:T(1024)} %get-tuple-element.599, s32[1536]{0:T(1024)} %get-tuple-element.598, s32[512]{0:T(512)S(1)} %bitcast.82, bf16[3,512,768]{2,1,0:T(8,128)(2,1)S(1)} %get-tuple-element.601, s32[]{:T(128)} %get-tuple-element.583), kind=kOutput, calls=%fused_computation.17.clone.1 | convolution fusion | flops 1211891200 | bytes 3164164 | tf_op jit(solution)/shard_map/while/body/eval_jaxpr/dot_general | solution.py:21
  196.1 3.3 %fusion.50 = f32[512]{0:T(512)S(1)} fusion(bf16[1536,768]{1,0:T(8,128)(2,1)} %get-tuple-element.602, s32[512]{0:T(512)S(1)} %bitcast.81, s32[1536]{0:T(1024)} %get-tuple-element.599, s32[1536]{0:T(1024)} %get-tuple-element.598, s32[512]{0:T(512)S(1)} %bitcast.82, bf16[3,512,768]{2,1,0:T(8,128)(2,1)S(1)} %get-tuple-element.601, s32[]{:T(128)} %get-tuple-element.583), kind=kOutput, calls=%fused_computation.17.clone.1 | convolution fusion | flops 1211891200 | bytes 3164164 | tf_op jit(solution)/shard_map/while/body/eval_jaxpr/dot_general | solution.py:21
  199.6 3.3 %fusion.50 = f32[512]{0:T(512)S(1)} fusion(bf16[1536,768]{1,0:T(8,128)(2,1)} %get-tuple-element.602, s32[512]{0:T(512)S(1)} %bitcast.81, s32[1536]{0:T(1024)} %get-tuple-element.599, s32[1536]{0:T(1024)} %get-tuple-element.598, s32[512]{0:T(512)S(1)} %bitcast.82, bf16[3,512,768]{2,1,0:T(8,128)(2,1)S(1)} %get-tuple-element.601, s32[]{:T(128)} %get-tuple-element.583), kind=kOutput, calls=%fused_computation.17.clone.1 | convolution fusion | flops 1211891200 | bytes 3164164 | tf_op jit(solution)/shard_map/while/body/eval_jaxpr/dot_general | solution.py:21
  203.0 8.0 %collective-permute-done.8 = bf16[1536,768]{1,0:T(8,128)(2,1)} collective-permute-done((bf16[1536,768]{1,0:T(8,128)(2,1)}, bf16[1536,768]{1,0:T(8,128)(2,1)}, u32[]{:S(2)}, u32[]{:S(2)}) %collective-permute-start.8) | collective-permute-done | bytes 2359328 | tf_op jit(solution)/shard_map/ppermute | solution.py:9
  211.0 10.2 %while.43 = (s32[]{:T(128)}, f32[3,512]{1,0:T(4,128)S(1)}, f32[3,512]{1,0:T(4,128)S(1)}, s32[3,512]{1,0:T(4,128)S(1)}, s32[1536]{0:T(1024)S(1)}, /*index=5*/s32[...) while((s32[]{:T(128)}, f32[3,512]{1,0:T(4,128)S(1)}, ...), condition=%wide.region_16.18_spmd, body=%wide.region_14.17_spmd.sunk | while | flops 1211891712 | bytes 3186813 | solution.py:29
  214.4 3.3 %fusion.53 = f32[512]{0:T(512)S(1)} fusion(bf16[1536,768]{1,0:T(8,128)(2,1)} %get-tuple-element.635, s32[512]{0:T(512)S(1)} %bitcast.83, s32[1536]{0:T(1024)S(1)} %get-tuple-element.632, s32[1536]{0:T(1024)S(1)} %get-tuple-element.631, s32[512]{0:T(512)S(1)} %bitcast.84, bf16[3,512,768]{2,1,0:T(8,128)(2,1)S(1)} %get-tuple-element.634, ...), kind=kOutput, calls=%fused_computation.25.clone.1 | convolution fusion | flops 1211891200 | bytes 3168260 | tf_op jit(solution)/shard_map/while/body/eval_jaxpr/dot_general | solution.py:21
  217.8 3.3 %fusion.53 = f32[512]{0:T(512)S(1)} fusion(bf16[1536,768]{1,0:T(8,128)(2,1)} %get-tuple-element.635, s32[512]{0:T(512)S(1)} %bitcast.83, s32[1536]{0:T(1024)S(1)} %get-tuple-element.632, s32[1536]{0:T(1024)S(1)} %get-tuple-element.631, s32[512]{0:T(512)S(1)} %bitcast.84, bf16[3,512,768]{2,1,0:T(8,128)(2,1)S(1)} %get-tuple-element.634, ...), kind=kOutput, calls=%fused_computation.25.clone.1 | convolution fusion | flops 1211891200 | bytes 3168260 | tf_op jit(solution)/shard_map/while/body/eval_jaxpr/dot_general | solution.py:21
  221.2 8.4 %gather_fusion.1 = f32[1536]{0:T(1024)S(1)} fusion(f32[1536]{0:T(1024)S(1)} %reshape.200, s32[2048]{0:T(1024)S(1)} %pad_clamp_fusion), kind=kCustom, calls=%fused_computation.4 | custom fusion | bytes 18432 | tf_op jit(solution)/shard_map/jit(_take)/gather | solution.py:93
  230.3 3.5 %all-to-all-start.2 = ((s32[32,1,48]{2,1,0:T(1,128)}), s32[32,1,48]{2,1,0:T(1,128)S(1)}, u32[]{:S(2)}, u32[]{:S(2)}) async-start(s32[32,1,48]{2,1,0:T(1,128)} %all_to_all.29), calls=%async_computation.2 | async-start | bytes 32768 | tf_op jit(solution)/shard_map/all_to_all | solution.py:103
  234.5 6.5 %all-to-all-done.2 = s32[32,1,48]{2,1,0:T(1,128)S(1)} async-done(((s32[32,1,48]{2,1,0:T(1,128)}), s32[32,1,48]{2,1,0:T(1,128)S(1)}, u32[]{:S(2)}, u32[]{:S(2)}) %all-to-all-start.2) | async-done | bytes 6176 | tf_op jit(solution)/shard_map/all_to_all | solution.py:103
  244.3 6.4 %all-to-all-done.4 = f32[32,1,48]{2,1,0:T(1,128)S(1)} async-done(((f32[32,1,48]{2,1,0:T(1,128)}), f32[32,1,48]{2,1,0:T(1,128)S(1)}, u32[]{:S(2)}, u32[]{:S(2)}) %all-to-all-start.4) | async-done | bytes 6176 | tf_op jit(solution)/shard_map/all_to_all | solution.py:96
  252.0 6.7 %scatter_custom_fusion.2 = f32[1536]{0:T(1024)} fusion(s32[1536]{0:T(1024)S(1)} %fusion.21, f32[1536]{0:T(1024)S(1)} %reshape.262, f32[]{:T(128)} %constant.123.clone.1), kind=kCustom, calls=%fused_computation.67 | custom fusion | bytes 6148 | tf_op jit(solution)/shard_map/scatter | solution.py:114
  (109 shorter events, 29.0 us)
Async XLA Ops:
  14.9 16.5 %copy-start = (bf16[1536,768]{1,0:T(8,128)(2,1)S(1)}, bf16[1536,768]{1,0:T(8,128)(2,1)}, u32[]{:S(2)}) copy-start(bf16[1536,768]{1,0:T(8,128)(2,1)} %param.13) | copy-start | bytes 7077892
  24.0 18.5 %all-to-all-start = ((s32[32,1,48]{2,1,0:T(1,128)}), s32[32,1,48]{2,1,0:T(1,128)S(1)}, u32[]{:S(2)}, u32[]{:S(2)}) async-start(s32[32,1,48]{2,1,0:T(1,128)} %all_to_all.25), calls=%async_computation | async-start | bytes 32768 | tf_op jit(solution)/shard_map/all_to_all | solution.py:64
  31.4 1.7 copy-start.1
  42.5 60.4 %all-to-all-start.3 = ((bf16[32,48,768]{2,1,0:T(8,128)(2,1)}), bf16[32,48,768]{2,1,0:T(8,128)(2,1)}, u32[]{:S(2)}, u32[]{:S(2)}) async-start(bf16[32,48,768]{2,1,0:T(8,128)(2,1)} %broadcast_select_fusion), calls=%async_computation.3 | async-start | bytes 4718592 | tf_op jit(solution)/shard_map/all_to_all | solution.py:57
  48.5 68.4 %copy-start.2 = (s32[1,1536]{1,0:T(1,128)S(1)}, s32[1,1536]{1,0:T(1,128)}, u32[]{:S(2)}) copy-start(s32[1,1536]{1,0:T(1,128)} %param.15) | copy-start | bytes 18436
  111.6 42.2 %collective-permute-start.2 = (bf16[1536,768]{1,0:T(8,128)(2,1)S(1)}, bf16[1536,768]{1,0:T(8,128)(2,1)}, u32[]{:S(2)}, u32[]{:S(2)}) collective-permute-start(bf16[1536,768]{1,0:T(8,128)(2,1)S(1)} %scatter_custom_fusion.1), channel_id=1, source_target_pairs={{0,1},{1,2},{2,3},{3,0},{4,5},{5,6},{6,7},{7,4},{8,9},{9,10},{10,1... | collective-permute-start | bytes 7077896 | tf_op jit(solution)/shard_map/ppermute | solution.py:9
  112.4 27.8 %all-to-all-start.1 = ((s32[32,1,48]{2,1,0:T(1,128)}), s32[32,1,48]{2,1,0:T(1,128)S(1)}, u32[]{:S(2)}, u32[]{:S(2)}) async-start(s32[32,1,48]{2,1,0:T(1,128)} %all_to_all.27), calls=%async_computation.1 | async-start | bytes 32768 | tf_op jit(solution)/shard_map/all_to_all | solution.py:71
  117.0 23.2 %collective-permute-start = (s32[1536]{0:T(1024)S(1)}, s32[1536]{0:T(1024)S(1)}, u32[]{:S(2)}, u32[]{:S(2)}) collective-permute-start(s32[1536]{0:T(1024)S(1)} %reduce.6), channel_id=1, source_target_pairs={{0,1},{1,2},{2,3},{3,0},{4,5},{5,6},{6,7},{7,4},{8,9},{9,10},{10,1... | collective-permute-start | bytes 18440 | tf_op jit(solution)/shard_map/ppermute | solution.py:9
  140.2 22.7 %collective-permute-start.3 = (s32[1536]{0:T(1024)S(1)}, s32[1536]{0:T(1024)}, u32[]{:S(2)}, u32[]{:S(2)}) collective-permute-start(s32[1536]{0:T(1024)S(1)} %collective-permute-done), channel_id=1, source_target_pairs={{0,1},{1,2},{2,3},{3,0},{4,5},{5,6},{6,7},{7,4},{8,9},{9,10},{10,1... | collective-permute-start | bytes 18440 | tf_op jit(solution)/shard_map/ppermute | solution.py:9
  147.1 6.6 %collective-permute-start.1 = (s32[1536]{0:T(1024)S(1)}, s32[1536]{0:T(1024)S(1)}, u32[]{:S(2)}, u32[]{:S(2)}) collective-permute-start(s32[1536]{0:T(1024)S(1)} %scatter_custom_fusion), channel_id=1, source_target_pairs={{0,1},{1,2},{2,3},{3,0},{4,5},{5,6},{6,7},{7,4},{8,9},{9,10},{10,1... | collective-permute-start | bytes 18440 | tf_op jit(solution)/shard_map/ppermute | solution.py:9
  153.7 9.4 %collective-permute-start.4 = (s32[1536]{0:T(1024)S(1)}, s32[1536]{0:T(1024)}, u32[]{:S(2)}, u32[]{:S(2)}) collective-permute-start(s32[1536]{0:T(1024)S(1)} %collective-permute-done.1), channel_id=1, source_target_pairs={{0,1},{1,2},{2,3},{3,0},{4,5},{5,6},{6,7},{7,4},{8,9},{9,10},{10,1... | collective-permute-start | bytes 18440 | tf_op jit(solution)/shard_map/ppermute | solution.py:9
  153.8 28.6 %collective-permute-start.5 = (bf16[1536,768]{1,0:T(8,128)(2,1)}, bf16[1536,768]{1,0:T(8,128)(2,1)}, u32[]{:S(2)}, u32[]{:S(2)}) collective-permute-start(bf16[1536,768]{1,0:T(8,128)(2,1)} %collective-permute-done.2), channel_id=1, source_target_pairs={{0,1},{1,2},{2,3},{3,0},{4,5},{5,6},{6,7},{7,4},{8,9},{9,10},{10,1... | collective-permute-start | bytes 7077896 | tf_op jit(solution)/shard_map/ppermute | solution.py:9
  163.0 40.0 %collective-permute-start.6 = (s32[1536]{0:T(1024)}, s32[1536]{0:T(1024)S(1)}, u32[]{:S(2)}, u32[]{:S(2)}) collective-permute-start(s32[1536]{0:T(1024)} %collective-permute-done.3), channel_id=1, source_target_pairs={{0,1},{1,2},{2,3},{3,0},{4,5},{5,6},{6,7},{7,4},{8,9},{9,10},{10,1... | collective-permute-start | bytes 18440 | tf_op jit(solution)/shard_map/ppermute | solution.py:9
  163.1 39.9 %collective-permute-start.7 = (s32[1536]{0:T(1024)}, s32[1536]{0:T(1024)S(1)}, u32[]{:S(2)}, u32[]{:S(2)}) collective-permute-start(s32[1536]{0:T(1024)} %collective-permute-done.4), channel_id=1, source_target_pairs={{0,1},{1,2},{2,3},{3,0},{4,5},{5,6},{6,7},{7,4},{8,9},{9,10},{10,1... | collective-permute-start | bytes 18440 | tf_op jit(solution)/shard_map/ppermute | solution.py:9
  182.4 28.6 %collective-permute-start.8 = (bf16[1536,768]{1,0:T(8,128)(2,1)}, bf16[1536,768]{1,0:T(8,128)(2,1)}, u32[]{:S(2)}, u32[]{:S(2)}) collective-permute-start(bf16[1536,768]{1,0:T(8,128)(2,1)} %collective-permute-done.5), channel_id=1, source_target_pairs={{0,1},{1,2},{2,3},{3,0},{4,5},{5,6},{6,7},{7,4},{8,9},{9,10},{10,1... | collective-permute-start | bytes 7077896 | tf_op jit(solution)/shard_map/ppermute | solution.py:9
  230.3 10.6 %all-to-all-start.2 = ((s32[32,1,48]{2,1,0:T(1,128)}), s32[32,1,48]{2,1,0:T(1,128)S(1)}, u32[]{:S(2)}, u32[]{:S(2)}) async-start(s32[32,1,48]{2,1,0:T(1,128)} %all_to_all.29), calls=%async_computation.2 | async-start | bytes 32768 | tf_op jit(solution)/shard_map/all_to_all | solution.py:103
  241.0 9.7 %all-to-all-start.4 = ((f32[32,1,48]{2,1,0:T(1,128)}), f32[32,1,48]{2,1,0:T(1,128)S(1)}, u32[]{:S(2)}, u32[]{:S(2)}) async-start(f32[32,1,48]{2,1,0:T(1,128)} %select_n.88), calls=%async_computation.4 | async-start | bytes 32768 | tf_op jit(solution)/shard_map/all_to_all | solution.py:96
where the time goes:
time: 260 us; the launch traced here: 259 us
  waiting for transfers between devices  110 us (42%)
  local copies, waits for them, and re-layouts  66.9 us (26%)
  matrix products  34.8 us (13%)
  starting transfers between devices  28.1 us (11%)
  other arithmetic  18.7 us (7%)
    all_to_all x1, waiting for transfers between devices, on_device(): lax.all_to_all(sent_unit.reshape(device_count, pair_rows, width), ('grp',...  53.1 us
    ppermute x9, waiting for transfers between devices, passed_along(): lax.ppermute(shard, axis, [(i, (i + by) % size) for i in range(size)])  43.6 us
    dot_general x12, matrix products, one_block(): lax.dot_general(unit_part, unit_other, (((1,), (1,)), ((), ())), preferre...  34.8 us
    scatter x1, local copies, waits for them, and re-layouts, on_device(): jnp.zeros((row_count, width), jnp.bfloat16).at[slot_pos]  8.72 us
    gather x1, local copies, waits for them, and re-layouts, on_device(): sent_index = jnp.take(data_index, ordering)  8.39 us
    gather x1, local copies, waits for them, and re-layouts, on_device(): sent_slot = jnp.take(route % row_count, ordering)  8.39 us
    gather x1, local copies, waits for them, and re-layouts, on_device(): home_score = jnp.take(best_score, ordering_back)  8.39 us
    gather x1, local copies, waits for them, and re-layouts, on_device(): home_pos = jnp.take(block_index % row_count, ordering_back)  8.39 us
  transfers between devices with their start and end apart: 14, of which 6 were waited for; matrix products, arithmetic and copies ran while one was open for 23% of the time, Pallas kernels for 0%

commit v1 on v0

v1 whole, which is shorter than its diff:
```python
import functools

import jax
import jax.numpy as jnp
from jax import lax
from jax.experimental import pallas as pl
from jax.experimental.pallas import tpu as pltpu
from jax.sharding import PartitionSpec as P

BF16, F32, I32 = jnp.bfloat16, jnp.float32, jnp.int32
LANES = 128
CLUSTERS = 4
VMEM = pl.BlockSpec(memory_space=pltpu.VMEM)
SMEM = pl.BlockSpec(memory_space=pltpu.SMEM)
ANY = pl.BlockSpec(memory_space=pl.ANY)
MIB = 1 << 20


def dot_nt(a, b):
    return lax.dot_general(a, b, (((1,), (1,)), ((), ())), preferred_element_type=F32)


def iota(shape, dim):
    return lax.broadcasted_iota(I32, shape, dim)


def one_hot(match):
    return jnp.where(match, 1.0, 0.0).astype(BF16)


def place_kernel(n, piece, family_rows, route_ref, cluster_ref, fam_ref, rank_ref, meta_ref):
    blocks = route_ref.shape[0]
    route = route_ref[...]
    fam = jnp.zeros_like(route)
    for f in range(1, n):
        fam = fam + jnp.where(route >= f * family_rows, 1, 0)
    rel = route - fam * family_rows
    pad = 16 - blocks % 16 if blocks % 16 else 0
    tall = blocks + pad
    fam_pad = jnp.concatenate([fam, jnp.full((pad, LANES), -1, I32)], axis=0) if pad else fam
    member = jnp.concatenate(
        [jnp.where(fam_pad == f, 1.0, 0.0) for f in range(n)], axis=0
    )
    member_low = member.astype(BF16)
    before = one_hot(iota((LANES, LANES), 0) < iota((LANES, LANES), 1))
    within = jnp.dot(member_low, before, preferred_element_type=F32)
    totals = jnp.dot(member_low, jnp.ones((LANES, LANES), BF16), preferred_element_type=F32)
    size = n * tall
    shift = tall.bit_length() - 1
    row, col = iota((size, size), 0), iota((size, size), 1)
    above = one_hot(((row >> shift) == (col >> shift)) & (col < row))
    ranks = within + jnp.dot(above, totals.astype(BF16), preferred_element_type=F32)
    ranks = ranks * member
    rank = jnp.zeros((tall, LANES), F32)
    for f in range(n):
        rank = rank + ranks[f * tall:(f + 1) * tall]
    rank = rank.astype(I32)

    def as_row(x):
        return jnp.concatenate([x[i:i + 1] for i in range(blocks)], axis=1)

    fam_row, rank_row, rel_row = as_row(fam), as_row(rank), as_row(rel)
    fam_ref[...] = fam_row
    rank_ref[...] = rank_row
    rows = fam_row.shape[1]
    mine = iota((n, rows), 0) == fam_row
    high = jnp.where(mine, (rel_row >> 6).astype(F32), 0.0)
    low = jnp.where(mine, (rel_row & 63).astype(F32), 0.0)
    at_rank = one_hot(iota((piece, rows), 0) == rank_row)
    packed = dot_nt(jnp.concatenate([high, low], axis=0).astype(BF16), at_rank)
    slots = packed[:n] * 64.0 + packed[n:]
    meta_ref[:n] = slots.astype(I32)
    cluster = cluster_ref[...]
    lane = iota((8, piece), 1)
    counts = jnp.zeros((8, piece), F32)
    for c in range(CLUSTERS - 1):
        counts = jnp.where(lane == c, jnp.sum(jnp.where(cluster <= c, 1.0, 0.0)), counts)
    meta_ref[n:] = counts.astype(I32)


def pack_kernel(n, piece, here_ref, emb_ref, fam_ref, rank_ref, *rest):
    outs, unit_ref = rest[:n], rest[n]
    rows, _ = emb_ref.shape
    grp = here_ref[0]

    @pl.loop(0, rows // 128)
    def _(i):
        at = pl.ds(pl.multiple_of(i * 128, 128), 128)
        x = emb_ref[at, :].astype(F32)
        total = jnp.sum(x * x, axis=1, keepdims=True)
        unit_ref[at, :] = (x * lax.rsqrt(total + 1e-06)).astype(BF16)

    pos = (fam_ref[...] ^ grp) * piece + rank_ref[...]
    group = max(1, min(n, 384 // piece))
    for start in range(0, n, group):
        select = one_hot(iota((group * piece, rows), 0) + start * piece == pos)
        got = jnp.dot(select, unit_ref[...], preferred_element_type=F32).astype(BF16)
        for i in range(group):
            outs[start + i][...] = got[i * piece:(i + 1) * piece]


def score_kernel(n, nb, piece, here_ref, left_ref, right_ref, kcl_ref, qcl_ref, *rest):
    pieces = [rest[d * nb:(d + 1) * nb] for d in range(n)]
    out_ref, keys, best, sems = rest[n * nb:]
    grp, blk = here_ref[0], here_ref[1]
    width = keys.shape[-1]
    copies = []
    for d in range(n):
        for e in range(nb):
            copy = pltpu.make_async_copy(
                pieces[d][e], keys.at[grp ^ d, blk ^ e], sems.at[d, e]
            )
            copy.start()
            copies.append(copy)
    best[...] = jnp.full(best.shape, -1.0, F32)
    for copy in copies:
        copy.wait()
    span = nb * piece

    def fold(query, key, causal):
        q = keys[query, blk]
        k = keys[key].reshape(span, width)
        scores = dot_nt(k, q)
        match = kcl_ref[key] == qcl_ref[query]
        if causal:
            match = match & (iota((span, piece), 0) < blk * piece + iota((span, piece), 1))
        scores = jnp.where(match, scores, -1.0)
        best[query] = jnp.maximum(best[query], jnp.max(scores.reshape(span // 8, 8, piece), axis=0))

    @pl.loop(0, n)
    def _(i):
        fold(i, i, True)

    @pl.loop(0, left_ref.shape[0])
    def _(i):
        one, two = grp ^ left_ref[i], grp ^ right_ref[i]
        fold(jnp.maximum(one, two), jnp.minimum(one, two), False)

    for i in range(n):
        out_ref[i:i + 1] = jnp.max(best[i], axis=0, keepdims=True)


def unpack_kernel(n, piece, score_ref, fam_ref, rank_ref, out_ref):
    x = score_ref[...]
    high = x.astype(BF16)
    rest = x - high.astype(F32)
    mid = rest.astype(BF16)
    low = (rest - mid.astype(F32)).astype(BF16)
    rows = fam_ref.shape[1]
    at_rank = one_hot(iota((piece, rows), 0) == rank_ref[...])
    got = jnp.dot(jnp.concatenate([high, mid, low], axis=0), at_rank, preferred_element_type=F32)
    value = got[:n] + got[n:2 * n] + got[2 * n:]
    value = jnp.where(iota((n, rows), 0) == fam_ref[...], value, 0.0)
    out_ref[...] = jnp.sum(value, axis=0, keepdims=True)


def shape(*dims, kind=F32):
    return jax.ShapeDtypeStruct(dims, kind)


def send(x, axis, by):
    return lax.ppermute(x, axis, [(i, i ^ by) for i in range(lax.axis_size(axis))])


def on_device(embeddings, route, cluster):
    rows, width = embeddings.shape
    n, nb = lax.axis_size("grp"), lax.axis_size("blk")
    piece = rows // n
    family_rows = rows * nb
    grp, blk = lax.axis_index("grp"), lax.axis_index("blk")
    here = jnp.stack([grp, blk]).astype(I32)
    blocks = rows // LANES

    fam, rank, meta = pl.pallas_call(
        functools.partial(place_kernel, n, piece, family_rows),
        out_shape=[shape(1, rows, kind=I32), shape(1, rows, kind=I32), shape(n + 8, piece, kind=I32)],
        in_specs=[VMEM] * 2,
        out_specs=[VMEM] * 3,
        compiler_params=pltpu.CompilerParams(vmem_limit_bytes=32 * MIB),
        name="place",
    )(route.reshape(blocks, LANES), cluster.reshape(blocks, LANES))

    sent = pl.pallas_call(
        functools.partial(pack_kernel, n, piece),
        out_shape=[shape(piece, width, kind=BF16)] * n,
        in_specs=[SMEM, VMEM, VMEM, VMEM],
        out_specs=[VMEM] * n,
        scratch_shapes=[pltpu.VMEM((rows, width), BF16)],
        compiler_params=pltpu.CompilerParams(vmem_limit_bytes=48 * MIB),
        name="pack",
    )(here, embeddings, fam, rank)

    everyone = lax.all_gather(meta, ("grp", "blk"))
    slots = lax.dynamic_index_in_dim(everyone[:, :n], grp, 1, keepdims=False)
    counts = lax.dynamic_slice_in_dim(everyone[:, n, :CLUSTERS - 1], grp * nb, nb, 0)
    bounds = jnp.sum(counts, axis=0)
    kinds = jnp.zeros_like(slots)
    for c in range(CLUSTERS - 1):
        kinds = kinds + (slots >= bounds[c]).astype(I32)
    kinds = kinds.reshape(n, nb, piece)
    query_kinds = lax.dynamic_index_in_dim(kinds, blk, 1, keepdims=True)
    key_kinds = kinds.reshape(n, nb * piece, 1)

    order = sorted(range(n), key=lambda d: -d)
    held = [None] * n
    for d in order:
        own = sent[d] if d == 0 else send(sent[d], "grp", d)
        held[d] = [own]
    for d in reversed(order):
        across = send(held[d][0], "blk", 2)
        held[d] += [send(held[d][0], "blk", 1), across, send(across, "blk", 1)]

    pairs = [(a, b) for a in range(n) for b in range(a)]
    left = jnp.array([a for a, _ in pairs], I32)
    right = jnp.array([b for _, b in pairs], I32)
    best = pl.pallas_call(
        functools.partial(score_kernel, n, nb, piece),
        out_shape=shape(n, piece),
        in_specs=[SMEM] * 3 + [VMEM] * 2 + [ANY] * (n * nb),
        out_specs=VMEM,
        scratch_shapes=[
            pltpu.VMEM((n, nb, piece, width), BF16),
            pltpu.VMEM((n, 8, piece), F32),
            pltpu.SemaphoreType.DMA((n, nb)),
        ],
        compiler_params=pltpu.CompilerParams(vmem_limit_bytes=48 * MIB),
        name="score",
    )(here, left, right, key_kinds, query_kinds, *[p for group in held for p in group])

    home = lax.all_to_all(best, "grp", split_axis=0, concat_axis=0, tiled=True)
    out = pl.pallas_call(
        functools.partial(unpack_kernel, n, piece),
        out_shape=shape(1, rows),
        in_specs=[VMEM] * 3,
        out_specs=VMEM,
        compiler_params=pltpu.CompilerParams(vmem_limit_bytes=32 * MIB),
        name="unpack",
    )(home, fam, rank)
    return out.reshape(rows)


def solution(mesh):
    in_specs = (P(("grp", "blk"), None), P(("grp", "blk")), P("grp", "blk"))
    return jax.shard_map(
        on_device, mesh=mesh, in_specs=in_specs, out_specs=P(("grp", "blk")), check_vma=False
    )
```

time: 260 us -> 208 us (0.80)
  blocking collectives: 0 us -> 54.9 us
  local copies, waits for them, and re-layouts: 66.9 us -> 21 us
  waiting for transfers between devices: 110 us -> 67.9 us
  matrix products: 34.8 us -> 0 us
  Pallas kernels: 0 us -> 29.7 us
  other arithmetic: 18.7 us -> 4.61 us
    all_to_all x5 -> x0, waiting for transfers between devices: 66 us -> none  [the longest x1 53.1 us: on_device(): lax.all_to_all(sent_unit.reshape(device_count, pair_rows, width), ('grp',...]
    all_gather x0 -> x1, blocking collectives: none -> 46.1 us  [on_device(): everyone = lax.all_gather(meta, ('grp', 'blk'))]
    gather x5 -> x0, local copies, waits for them, and re-layouts: 39.2 us -> none  [the longest x1 8.39 us: on_device(): sent_index = jnp.take(data_index, ordering)]
    dot_general x12 -> x0, matrix products: 34.8 us -> none  [one_block(): lax.dot_general(unit_part, unit_other, (((1,), (1,)), ((), ())), preferre...]
    pallas_call x0 -> x4, Pallas kernels: none -> 29.7 us  [the longest x1 23 us: on_device(): pl.pallas_call(functools.partial(score_kernel, n, nb, piece), out_shape=s...]
    ppermute x9 -> x31, starting transfers between devices: 4.27 us -> 29.1 us  [send(): lax.ppermute(x, axis, [(i, i ^ by) for i in range(lax.axis_size(axis))])]
    ppermute x9 -> x31, waiting for transfers between devices: 43.6 us -> 67.9 us  [send(): lax.ppermute(x, axis, [(i, i ^ by) for i in range(lax.axis_size(axis))])]
    all_to_all x5 -> x0, starting transfers between devices: 23.8 us -> none  [the longest x1 7.3 us: on_device(): lax.all_to_all(sent_slot.reshape(device_count, pair_rows), ('grp', 'blk')...]
  transfers between devices with their start and end apart: 14 -> 31, of which waited for: 6 -> 10; matrix products, arithmetic and copies ran while one was open for 23% -> 7% of each run, Pallas kernels for 0% -> 0%
where the time goes in v1:
time: 208 us
  waiting for transfers between devices  67.9 us (33%)
  blocking collectives  54.9 us (26%)
  Pallas kernels  29.7 us (14%)
  starting transfers between devices  29.1 us (14%)
  local copies, waits for them, and re-layouts  21 us (10%)
  other arithmetic  4.61 us (2%)
    ppermute x31, waiting for transfers between devices, send(): lax.ppermute(x, axis, [(i, i ^ by) for i in range(lax.axis_size(axis))])  67.9 us
    all_gather x1, blocking collectives, on_device(): everyone = lax.all_gather(meta, ('grp', 'blk'))  46.1 us
    ppermute x31, starting transfers between devices, send(): lax.ppermute(x, axis, [(i, i ^ by) for i in range(lax.axis_size(axis))])  29.1 us
    pallas_call x1, Pallas kernels, on_device(): pl.pallas_call(functools.partial(score_kernel, n, nb, piece), out_shape=s...  23 us
    unnamed x33, local copies, waits for them, and re-layouts  9.55 us
    all_to_all x1, blocking collectives, on_device(): home = lax.all_to_all(best, 'grp', split_axis=0, concat_axis=0, tiled=True)  8.88 us
    add x2, local copies, waits for them, and re-layouts, on_device(): kinds = kinds + (slots >= bounds[c]).astype(I32)  5.9 us
    pallas_call x1, Pallas kernels, on_device(): pl.pallas_call(functools.partial(pack_kernel, n, piece), out_shape=[shape...  5.86 us
  transfers between devices with their start and end apart: 31, of which 10 were waited for; matrix products, arithmetic and copies ran while one was open for 7% of the time, Pallas kernels for 0%

profile of v1, /device:TPU:0, one launch (start us, length us, event | category | flops | bytes accessed | tf_op | source)
XLA Modules:
  0.0 207.5 jit_solution(17781346041758893734)
XLA Ops:
  2.1 1.7 copy-done
  3.8 5.9 %pack.1 = (bf16[192,768]{1,0:T(8,128)(2,1)S(1)}, bf16[192,768]{1,0:T(8,128)(2,1)S(1)}, bf16[192,768]{1,0:T(8,128)(2,1)S(1)}, bf16[192,768]{1,0:T(8,128)(2,1)S(1)...) custom-call(s32[2]{0:T(128)S(1)} %pad_add_fusion.here_ref, ...), custom_call_target="tpu_custom_call" | custom-call | tf_op jit(solution)/shard_map/pack/pallas_call | solution.py:183
  9.6 3.1 %collective-permute-start.7 = (bf16[192,768]{1,0:T(8,128)(2,1)S(1)}, bf16[192,768]{1,0:T(8,128)(2,1)S(1)}, u32[]{:S(2)}, u32[]{:S(2)}) collective-permute-start(bf16[192,768]{1,0:T(8,128)(2,1)S(1)} %get-tuple-element.21), channel_id=1, source_target_pairs={{0,8},{4,12},{8,0},{12,4},{16,24},{20,28},{24,16},{28,20},{1,9},{5... | collective-permute-start | bytes 884744 | tf_op jit(solution)/shard_map/ppermute | solution.py:162
  12.7 1.4 collective-permute-start.11
  14.1 2.6 %collective-permute-start.15 = (bf16[192,768]{1,0:T(8,128)(2,1)S(1)}, bf16[192,768]{1,0:T(8,128)(2,1)S(1)}, u32[]{:S(2)}, u32[]{:S(2)}) collective-permute-start(bf16[192,768]{1,0:T(8,128)(2,1)S(1)} %get-tuple-element.23), channel_id=1, source_target_pairs={{0,16},{4,20},{8,24},{12,28},{16,0},{20,4},{24,8},{28,12},{1,17},{... | collective-permute-start | bytes 884744 | tf_op jit(solution)/shard_map/ppermute | solution.py:162
  16.7 3.9 %collective-permute-start.23 = (bf16[192,768]{1,0:T(8,128)(2,1)S(1)}, bf16[192,768]{1,0:T(8,128)(2,1)S(1)}, u32[]{:S(2)}, u32[]{:S(2)}) collective-permute-start(bf16[192,768]{1,0:T(8,128)(2,1)S(1)} %get-tuple-element.25), channel_id=1, source_target_pairs={{0,24},{4,28},{8,16},{12,20},{16,8},{20,12},{24,0},{28,4},{1,25},{... | collective-permute-start | bytes 884744 | tf_op jit(solution)/shard_map/ppermute | solution.py:162
  20.6 11.1 %collective-permute-done.7.rest_8_ = bf16[192,768]{1,0:T(8,128)(2,1)S(1)} collective-permute-done((bf16[192,768]{1,0:T(8,128)(2,1)S(1)}, bf16[192,768]{1,0:T(8,128)(2,1)S(1)}, u32[]{:S(2)}, u32[]{:S(2)}) %collective-permute-start.7) | collective-permute-done | bytes 294944 | tf_op jit(solution)/shard_map/ppermute | solution.py:162
  31.7 4.0 %collective-permute-start.27 = (bf16[192,768]{1,0:T(8,128)(2,1)S(1)}, bf16[192,768]{1,0:T(8,128)(2,1)}, u32[]{:S(2)}, u32[]{:S(2)}) collective-permute-start(bf16[192,768]{1,0:T(8,128)(2,1)S(1)} %get-tuple-element.26), channel_id=1, source_target_pairs={{0,28},{4,24},{8,20},{12,16},{16,12},{20,8},{24,4},{28,0},{1,29},{... | collective-permute-start | bytes 884744 | tf_op jit(solution)/shard_map/ppermute | solution.py:162
  35.7 3.3 %collective-permute-done.11.rest_12_ = bf16[192,768]{1,0:T(8,128)(2,1)S(1)} collective-permute-done((bf16[192,768]{1,0:T(8,128)(2,1)S(1)}, bf16[192,768]{1,0:T(8,128)(2,1)S(1)}, u32[]{:S(2)}, u32[]{:S(2)}) %collective-permute-start.11) | collective-permute-done | bytes 294944 | tf_op jit(solution)/shard_map/ppermute | solution.py:162
  39.0 1.4 collective-permute-start.1
  40.4 15.8 %collective-permute-done.19.rest_20_ = bf16[192,768]{1,0:T(8,128)(2,1)S(1)} collective-permute-done((bf16[192,768]{1,0:T(8,128)(2,1)S(1)}, bf16[192,768]{1,0:T(8,128)(2,1)S(1)}, u32[]{:S(2)}, u32[]{:S(2)}) %collective-permute-start.19) | collective-permute-done | bytes 294944 | tf_op jit(solution)/shard_map/ppermute | solution.py:162
  56.2 1.9 collective-permute-start.9
  58.3 1.9 collective-permute-start.17
  60.3 1.9 collective-permute-start.25
  62.2 3.9 %collective-permute-done.9.rest_10_ = bf16[192,768]{1,0:T(8,128)(2,1)S(1)} collective-permute-done((bf16[192,768]{1,0:T(8,128)(2,1)S(1)}, bf16[192,768]{1,0:T(8,128)(2,1)S(1)}, u32[]{:S(2)}, u32[]{:S(2)}) %collective-permute-start.9) | collective-permute-done | bytes 294944 | tf_op jit(solution)/shard_map/ppermute | solution.py:162
  66.0 1.9 collective-permute-start.29
  67.9 4.4 %collective-permute-done.13.rest_14_ = bf16[192,768]{1,0:T(8,128)(2,1)S(1)} collective-permute-done((bf16[192,768]{1,0:T(8,128)(2,1)S(1)}, bf16[192,768]{1,0:T(8,128)(2,1)S(1)}, u32[]{:S(2)}, u32[]{:S(2)}) %collective-permute-start.13) | collective-permute-done | bytes 294944 | tf_op jit(solution)/shard_map/ppermute | solution.py:162
  72.4 1.9 collective-permute-start.5
  74.2 4.4 %collective-permute-done.17.rest_18_ = bf16[192,768]{1,0:T(8,128)(2,1)S(1)} collective-permute-done((bf16[192,768]{1,0:T(8,128)(2,1)S(1)}, bf16[192,768]{1,0:T(8,128)(2,1)S(1)}, u32[]{:S(2)}, u32[]{:S(2)}) %collective-permute-start.17) | collective-permute-done | bytes 294944 | tf_op jit(solution)/shard_map/ppermute | solution.py:162
  78.7 6.4 %collective-permute-done.21.rest_22_ = bf16[192,768]{1,0:T(8,128)(2,1)} collective-permute-done((bf16[192,768]{1,0:T(8,128)(2,1)S(1)}, bf16[192,768]{1,0:T(8,128)(2,1)}, u32[]{:S(2)}, u32[]{:S(2)}) %collective-permute-start.21) | collective-permute-done | bytes 294944 | tf_op jit(solution)/shard_map/ppermute | solution.py:162
  85.1 6.3 %collective-permute-done.25.rest_26_ = bf16[192,768]{1,0:T(8,128)(2,1)} collective-permute-done((bf16[192,768]{1,0:T(8,128)(2,1)S(1)}, bf16[192,768]{1,0:T(8,128)(2,1)}, u32[]{:S(2)}, u32[]{:S(2)}) %collective-permute-start.25) | collective-permute-done | bytes 294944 | tf_op jit(solution)/shard_map/ppermute | solution.py:162
  91.4 6.2 %collective-permute-done.29.rest_30_ = bf16[192,768]{1,0:T(8,128)(2,1)S(1)} collective-permute-done((bf16[192,768]{1,0:T(8,128)(2,1)}, bf16[192,768]{1,0:T(8,128)(2,1)S(1)}, u32[]{:S(2)}, u32[]{:S(2)}) %collective-permute-start.29) | collective-permute-done | bytes 294944 | tf_op jit(solution)/shard_map/ppermute | solution.py:162
  97.6 6.0 %collective-permute-done.5.rest_6_ = bf16[192,768]{1,0:T(8,128)(2,1)S(1)} collective-permute-done((bf16[192,768]{1,0:T(8,128)(2,1)S(1)}, bf16[192,768]{1,0:T(8,128)(2,1)S(1)}, u32[]{:S(2)}, u32[]{:S(2)}) %collective-permute-start.5) | collective-permute-done | bytes 294944 | tf_op jit(solution)/shard_map/ppermute | solution.py:162
  107.6 46.1 %all-gather = s32[512,192]{1,0:T(8,128)} all-gather(s32[16,192]{1,0:T(8,128)S(1)} %get-tuple-element.16), channel_id=2, replica_groups=mesh['grp'=8,'blk'=4] {'grp','blk'}, dimensions={0}, use_global_device_ids=true | all-gather | bytes 405504 | tf_op jit(solution)/shard_map/all_gather | solution.py:193
  153.7 1.5 slice.21
  155.2 1.7 slice.20
  158.2 1.0 constant_dynamic-slice_fusion.1
  160.6 2.5 %convert_add_fusion = s32[32,1,192]{2,0,1:T(8,128)} fusion(s32[32,1,192]{2,1,0:T(1,128)S(1)} %constant_dynamic-slice_fusion.1, s32[]{:T(128)} %bitcast.6, s32[]{:T(128)} %bitcast.5, s32[]{:T(128)} %bitcast.4), kind=kLoop, calls=%fused_computation | loop fusion | flops 49152 | bytes 49164 | tf_op jit(solution)/shard_map/add | solution.py:199
  163.1 1.4 add.46
  164.5 4.5 %add.48.kcl_ref = s32[8,768,1]{2,1,0:T(8,128)} reshape(s32[32,1,192]{2,0,1:T(8,128)} %convert_add_fusion) | data formatting | bytes 49152 | tf_op jit(solution)/shard_map/add | solution.py:199
  174.7 23.0 %score.1 = f32[8,192]{1,0:T(8,128)S(1)} custom-call(s32[2]{0:T(128)S(1)} %copy-done.9, s32[28]{0:T(128)S(1)} %copy-done.10, s32[28]{0:T(128)S(1)} %copy-done.11, s32[8,768,1]{2,1,0:T(8,128)} %add.48.kcl_ref, s32[8,1,192]{2,1,0:T(1,128)S(1)} %constant_dynamic-slice_fusion.qcl_ref, bf16[192,768]{1,0:T(8,128)(2,1)S(1)} %get-tuple-element.19.rest_0_, ...), custom_call_target="tpu_custom_call" | custom-call | tf_op jit(solution)/shard_map/score/pallas_call | solution.py:216
  197.7 8.9 %all_to_all.11 = f32[8,1,192]{2,1,0:T(1,128)S(1)} all-to-all(f32[8,1,192]{2,1,0:T(1,128)S(1)} %copy.11), channel_id=1, replica_groups=mesh['grp'=8,'blk'=4] {'grp'}, dimensions={0} | all-to-all | bytes 12288 | tf_op jit(solution)/shard_map/all_to_all | solution.py:230
  (82 shorter events, 15.7 us)
Async XLA Ops:
  2.1 104.8 %copy-start.8 = (s32[2]{0:T(128)}, s32[2]{0:T(128)S(1)}, u32[]{:S(2)}) copy-start(s32[2]{0:T(128)S(1)} %pad_add_fusion.here_ref) | copy-start | bytes 28
  9.6 22.1 %collective-permute-start.7 = (bf16[192,768]{1,0:T(8,128)(2,1)S(1)}, bf16[192,768]{1,0:T(8,128)(2,1)S(1)}, u32[]{:S(2)}, u32[]{:S(2)}) collective-permute-start(bf16[192,768]{1,0:T(8,128)(2,1)S(1)} %get-tuple-element.21), channel_id=1, source_target_pairs={{0,8},{4,12},{8,0},{12,4},{16,24},{20,28},{24,16},{28,20},{1,9},{5... | collective-permute-start | bytes 884744 | tf_op jit(solution)/shard_map/ppermute | solution.py:162
  12.7 26.2 %collective-permute-start.11 = (bf16[192,768]{1,0:T(8,128)(2,1)S(1)}, bf16[192,768]{1,0:T(8,128)(2,1)S(1)}, u32[]{:S(2)}, u32[]{:S(2)}) collective-permute-start(bf16[192,768]{1,0:T(8,128)(2,1)S(1)} %get-tuple-element.22), channel_id=1, source_target_pairs={{0,12},{4,8},{8,4},{12,0},{16,28},{20,24},{24,20},{28,16},{1,13},{... | collective-permute-start | bytes 884744 | tf_op jit(solution)/shard_map/ppermute | solution.py:162
  14.1 24.9 %collective-permute-start.15 = (bf16[192,768]{1,0:T(8,128)(2,1)S(1)}, bf16[192,768]{1,0:T(8,128)(2,1)S(1)}, u32[]{:S(2)}, u32[]{:S(2)}) collective-permute-start(bf16[192,768]{1,0:T(8,128)(2,1)S(1)} %get-tuple-element.23), channel_id=1, source_target_pairs={{0,16},{4,20},{8,24},{12,28},{16,0},{20,4},{24,8},{28,12},{1,17},{... | collective-permute-start | bytes 884744 | tf_op jit(solution)/shard_map/ppermute | solution.py:162
  16.7 39.5 %collective-permute-start.19 = (bf16[192,768]{1,0:T(8,128)(2,1)S(1)}, bf16[192,768]{1,0:T(8,128)(2,1)S(1)}, u32[]{:S(2)}, u32[]{:S(2)}) collective-permute-start(bf16[192,768]{1,0:T(8,128)(2,1)S(1)} %get-tuple-element.24), channel_id=1, source_target_pairs={{0,20},{4,16},{8,28},{12,24},{16,4},{20,0},{24,12},{28,8},{1,21},{... | collective-permute-start | bytes 884744 | tf_op jit(solution)/shard_map/ppermute | solution.py:162
  16.7 39.5 %collective-permute-start.23 = (bf16[192,768]{1,0:T(8,128)(2,1)S(1)}, bf16[192,768]{1,0:T(8,128)(2,1)S(1)}, u32[]{:S(2)}, u32[]{:S(2)}) collective-permute-start(bf16[192,768]{1,0:T(8,128)(2,1)S(1)} %get-tuple-element.25), channel_id=1, source_target_pairs={{0,24},{4,28},{8,16},{12,20},{16,8},{20,12},{24,0},{28,4},{1,25},{... | collective-permute-start | bytes 884744 | tf_op jit(solution)/shard_map/ppermute | solution.py:162
  31.7 26.4 %collective-permute-start.27 = (bf16[192,768]{1,0:T(8,128)(2,1)S(1)}, bf16[192,768]{1,0:T(8,128)(2,1)}, u32[]{:S(2)}, u32[]{:S(2)}) collective-permute-start(bf16[192,768]{1,0:T(8,128)(2,1)S(1)} %get-tuple-element.26), channel_id=1, source_target_pairs={{0,28},{4,24},{8,20},{12,16},{16,12},{20,8},{24,4},{28,0},{1,29},{... | collective-permute-start | bytes 884744 | tf_op jit(solution)/shard_map/ppermute | solution.py:162
  39.0 19.3 %collective-permute-start.3 = (bf16[192,768]{1,0:T(8,128)(2,1)S(1)}, bf16[192,768]{1,0:T(8,128)(2,1)S(1)}, u32[]{:S(2)}, u32[]{:S(2)}) collective-permute-start(bf16[192,768]{1,0:T(8,128)(2,1)S(1)} %get-tuple-element.20), channel_id=1, source_target_pairs={{0,4},{4,0},{8,12},{12,8},{16,20},{20,16},{24,28},{28,24},{1,5},{5... | collective-permute-start | bytes 884744 | tf_op jit(solution)/shard_map/ppermute | solution.py:162
  39.0 21.2 %collective-permute-start.1 = (bf16[192,768]{1,0:T(8,128)(2,1)S(1)}, bf16[192,768]{1,0:T(8,128)(2,1)S(1)}, u32[]{:S(2)}, u32[]{:S(2)}) collective-permute-start(bf16[192,768]{1,0:T(8,128)(2,1)S(1)} %get-tuple-element.19.rest_0_), channel_id=1, source_target_pairs={{0,2},{1,3},{2,0},{3,1},{4,6},{5,7},{6,4},{7,5},{8,10},{9,11},{10,... | collective-permute-start | bytes 884744 | tf_op jit(solution)/shard_map/ppermute | solution.py:162
  56.2 4.1 %collective-permute-start = (bf16[192,768]{1,0:T(8,128)(2,1)S(1)}, bf16[192,768]{1,0:T(8,128)(2,1)S(1)}, u32[]{:S(2)}, u32[]{:S(2)}) collective-permute-start(bf16[192,768]{1,0:T(8,128)(2,1)S(1)} %get-tuple-element.19.rest_0_), channel_id=1, source_target_pairs={{0,1},{1,0},{2,3},{3,2},{4,5},{5,4},{6,7},{7,6},{8,9},{9,8},{10,11... | collective-permute-start | bytes 884744 | tf_op jit(solution)/shard_map/ppermute | solution.py:162
  56.2 9.9 %collective-permute-start.9 = (bf16[192,768]{1,0:T(8,128)(2,1)S(1)}, bf16[192,768]{1,0:T(8,128)(2,1)S(1)}, u32[]{:S(2)}, u32[]{:S(2)}) collective-permute-start(bf16[192,768]{1,0:T(8,128)(2,1)S(1)} %collective-permute-done.7.rest_8_), channel_id=1, source_target_pairs={{0,2},{1,3},{2,0},{3,1},{4,6},{5,7},{6,4},{7,5},{8,10},{9,11},{10,... | collective-permute-start | bytes 884744 | tf_op jit(solution)/shard_map/ppermute | solution.py:162
  58.1 14.2 %collective-permute-start.13 = (bf16[192,768]{1,0:T(8,128)(2,1)S(1)}, bf16[192,768]{1,0:T(8,128)(2,1)S(1)}, u32[]{:S(2)}, u32[]{:S(2)}) collective-permute-start(bf16[192,768]{1,0:T(8,128)(2,1)S(1)} %collective-permute-done.11.rest_12_), channel_id=1, source_target_pairs={{0,2},{1,3},{2,0},{3,1},{4,6},{5,7},{6,4},{7,5},{8,10},{9,11},{10,... | collective-permute-start | bytes 884744 | tf_op jit(solution)/shard_map/ppermute | solution.py:162
  58.3 20.4 %collective-permute-start.17 = (bf16[192,768]{1,0:T(8,128)(2,1)S(1)}, bf16[192,768]{1,0:T(8,128)(2,1)S(1)}, u32[]{:S(2)}, u32[]{:S(2)}) collective-permute-start(bf16[192,768]{1,0:T(8,128)(2,1)S(1)} %collective-permute-done.15.rest_16_), channel_id=1, source_target_pairs={{0,2},{1,3},{2,0},{3,1},{4,6},{5,7},{6,4},{7,5},{8,10},{9,11},{10,... | collective-permute-start | bytes 884744 | tf_op jit(solution)/shard_map/ppermute | solution.py:162
  60.1 25.0 %collective-permute-start.21 = (bf16[192,768]{1,0:T(8,128)(2,1)S(1)}, bf16[192,768]{1,0:T(8,128)(2,1)}, u32[]{:S(2)}, u32[]{:S(2)}) collective-permute-start(bf16[192,768]{1,0:T(8,128)(2,1)S(1)} %collective-permute-done.19.rest_20_), channel_id=1, source_target_pairs={{0,2},{1,3},{2,0},{3,1},{4,6},{5,7},{6,4},{7,5},{8,10},{9,11},{10,... | collective-permute-start | bytes 884744 | tf_op jit(solution)/shard_map/ppermute | solution.py:162
  60.3 31.1 %collective-permute-start.25 = (bf16[192,768]{1,0:T(8,128)(2,1)S(1)}, bf16[192,768]{1,0:T(8,128)(2,1)}, u32[]{:S(2)}, u32[]{:S(2)}) collective-permute-start(bf16[192,768]{1,0:T(8,128)(2,1)S(1)} %collective-permute-done.23.rest_24_), channel_id=1, source_target_pairs={{0,2},{1,3},{2,0},{3,1},{4,6},{5,7},{6,4},{7,5},{8,10},{9,11},{10,... | collective-permute-start | bytes 884744 | tf_op jit(solution)/shard_map/ppermute | solution.py:162
  66.0 31.6 %collective-permute-start.29 = (bf16[192,768]{1,0:T(8,128)(2,1)}, bf16[192,768]{1,0:T(8,128)(2,1)S(1)}, u32[]{:S(2)}, u32[]{:S(2)}) collective-permute-start(bf16[192,768]{1,0:T(8,128)(2,1)} %collective-permute-done.27.rest_28_), channel_id=1, source_target_pairs={{0,2},{1,3},{2,0},{3,1},{4,6},{5,7},{6,4},{7,5},{8,10},{9,11},{10,... | collective-permute-start | bytes 884744 | tf_op jit(solution)/shard_map/ppermute | solution.py:162
  72.4 31.3 %collective-permute-start.5 = (bf16[192,768]{1,0:T(8,128)(2,1)S(1)}, bf16[192,768]{1,0:T(8,128)(2,1)S(1)}, u32[]{:S(2)}, u32[]{:S(2)}) collective-permute-start(bf16[192,768]{1,0:T(8,128)(2,1)S(1)} %collective-permute-done.3.rest_4_), channel_id=1, source_target_pairs={{0,2},{1,3},{2,0},{3,1},{4,6},{5,7},{6,4},{7,5},{8,10},{9,11},{10,... | collective-permute-start | bytes 884744 | tf_op jit(solution)/shard_map/ppermute | solution.py:162
  78.7 25.0 %collective-permute-start.2 = (bf16[192,768]{1,0:T(8,128)(2,1)S(1)}, bf16[192,768]{1,0:T(8,128)(2,1)S(1)}, u32[]{:S(2)}, u32[]{:S(2)}) collective-permute-start(bf16[192,768]{1,0:T(8,128)(2,1)S(1)} %collective-permute-done.1.rest_2_), channel_id=1, source_target_pairs={{0,1},{1,0},{2,3},{3,2},{4,5},{5,4},{6,7},{7,6},{8,9},{9,8},{10,11... | collective-permute-start | bytes 884744 | tf_op jit(solution)/shard_map/ppermute | solution.py:162
  85.1 19.8 %collective-permute-start.12 = (bf16[192,768]{1,0:T(8,128)(2,1)S(1)}, bf16[192,768]{1,0:T(8,128)(2,1)S(1)}, u32[]{:S(2)}, u32[]{:S(2)}) collective-permute-start(bf16[192,768]{1,0:T(8,128)(2,1)S(1)} %collective-permute-done.11.rest_12_), channel_id=1, source_target_pairs={{0,1},{1,0},{2,3},{3,2},{4,5},{5,4},{6,7},{7,6},{8,9},{9,8},{10,11... | collective-permute-start | bytes 884744 | tf_op jit(solution)/shard_map/ppermute | solution.py:162
  91.4 14.1 %collective-permute-start.16 = (bf16[192,768]{1,0:T(8,128)(2,1)S(1)}, bf16[192,768]{1,0:T(8,128)(2,1)S(1)}, u32[]{:S(2)}, u32[]{:S(2)}) collective-permute-start(bf16[192,768]{1,0:T(8,128)(2,1)S(1)} %collective-permute-done.15.rest_16_), channel_id=1, source_target_pairs={{0,1},{1,0},{2,3},{3,2},{4,5},{5,4},{6,7},{7,6},{8,9},{9,8},{10,11... | collective-permute-start | bytes 884744 | tf_op jit(solution)/shard_map/ppermute | solution.py:162
  97.6 9.2 %collective-permute-start.20 = (bf16[192,768]{1,0:T(8,128)(2,1)S(1)}, bf16[192,768]{1,0:T(8,128)(2,1)S(1)}, u32[]{:S(2)}, u32[]{:S(2)}) collective-permute-start(bf16[192,768]{1,0:T(8,128)(2,1)S(1)} %collective-permute-done.19.rest_20_), channel_id=1, source_target_pairs={{0,1},{1,0},{2,3},{3,2},{4,5},{5,4},{6,7},{7,6},{8,9},{9,8},{10,11... | collective-permute-start | bytes 884744 | tf_op jit(solution)/shard_map/ppermute | solution.py:162
  103.6 3.2 %collective-permute-start.24 = (bf16[192,768]{1,0:T(8,128)(2,1)S(1)}, bf16[192,768]{1,0:T(8,128)(2,1)S(1)}, u32[]{:S(2)}, u32[]{:S(2)}) collective-permute-start(bf16[192,768]{1,0:T(8,128)(2,1)S(1)} %collective-permute-done.23.rest_24_), channel_id=1, source_target_pairs={{0,1},{1,0},{2,3},{3,2},{4,5},{5,4},{6,7},{7,6},{8,9},{9,8},{10,11... | collective-permute-start | bytes 884744 | tf_op jit(solution)/shard_map/ppermute | solution.py:162
  104.4 54.8 %collective-permute-start.28 = (bf16[192,768]{1,0:T(8,128)(2,1)}, bf16[192,768]{1,0:T(8,128)(2,1)}, u32[]{:S(2)}, u32[]{:S(2)}) collective-permute-start(bf16[192,768]{1,0:T(8,128)(2,1)} %collective-permute-done.27.rest_28_), channel_id=1, source_target_pairs={{0,1},{1,0},{2,3},{3,2},{4,5},{5,4},{6,7},{7,6},{8,9},{9,8},{10,11... | collective-permute-start | bytes 884744 | tf_op jit(solution)/shard_map/ppermute | solution.py:162
  105.6 54.0 %collective-permute-start.4 = (bf16[192,768]{1,0:T(8,128)(2,1)S(1)}, bf16[192,768]{1,0:T(8,128)(2,1)}, u32[]{:S(2)}, u32[]{:S(2)}) collective-permute-start(bf16[192,768]{1,0:T(8,128)(2,1)S(1)} %collective-permute-done.3.rest_4_), channel_id=1, source_target_pairs={{0,1},{1,0},{2,3},{3,2},{4,5},{5,4},{6,7},{7,6},{8,9},{9,8},{10,11... | collective-permute-start | bytes 884744 | tf_op jit(solution)/shard_map/ppermute | solution.py:162
  106.3 53.5 %collective-permute-start.8 = (bf16[192,768]{1,0:T(8,128)(2,1)S(1)}, bf16[192,768]{1,0:T(8,128)(2,1)}, u32[]{:S(2)}, u32[]{:S(2)}) collective-permute-start(bf16[192,768]{1,0:T(8,128)(2,1)S(1)} %collective-permute-done.7.rest_8_), channel_id=1, source_target_pairs={{0,1},{1,0},{2,3},{3,2},{4,5},{5,4},{6,7},{7,6},{8,9},{9,8},{10,11... | collective-permute-start | bytes 884744 | tf_op jit(solution)/shard_map/ppermute | solution.py:162
  106.8 53.3 %collective-permute-start.10 = (bf16[192,768]{1,0:T(8,128)(2,1)S(1)}, bf16[192,768]{1,0:T(8,128)(2,1)}, u32[]{:S(2)}, u32[]{:S(2)}) collective-permute-start(bf16[192,768]{1,0:T(8,128)(2,1)S(1)} %collective-permute-done.9.rest_10_), channel_id=1, source_target_pairs={{0,1},{1,0},{2,3},{3,2},{4,5},{5,4},{6,7},{7,6},{8,9},{9,8},{10,11... | collective-permute-start | bytes 884744 | tf_op jit(solution)/shard_map/ppermute | solution.py:162
  106.9 53.4 %collective-permute-start.14 = (bf16[192,768]{1,0:T(8,128)(2,1)S(1)}, bf16[192,768]{1,0:T(8,128)(2,1)}, u32[]{:S(2)}, u32[]{:S(2)}) collective-permute-start(bf16[192,768]{1,0:T(8,128)(2,1)S(1)} %collective-permute-done.13.rest_14_), channel_id=1, source_target_pairs={{0,1},{1,0},{2,3},{3,2},{4,5},{5,4},{6,7},{7,6},{8,9},{9,8},{10,11... | collective-permute-start | bytes 884744 | tf_op jit(solution)/shard_map/ppermute | solution.py:162
  159.2 10.6 %collective-permute-start.18 = (bf16[192,768]{1,0:T(8,128)(2,1)S(1)}, bf16[192,768]{1,0:T(8,128)(2,1)}, u32[]{:S(2)}, u32[]{:S(2)}) collective-permute-start(bf16[192,768]{1,0:T(8,128)(2,1)S(1)} %collective-permute-done.17.rest_18_), channel_id=1, source_target_pairs={{0,1},{1,0},{2,3},{3,2},{4,5},{5,4},{6,7},{7,6},{8,9},{9,8},{10,11... | collective-permute-start | bytes 884744 | tf_op jit(solution)/shard_map/ppermute | solution.py:162
  159.6 10.2 %collective-permute-start.22 = (bf16[192,768]{1,0:T(8,128)(2,1)}, bf16[192,768]{1,0:T(8,128)(2,1)}, u32[]{:S(2)}, u32[]{:S(2)}) collective-permute-start(bf16[192,768]{1,0:T(8,128)(2,1)} %collective-permute-done.21.rest_22_), channel_id=1, source_target_pairs={{0,1},{1,0},{2,3},{3,2},{4,5},{5,4},{6,7},{7,6},{8,9},{9,8},{10,11... | collective-permute-start | bytes 884744 | tf_op jit(solution)/shard_map/ppermute | solution.py:162
  159.8 10.1 %collective-permute-start.26 = (bf16[192,768]{1,0:T(8,128)(2,1)}, bf16[192,768]{1,0:T(8,128)(2,1)}, u32[]{:S(2)}, u32[]{:S(2)}) collective-permute-start(bf16[192,768]{1,0:T(8,128)(2,1)} %collective-permute-done.25.rest_26_), channel_id=1, source_target_pairs={{0,1},{1,0},{2,3},{3,2},{4,5},{5,4},{6,7},{7,6},{8,9},{9,8},{10,11... | collective-permute-start | bytes 884744 | tf_op jit(solution)/shard_map/ppermute | solution.py:162
  160.1 9.7 %collective-permute-start.30 = (bf16[192,768]{1,0:T(8,128)(2,1)}, bf16[192,768]{1,0:T(8,128)(2,1)}, u32[]{:S(2)}, u32[]{:S(2)}) collective-permute-start(bf16[192,768]{1,0:T(8,128)(2,1)} %copy-done.13), channel_id=1, source_target_pairs={{0,1},{1,0},{2,3},{3,2},{4,5},{5,4},{6,7},{7,6},{8,9},{9,8},{10,11... | collective-permute-start | bytes 884744 | tf_op jit(solution)/shard_map/ppermute | solution.py:162
  160.3 9.6 %collective-permute-start.6 = (bf16[192,768]{1,0:T(8,128)(2,1)S(1)}, bf16[192,768]{1,0:T(8,128)(2,1)}, u32[]{:S(2)}, u32[]{:S(2)}) collective-permute-start(bf16[192,768]{1,0:T(8,128)(2,1)S(1)} %collective-permute-done.5.rest_6_), channel_id=1, source_target_pairs={{0,1},{1,0},{2,3},{3,2},{4,5},{5,4},{6,7},{7,6},{8,9},{9,8},{10,11... | collective-permute-start | bytes 884744 | tf_op jit(solution)/shard_map/ppermute | solution.py:162
  (15 other events, 71.3 us)

commit v2 on v1

v2 whole, which is shorter than its diff:
```python
import functools

import jax
import jax.numpy as jnp
from jax import lax
from jax.experimental import pallas as pl
from jax.experimental.pallas import tpu as pltpu
from jax.sharding import PartitionSpec as P

BF16, F32, I32 = jnp.bfloat16, jnp.float32, jnp.int32
LANES = 128
CLUSTERS = 4
VMEM = pl.BlockSpec(memory_space=pltpu.VMEM)
SMEM = pl.BlockSpec(memory_space=pltpu.SMEM)
ANY = pl.BlockSpec(memory_space=pl.ANY)
MIB = 1 << 20


def dot_nt(a, b):
    return lax.dot_general(a, b, (((1,), (1,)), ((), ())), preferred_element_type=F32)


def iota(shape, dim):
    return lax.broadcasted_iota(I32, shape, dim)


def one_hot(match):
    return jnp.where(match, 1.0, 0.0).astype(BF16)


def place_kernel(n, nb, piece, family_rows, route_ref, cluster_ref, fam_ref, rank_ref, meta_ref):
    blocks = route_ref.shape[0]
    route = route_ref[...]
    fam = jnp.zeros_like(route)
    for f in range(1, n):
        fam = fam + jnp.where(route >= f * family_rows, 1, 0)
    rel = route - fam * family_rows
    pad = 16 - blocks % 16 if blocks % 16 else 0
    tall = blocks + pad
    fam_pad = jnp.concatenate([fam, jnp.full((pad, LANES), -1, I32)], axis=0) if pad else fam
    member = jnp.concatenate(
        [jnp.where(fam_pad == f, 1.0, 0.0) for f in range(n)], axis=0
    )
    member_low = member.astype(BF16)
    before = one_hot(iota((LANES, LANES), 0) < iota((LANES, LANES), 1))
    within = jnp.dot(member_low, before, preferred_element_type=F32)
    totals = jnp.dot(member_low, jnp.ones((LANES, LANES), BF16), preferred_element_type=F32)
    size = n * tall
    shift = tall.bit_length() - 1
    row, col = iota((size, size), 0), iota((size, size), 1)
    above = one_hot(((row >> shift) == (col >> shift)) & (col < row))
    ranks = within + jnp.dot(above, totals.astype(BF16), preferred_element_type=F32)
    ranks = ranks * member
    rank = jnp.zeros((tall, LANES), F32)
    for f in range(n):
        rank = rank + ranks[f * tall:(f + 1) * tall]
    rank = rank.astype(I32)

    def as_row(x):
        return jnp.concatenate([x[i:i + 1] for i in range(blocks)], axis=1)

    fam_row, rank_row, rel_row = as_row(fam), as_row(rank), as_row(rel)
    fam_ref[...] = fam_row
    rank_ref[...] = rank_row
    rows = fam_row.shape[1]
    mine = iota((n, rows), 0) == fam_row
    high = jnp.where(mine, (rel_row >> 6).astype(F32), 0.0)
    low = jnp.where(mine, (rel_row & 63).astype(F32), 0.0)
    at_rank = one_hot(iota((piece, rows), 0) == rank_row)
    packed = dot_nt(jnp.concatenate([high, low], axis=0).astype(BF16), at_rank)
    slots = packed[:n] * 64.0 + packed[n:]
    cluster = cluster_ref[...]
    wide = meta_ref.shape[-1]
    lane = iota((n, wide - piece), 1)
    counts = jnp.zeros((n, wide - piece), F32)
    for c in range(CLUSTERS - 1):
        counts = jnp.where(lane == c, jnp.sum(jnp.where(cluster <= c, 1.0, 0.0)), counts)
    meta = jnp.concatenate([slots, counts], axis=1).astype(I32)
    for f in range(n):
        for e in range(nb):
            meta_ref[f * nb + e] = meta[f:f + 1]


def pack_kernel(n, piece, here_ref, emb_ref, fam_ref, rank_ref, *rest):
    outs, unit_ref = rest[:n], rest[n]
    rows, _ = emb_ref.shape
    grp = here_ref[0]

    @pl.loop(0, rows // 128)
    def _(i):
        at = pl.ds(pl.multiple_of(i * 128, 128), 128)
        x = emb_ref[at, :].astype(F32)
        total = jnp.sum(x * x, axis=1, keepdims=True)
        unit_ref[at, :] = (x * lax.rsqrt(total + 1e-06)).astype(BF16)

    pos = (fam_ref[...] ^ grp) * piece + rank_ref[...]
    group = max(1, min(n, 384 // piece))
    for start in range(0, n, group):
        select = one_hot(iota((group * piece, rows), 0) + start * piece == pos)
        got = jnp.dot(select, unit_ref[...], preferred_element_type=F32).astype(BF16)
        for i in range(group):
            outs[start + i][...] = got[i * piece:(i + 1) * piece]


def kinds_kernel(n, nb, piece, here_ref, meta_ref, key_ref, query_ref):
    grp, blk = here_ref[0], here_ref[1]
    wide = meta_ref.shape[-1]
    counts = meta_ref[grp * nb]
    for e in range(1, nb):
        counts = counts + meta_ref[grp * nb + e]
    lane = iota((1, wide), 1)
    bounds = [
        jnp.sum(jnp.where(lane == piece + c, counts, 0).astype(F32)) for c in range(CLUSTERS - 1)
    ]
    first = iota((8, piece), 0) == 0
    ones = jnp.where(iota((8, LANES), 0) == 0, 1.0, 0.0).astype(BF16)

    def kinds(source):
        slots = meta_ref[source].astype(F32)[:, :piece]
        total = jnp.zeros_like(slots)
        for bound in bounds:
            total = total + jnp.where(slots >= bound, 1.0, 0.0)
        return total

    @pl.loop(0, n * nb)
    def _(source):
        tall = jnp.where(first, kinds(source), 0.0).astype(BF16)
        key_ref[source] = lax.dot_general(
            tall, ones, (((0,), (0,)), ((), ())), preferred_element_type=F32
        )

    @pl.loop(0, n)
    def _(i):
        query_ref[i] = kinds(i * nb + blk)


def stage_kernel(n, nb, piece, lo, hi, here_ref, kcl_ref, qcl_ref, *rest):
    count = hi - lo
    pieces = [rest[i * nb:(i + 1) * nb] for i in range(count)]
    rest = rest[count * nb + (2 if lo else 0):]
    if hi < n:
        keys, best = rest
    else:
        outs, (keys, best) = rest[:n], rest[n:]
    grp, blk = here_ref[0], here_ref[1]
    width = keys.shape[-1]
    span = nb * piece
    if not lo:
        best[...] = jnp.full(best.shape, -1.0, F32)
    for i in range(count):
        for e in range(nb):
            keys[grp ^ (lo + i), blk ^ e] = pieces[i][e][...]

    def fold(query, key, causal):
        q = keys[query, blk]
        k = keys[key].reshape(span, width)
        scores = dot_nt(k, q)
        kinds = kcl_ref[pl.ds(key * nb, nb)].reshape(span, LANES)
        parts = []
        for at in range(0, piece, LANES):
            w = min(LANES, piece - at)
            match = kinds[:, :w] == qcl_ref[query][:, at:at + w]
            if causal:
                early = iota((span, w), 0) - iota((span, w), 1) < blk * piece + at
                match = match & early
            part = jnp.where(match, scores[:, at:at + w], -1.0)
            parts.append(jnp.max(part.reshape(span // 8, 8, w), axis=0))
        folded = jnp.concatenate(parts, axis=1) if len(parts) > 1 else parts[0]
        best[query] = jnp.maximum(best[query], folded)

    @pl.loop(lo, hi)
    def _(a):
        one = grp ^ a
        fold(one, one, True)

        @pl.loop(0, a)
        def _(b):
            two = grp ^ b
            fold(jnp.maximum(one, two), jnp.minimum(one, two), False)

    if hi == n:
        for d in range(n):
            outs[d][...] = jnp.max(best[grp ^ d], axis=0, keepdims=True)


def unpack_kernel(n, piece, here_ref, fam_ref, rank_ref, *rest):
    scores, out_ref = rest[:n], rest[n]
    x = jnp.concatenate([r[...] for r in scores], axis=0)
    high = x.astype(BF16)
    rest = x - high.astype(F32)
    mid = rest.astype(BF16)
    low = (rest - mid.astype(F32)).astype(BF16)
    rows = fam_ref.shape[1]
    at_rank = one_hot(iota((piece, rows), 0) == rank_ref[...])
    got = jnp.dot(jnp.concatenate([high, mid, low], axis=0), at_rank, preferred_element_type=F32)
    value = got[:n] + got[n:2 * n] + got[2 * n:]
    value = jnp.where(iota((n, rows), 0) == (fam_ref[...] ^ here_ref[0]), value, 0.0)
    out_ref[...] = jnp.sum(value, axis=0, keepdims=True)


def shape(*dims, kind=F32):
    return jax.ShapeDtypeStruct(dims, kind)


def send(x, axis, by):
    return lax.ppermute(x, axis, [(i, i ^ by) for i in range(lax.axis_size(axis))])


def after(x, *deps):
    return lax.optimization_barrier((x,) + deps)[0]


def limit(mib):
    return pltpu.CompilerParams(vmem_limit_bytes=mib * MIB)


def on_device(embeddings, route, cluster):
    rows, width = embeddings.shape
    n, nb = lax.axis_size("grp"), lax.axis_size("blk")
    piece = rows // n
    grp, blk = lax.axis_index("grp"), lax.axis_index("blk")
    here = jnp.stack([grp, blk]).astype(I32)
    blocks = rows // LANES
    wide = -(-(piece + CLUSTERS - 1) // LANES) * LANES

    fam, rank, meta = pl.pallas_call(
        functools.partial(place_kernel, n, nb, piece, rows * nb),
        out_shape=[shape(1, rows, kind=I32)] * 2 + [shape(n * nb, 1, wide, kind=I32)],
        in_specs=[VMEM] * 2,
        out_specs=[VMEM] * 3,
        compiler_params=limit(16),
        name="place",
    )(route.reshape(blocks, LANES), cluster.reshape(blocks, LANES))

    sent = pl.pallas_call(
        functools.partial(pack_kernel, n, piece),
        out_shape=[shape(piece, width, kind=BF16)] * n,
        in_specs=[SMEM, VMEM, VMEM, VMEM],
        out_specs=[VMEM] * n,
        scratch_shapes=[pltpu.VMEM((rows, width), BF16)],
        compiler_params=limit(16),
        name="pack",
    )(here, embeddings, fam, rank)

    held = [None] * n
    def spread(own, across):
        return [own, send(own, "blk", 1), across, send(across, "blk", 1)]

    half = n // 2
    across = [None] * n
    own = [sent[0]] + [None] * (n - 1)
    own[half] = send(sent[half], "grp", half)
    own[half + 1] = send(sent[half + 1], "grp", half + 1)
    across[0] = send(own[0], "blk", 2)
    for d in range(1, half):
        own[d] = send(sent[d] if d < 3 else after(sent[d], own[d - 2]), "grp", d)
    for d in range(half + 2, n):
        own[d] = send(after(sent[d], own[d - 1 if d > half + 2 else half]), "grp", d)
    for d in range(1, n):
        across[d] = send(own[d] if d < 2 else after(own[d], across[d - 2]), "blk", 2)
    held = [spread(own[d], across[d]) for d in range(n)]

    heard = lax.all_to_all(
        after(meta, own[1]), ("grp", "blk"), split_axis=0, concat_axis=0, tiled=True
    )
    key_kinds, query_kinds = pl.pallas_call(
        functools.partial(kinds_kernel, n, nb, piece),
        out_shape=[shape(n * nb, piece, LANES), shape(n, 1, piece)],
        in_specs=[SMEM, VMEM],
        out_specs=[VMEM] * 2,
        compiler_params=limit(16),
        name="kinds",
    )(here, heard)

    cuts = [0, half, half + 2, half + 3, n] if n == 8 else list(range(0, n + 1, 8))
    state = []
    for lo, hi in zip(cuts, cuts[1:]):
        last = hi == n
        kept = [shape(n, nb, piece, width, kind=BF16), shape(n, 8, piece)]
        folds = sum(d + 1 for d in range(lo, hi))
        args = [here, key_kinds, query_kinds] + [p for d in range(lo, hi) for p in held[d]] + list(state)
        state = pl.pallas_call(
            functools.partial(stage_kernel, n, nb, piece, lo, hi),
            out_shape=([shape(1, piece)] * n if last else []) + kept,
            in_specs=[SMEM] + [VMEM] * (len(args) - 1),
            out_specs=[VMEM] * ((n if last else 0) + 2),
            input_output_aliases={
                len(args) - 2 + i: (n if last else 0) + i for i in range(2)
            } if lo else {},
            compiler_params=limit(12),
            cost_estimate=pl.CostEstimate(
                flops=folds * 2 * piece * piece * nb * width, bytes_accessed=0, transcendentals=0
            ),
            name="stage",
        )(*args)
    best = state[:n]

    home = [best[0]] + [send(best[d], "grp", d) for d in range(1, n)]
    out = pl.pallas_call(
        functools.partial(unpack_kernel, n, piece),
        out_shape=shape(1, rows),
        in_specs=[SMEM] + [VMEM] * (2 + n),
        out_specs=VMEM,
        compiler_params=limit(16),
        name="unpack",
    )(here, fam, rank, *home)
    return out.reshape(rows)


def solution(mesh):
    in_specs = (P(("grp", "blk"), None), P(("grp", "blk")), P("grp", "blk"))
    return jax.shard_map(
        on_device, mesh=mesh, in_specs=in_specs, out_specs=P(("grp", "blk")), check_vma=False
    )
```

time: 208 us -> 134 us (0.64)
  blocking collectives: 54.9 us -> 13.7 us
  waiting for transfers between devices: 67.9 us -> 39.3 us
  local copies, waits for them, and re-layouts: 21 us -> 2.35 us
  starting transfers between devices: 29.1 us -> 41.6 us
  Pallas kernels: 29.7 us -> 35.2 us
  other arithmetic: 4.61 us -> 1.41 us
    all_gather x1 -> x0, blocking collectives: 46.1 us -> none  [on_device(): everyone = lax.all_gather(meta, ('grp', 'blk'))]
    ppermute x31 -> x38, waiting for transfers between devices: 67.9 us -> 39.3 us  [send(): lax.ppermute(x, axis, [(i, i ^ by) for i in range(lax.axis_size(axis))])]
    ppermute x31 -> x38, starting transfers between devices: 29.1 us -> 41.6 us  [send(): lax.ppermute(x, axis, [(i, i ^ by) for i in range(lax.axis_size(axis))])]
    unnamed x33 -> x4, local copies, waits for them, and re-layouts: 9.55 us -> 2.35 us
    add x2 -> x0, local copies, waits for them, and re-layouts: 5.9 us -> none  [on_device(): kinds = kinds + (slots >= bounds[c]).astype(I32)]
    pallas_call x2 -> x6, Pallas kernels: 23.6 us -> 28.6 us  [the longest x4 20.7 us: on_device(): pl.pallas_call(functools.partial(stage_kernel, n, nb, piece, lo, hi), out...]
    all_to_all x1, blocking collectives: 8.88 us -> 13.7 us  [on_device(): lax.all_to_all(after(meta, own[1]), ('grp', 'blk'), split_axis=0, concat_...]
    slice x3 -> x0, local copies, waits for them, and re-layouts: 3.8 us -> none  [the longest x1 1.67 us: on_device(): slots = lax.dynamic_index_in_dim(everyone[:, :n], grp, 1, keepdims=False)]
  transfers between devices with their start and end apart: 31 -> 38, of which waited for: 10 -> 10; matrix products, arithmetic and copies ran while one was open for 7% -> 0% of each run, Pallas kernels for 0% -> 17%
where the time goes in v2:
time: 134 us
  starting transfers between devices  41.6 us (31%)
  waiting for transfers between devices  39.3 us (29%)
  Pallas kernels  35.2 us (26%)
  blocking collectives  13.7 us (10%)
  local copies, waits for them, and re-layouts  2.35 us (2%)
  other arithmetic  1.41 us (1%)
    ppermute x38, starting transfers between devices, send(): lax.ppermute(x, axis, [(i, i ^ by) for i in range(lax.axis_size(axis))])  41.6 us
    ppermute x38, waiting for transfers between devices, send(): lax.ppermute(x, axis, [(i, i ^ by) for i in range(lax.axis_size(axis))])  39.3 us
    pallas_call x4, Pallas kernels, on_device(): pl.pallas_call(functools.partial(stage_kernel, n, nb, piece, lo, hi), out...  20.7 us
    all_to_all x1, blocking collectives, on_device(): lax.all_to_all(after(meta, own[1]), ('grp', 'blk'), split_axis=0, concat_...  13.7 us
    pallas_call x1, Pallas kernels, on_device(): pl.pallas_call(functools.partial(kinds_kernel, n, nb, piece), out_shape=[...  7.23 us
    pallas_call x1, Pallas kernels, on_device(): pl.pallas_call(functools.partial(pack_kernel, n, piece), out_shape=[shape...  5.86 us
  transfers between devices with their start and end apart: 38, of which 10 were waited for; matrix products, arithmetic and copies ran while one was open for 0% of the time, Pallas kernels for 17%

profile of v2, /device:TPU:0, one launch (start us, length us, event | category | flops | bytes accessed | tf_op | source)
XLA Modules:
  0.0 133.7 jit_solution(1443235912906186355)
XLA Ops:
  2.1 1.7 %copy-done = bf16[1536,768]{1,0:T(8,128)(2,1)S(1)} copy-done((bf16[1536,768]{1,0:T(8,128)(2,1)S(1)}, bf16[1536,768]{1,0:T(8,128)(2,1)}, u32[]{:S(2)}) %copy-start) | copy-done | bytes 2359320
  3.8 5.9 %pack.1 = (bf16[192,768]{1,0:T(8,128)(2,1)S(1)}, bf16[192,768]{1,0:T(8,128)(2,1)S(1)}, bf16[192,768]{1,0:T(8,128)(2,1)S(1)}, bf16[192,768]{1,0:T(8,128)(2,1)S(1)...) custom-call(s32[2]{0:T(128)S(1)} %pad_add_fusion.here_ref, ...), custom_call_target="tpu_custom_call" | custom-call | tf_op jit(solution)/shard_map/pack/pallas_call | solution.py:235
  9.6 3.0 %collective-permute-start = (bf16[192,768]{1,0:T(8,128)(2,1)S(1)}, bf16[192,768]{1,0:T(8,128)(2,1)S(1)}, u32[]{:S(2)}, u32[]{:S(2)}) collective-permute-start(bf16[192,768]{1,0:T(8,128)(2,1)S(1)} %get-tuple-element.45), channel_id=1, source_target_pairs={{0,4},{4,0},{8,12},{12,8},{16,20},{20,16},{24,28},{28,24},{1,5},{5... | collective-permute-start | bytes 884744 | tf_op jit(solution)/shard_map/ppermute | solution.py:206
  12.6 1.5 %collective-permute-start.14 = (bf16[192,768]{1,0:T(8,128)(2,1)S(1)}, bf16[192,768]{1,0:T(8,128)(2,1)S(1)}, u32[]{:S(2)}, u32[]{:S(2)}) collective-permute-start(bf16[192,768]{1,0:T(8,128)(2,1)S(1)} %get-tuple-element.61.rest_0_), channel_id=1, source_target_pairs={{0,2},{1,3},{2,0},{3,1},{4,6},{5,7},{6,4},{7,5},{8,10},{9,11},{10,... | collective-permute-start | bytes 884744 | tf_op jit(solution)/shard_map/ppermute | solution.py:206
  14.2 1.6 %collective-permute-start.13 = (bf16[192,768]{1,0:T(8,128)(2,1)S(1)}, bf16[192,768]{1,0:T(8,128)(2,1)S(1)}, u32[]{:S(2)}, u32[]{:S(2)}) collective-permute-start(bf16[192,768]{1,0:T(8,128)(2,1)S(1)} %get-tuple-element.60), channel_id=1, source_target_pairs={{0,8},{4,12},{8,0},{12,4},{16,24},{20,28},{24,16},{28,20},{1,9},{5... | collective-permute-start | bytes 884744 | tf_op jit(solution)/shard_map/ppermute | solution.py:206
  15.7 2.6 %collective-permute-start.1 = (bf16[192,768]{1,0:T(8,128)(2,1)S(1)}, bf16[192,768]{1,0:T(8,128)(2,1)S(1)}, u32[]{:S(2)}, u32[]{:S(2)}) collective-permute-start(bf16[192,768]{1,0:T(8,128)(2,1)S(1)} %get-tuple-element.51), channel_id=1, source_target_pairs={{0,16},{4,20},{8,24},{12,28},{16,0},{20,4},{24,8},{28,12},{1,17},{... | collective-permute-start | bytes 884744 | tf_op jit(solution)/shard_map/ppermute | solution.py:206
  18.3 1.3 collective-permute-done.rest_4_
  19.6 2.8 %collective-permute-start.6 = (bf16[192,768]{1,0:T(8,128)(2,1)S(1)}, bf16[192,768]{1,0:T(8,128)(2,1)S(1)}, u32[]{:S(2)}, u32[]{:S(2)}) collective-permute-start(bf16[192,768]{1,0:T(8,128)(2,1)S(1)} %get-tuple-element.56), channel_id=1, source_target_pairs={{0,12},{4,8},{8,4},{12,0},{16,28},{20,24},{24,20},{28,16},{1,13},{... | collective-permute-start | bytes 884744 | tf_op jit(solution)/shard_map/ppermute | solution.py:206
  22.4 1.5 %collective-permute-start.7 = (bf16[192,768]{1,0:T(8,128)(2,1)S(1)}, bf16[192,768]{1,0:T(8,128)(2,1)S(1)}, u32[]{:S(2)}, u32[]{:S(2)}) collective-permute-start(bf16[192,768]{1,0:T(8,128)(2,1)S(1)} %collective-permute-done.rest_4_), channel_id=1, source_target_pairs={{0,2},{1,3},{2,0},{3,1},{4,6},{5,7},{6,4},{7,5},{8,10},{9,11},{10,... | collective-permute-start | bytes 884744 | tf_op jit(solution)/shard_map/ppermute | solution.py:206
  23.9 6.6 %collective-permute-done.13.rest_8_ = bf16[192,768]{1,0:T(8,128)(2,1)S(1)} collective-permute-done((bf16[192,768]{1,0:T(8,128)(2,1)S(1)}, bf16[192,768]{1,0:T(8,128)(2,1)S(1)}, u32[]{:S(2)}, u32[]{:S(2)}) %collective-permute-start.13) | collective-permute-done | bytes 294944 | tf_op jit(solution)/shard_map/ppermute | solution.py:206
  30.5 0.9 collective-permute-start.5
  31.9 7.8 %collective-permute-done.6.rest_12_ = bf16[192,768]{1,0:T(8,128)(2,1)S(1)} collective-permute-done((bf16[192,768]{1,0:T(8,128)(2,1)S(1)}, bf16[192,768]{1,0:T(8,128)(2,1)S(1)}, u32[]{:S(2)}, u32[]{:S(2)}) %collective-permute-start.6) | collective-permute-done | bytes 294944 | tf_op jit(solution)/shard_map/ppermute | solution.py:206
  39.7 2.7 %collective-permute-start.2 = (bf16[192,768]{1,0:T(8,128)(2,1)S(1)}, bf16[192,768]{1,0:T(8,128)(2,1)S(1)}, u32[]{:S(2)}, u32[]{:S(2)}) collective-permute-start(bf16[192,768]{1,0:T(8,128)(2,1)S(1)} %get-tuple-element.52), channel_id=1, source_target_pairs={{0,24},{4,28},{8,16},{12,20},{16,8},{20,12},{24,0},{28,4},{1,25},{... | collective-permute-start | bytes 884744 | tf_op jit(solution)/shard_map/ppermute | solution.py:206
  43.0 9.9 %collective-permute-done.5.rest_4_ = bf16[192,768]{1,0:T(8,128)(2,1)S(1)} collective-permute-done((bf16[192,768]{1,0:T(8,128)(2,1)S(1)}, bf16[192,768]{1,0:T(8,128)(2,1)S(1)}, u32[]{:S(2)}, u32[]{:S(2)}) %collective-permute-start.5) | collective-permute-done | bytes 294944 | tf_op jit(solution)/shard_map/ppermute | solution.py:206
  54.4 3.0 %collective-permute-start.3 = (bf16[192,768]{1,0:T(8,128)(2,1)S(1)}, bf16[192,768]{1,0:T(8,128)(2,1)S(1)}, u32[]{:S(2)}, u32[]{:S(2)}) collective-permute-start(bf16[192,768]{1,0:T(8,128)(2,1)S(1)} %get-tuple-element.53), channel_id=1, source_target_pairs={{0,28},{4,24},{8,20},{12,16},{16,12},{20,8},{24,4},{28,0},{1,29},{... | collective-permute-start | bytes 884744 | tf_op jit(solution)/shard_map/ppermute | solution.py:206
  57.4 1.5 %collective-permute-start.9 = (bf16[192,768]{1,0:T(8,128)(2,1)S(1)}, bf16[192,768]{1,0:T(8,128)(2,1)S(1)}, u32[]{:S(2)}, u32[]{:S(2)}) collective-permute-start(bf16[192,768]{1,0:T(8,128)(2,1)S(1)} %collective-permute-done.5.rest_4_), channel_id=1, source_target_pairs={{0,2},{1,3},{2,0},{3,1},{4,6},{5,7},{6,4},{7,5},{8,10},{9,11},{10,... | collective-permute-start | bytes 884744 | tf_op jit(solution)/shard_map/ppermute | solution.py:206
  59.4 4.3 %collective-permute-done.16.rest_2_ = bf16[192,768]{1,0:T(8,128)(2,1)S(1)} collective-permute-done((bf16[192,768]{1,0:T(8,128)(2,1)S(1)}, bf16[192,768]{1,0:T(8,128)(2,1)S(1)}, u32[]{:S(2)}, u32[]{:S(2)}) %collective-permute-start.16) | collective-permute-done | bytes 294944 | tf_op jit(solution)/shard_map/ppermute | solution.py:206
  63.8 2.5 %collective-permute-done.3.rest_0_ = bf16[192,768]{1,0:T(8,128)(2,1)S(1)} collective-permute-done((bf16[192,768]{1,0:T(8,128)(2,1)S(1)}, bf16[192,768]{1,0:T(8,128)(2,1)S(1)}, u32[]{:S(2)}, u32[]{:S(2)}) %collective-permute-start.3) | collective-permute-done | bytes 294944 | tf_op jit(solution)/shard_map/ppermute | solution.py:206
  66.3 2.9 %collective-permute-done.9.rest_6_ = bf16[192,768]{1,0:T(8,128)(2,1)S(1)} collective-permute-done((bf16[192,768]{1,0:T(8,128)(2,1)S(1)}, bf16[192,768]{1,0:T(8,128)(2,1)S(1)}, u32[]{:S(2)}, u32[]{:S(2)}) %collective-permute-start.9) | collective-permute-done | bytes 294944 | tf_op jit(solution)/shard_map/ppermute | solution.py:206
  69.7 1.6 %collective-permute-start.10 = (bf16[192,768]{1,0:T(8,128)(2,1)S(1)}, bf16[192,768]{1,0:T(8,128)(2,1)S(1)}, u32[]{:S(2)}, u32[]{:S(2)}) collective-permute-start(bf16[192,768]{1,0:T(8,128)(2,1)S(1)} %collective-permute-done.3.rest_0_), channel_id=1, source_target_pairs={{0,2},{1,3},{2,0},{3,1},{4,6},{5,7},{6,4},{7,5},{8,10},{9,11},{10,... | collective-permute-start | bytes 884744 | tf_op jit(solution)/shard_map/ppermute | solution.py:206
  71.5 13.7 %all_to_all.5.meta_ref = s32[32,1,256]{2,1,0:T(1,128)S(1)} all-to-all(s32[32,1,256]{2,1,0:T(1,128)S(1)} %get-tuple-element.46), channel_id=1, replica_groups=mesh['grp'=8,'blk'=4] {'grp','blk'}, dimensions={0} | all-to-all | bytes 65536 | tf_op jit(solution)/shard_map/all_to_all | solution.py:263
  85.1 7.2 %kinds.1 = (f32[32,192,128]{2,1,0:T(8,128)S(1)}, f32[8,1,192]{2,1,0:T(1,128)S(1)}) custom-call(s32[2]{0:T(128)S(1)} %pad_add_fusion.here_ref, s32[32,1,256]{2,1,0:T(1,128)S(1)} %all_to_all.5.meta_ref), custom_call_target="tpu_custom_call" | custom-call | tf_op jit(solution)/shard_map/kinds/pallas_call | solution.py:266
  93.0 5.8 %stage.4 = (bf16[8,4,192,768]{3,2,1,0:T(8,128)(2,1)S(1)}, f32[8,8,192]{2,1,0:T(8,128)S(1)}) custom-call(s32[2]{0:T(128)S(1)} %pad_add_fusion.here_ref, f32[32,192,128]{2,1,0:T(8,128)S(1)} %get-tuple-element.47.kcl_ref, f32[8,1,192]{2,1,0:T(1,128)S(1)} %get-tuple-element.48.qcl_ref, bf16[192,768]{1,0:T(8,128)(2,1)S(1)} %get-tuple-element.61.rest_0_, ...), custom_call_target="tpu_custom_call" | custom-call | flops 2264924160 | tf_op jit(solution)/shard_map/stage/pallas_call | solution.py:282
  99.4 6.2 %stage.5 = (bf16[8,4,192,768]{3,2,1,0:T(8,128)(2,1)S(1)}, f32[8,8,192]{2,1,0:T(8,128)S(1)}) custom-call(s32[2]{0:T(128)S(1)} %pad_add_fusion.here_ref, f32[32,192,128]{2,1,0:T(8,128)S(1)} %get-tuple-element.47.kcl_ref, f32[8,1,192]{2,1,0:T(1,128)S(1)} %get-tuple-element.48.qcl_ref, ...), custom_call_target="tpu_custom_call", output_to_operand_aliasing={{0}: (11, {}), {1}: (12, {})} | custom-call | flops 2491416576 | tf_op jit(solution)/shard_map/stage/pallas_call | solution.py:282
  105.6 4.1 %stage.6 = (bf16[8,4,192,768]{3,2,1,0:T(8,128)(2,1)S(1)}, f32[8,8,192]{2,1,0:T(8,128)S(1)}) custom-call(s32[2]{0:T(128)S(1)} %pad_add_fusion.here_ref, f32[32,192,128]{2,1,0:T(8,128)S(1)} %get-tuple-element.47.kcl_ref, f32[8,1,192]{2,1,0:T(1,128)S(1)} %get-tuple-element.48.qcl_ref, ...), custom_call_target="tpu_custom_call", output_to_operand_aliasing={{0}: (7, {}), {1}: (8, {})} | custom-call | flops 1585446912 | tf_op jit(solution)/shard_map/stage/pallas_call | solution.py:282
  109.7 4.6 %stage.7 = (f32[1,192]{1,0:T(1,128)S(1)}, f32[1,192]{1,0:T(1,128)S(1)}, f32[1,192]{1,0:T(1,128)S(1)}, f32[1,192]{1,0:T(1,128)S(1)}, f32[1,192]{1,0:T(1,128)S(1)}...) custom-call(s32[2]{0:T(128)S(1)} %pad_add_fusion.here_ref, ...), custom_call_target="tpu_custom_call", output_to_operand_aliasing={{8}: (7, {}), {9}: (8, {})} | custom-call | flops 1811939328 | tf_op jit(solution)/shard_map/stage/pallas_call | solution.py:282
  115.0 4.2 %collective-permute-start.32 = (f32[1,192]{1,0:T(1,128)S(1)}, f32[1,192]{1,0:T(1,128)S(1)}, u32[]{:S(2)}, u32[]{:S(2)}) collective-permute-start(f32[1,192]{1,0:T(1,128)S(1)} %get-tuple-element.73), channel_id=1, source_target_pairs={{0,8},{4,12},{8,0},{12,4},{16,24},{20,28},{24,16},{28,20},{1,9},{5... | collective-permute-start | bytes 2312 | tf_op jit(solution)/shard_map/ppermute | solution.py:206
  119.2 0.8 collective-permute-start.33
  120.0 3.7 %collective-permute-start.34 = (f32[1,192]{1,0:T(1,128)S(1)}, f32[1,192]{1,0:T(1,128)S(1)}, u32[]{:S(2)}, u32[]{:S(2)}) collective-permute-start(f32[1,192]{1,0:T(1,128)S(1)} %get-tuple-element.75), channel_id=1, source_target_pairs={{0,16},{4,20},{8,24},{12,28},{16,0},{20,4},{24,8},{28,12},{1,17},{... | collective-permute-start | bytes 2312 | tf_op jit(solution)/shard_map/ppermute | solution.py:206
  123.7 2.4 %collective-permute-start.36 = (f32[1,192]{1,0:T(1,128)S(1)}, f32[1,192]{1,0:T(1,128)S(1)}, u32[]{:S(2)}, u32[]{:S(2)}) collective-permute-start(f32[1,192]{1,0:T(1,128)S(1)} %get-tuple-element.77), channel_id=1, source_target_pairs={{0,24},{4,28},{8,16},{12,20},{16,8},{20,12},{24,0},{28,4},{1,25},{... | collective-permute-start | bytes 2312 | tf_op jit(solution)/shard_map/ppermute | solution.py:206
  126.0 2.4 %collective-permute-start.37 = (f32[1,192]{1,0:T(1,128)S(1)}, f32[1,192]{1,0:T(1,128)S(1)}, u32[]{:S(2)}, u32[]{:S(2)}) collective-permute-start(f32[1,192]{1,0:T(1,128)S(1)} %get-tuple-element.78), channel_id=1, source_target_pairs={{0,28},{4,24},{8,20},{12,16},{16,12},{20,8},{24,4},{28,0},{1,29},{... | collective-permute-start | bytes 2312 | tf_op jit(solution)/shard_map/ppermute | solution.py:206
  129.0 3.3 %collective-permute-done.37.rest_7_ = f32[1,192]{1,0:T(1,128)S(1)} collective-permute-done((f32[1,192]{1,0:T(1,128)S(1)}, f32[1,192]{1,0:T(1,128)S(1)}, u32[]{:S(2)}, u32[]{:S(2)}) %collective-permute-start.37) | collective-permute-done | bytes 800 | tf_op jit(solution)/shard_map/ppermute | solution.py:206
  (60 shorter events, 9.7 us)
Async XLA Ops:
  9.6 10.0 %collective-permute-start = (bf16[192,768]{1,0:T(8,128)(2,1)S(1)}, bf16[192,768]{1,0:T(8,128)(2,1)S(1)}, u32[]{:S(2)}, u32[]{:S(2)}) collective-permute-start(bf16[192,768]{1,0:T(8,128)(2,1)S(1)} %get-tuple-element.45), channel_id=1, source_target_pairs={{0,4},{4,0},{8,12},{12,8},{16,20},{20,16},{24,28},{28,24},{1,5},{5... | collective-permute-start | bytes 884744 | tf_op jit(solution)/shard_map/ppermute | solution.py:206
  12.6 11.3 %collective-permute-start.14 = (bf16[192,768]{1,0:T(8,128)(2,1)S(1)}, bf16[192,768]{1,0:T(8,128)(2,1)S(1)}, u32[]{:S(2)}, u32[]{:S(2)}) collective-permute-start(bf16[192,768]{1,0:T(8,128)(2,1)S(1)} %get-tuple-element.61.rest_0_), channel_id=1, source_target_pairs={{0,2},{1,3},{2,0},{3,1},{4,6},{5,7},{6,4},{7,5},{8,10},{9,11},{10,... | collective-permute-start | bytes 884744 | tf_op jit(solution)/shard_map/ppermute | solution.py:206
  14.2 16.3 %collective-permute-start.13 = (bf16[192,768]{1,0:T(8,128)(2,1)S(1)}, bf16[192,768]{1,0:T(8,128)(2,1)S(1)}, u32[]{:S(2)}, u32[]{:S(2)}) collective-permute-start(bf16[192,768]{1,0:T(8,128)(2,1)S(1)} %get-tuple-element.60), channel_id=1, source_target_pairs={{0,8},{4,12},{8,0},{12,4},{16,24},{20,28},{24,16},{28,20},{1,9},{5... | collective-permute-start | bytes 884744 | tf_op jit(solution)/shard_map/ppermute | solution.py:206
  15.7 15.7 %collective-permute-start.1 = (bf16[192,768]{1,0:T(8,128)(2,1)S(1)}, bf16[192,768]{1,0:T(8,128)(2,1)S(1)}, u32[]{:S(2)}, u32[]{:S(2)}) collective-permute-start(bf16[192,768]{1,0:T(8,128)(2,1)S(1)} %get-tuple-element.51), channel_id=1, source_target_pairs={{0,16},{4,20},{8,24},{12,28},{16,0},{20,4},{24,8},{28,12},{1,17},{... | collective-permute-start | bytes 884744 | tf_op jit(solution)/shard_map/ppermute | solution.py:206
  19.6 20.0 %collective-permute-start.6 = (bf16[192,768]{1,0:T(8,128)(2,1)S(1)}, bf16[192,768]{1,0:T(8,128)(2,1)S(1)}, u32[]{:S(2)}, u32[]{:S(2)}) collective-permute-start(bf16[192,768]{1,0:T(8,128)(2,1)S(1)} %get-tuple-element.56), channel_id=1, source_target_pairs={{0,12},{4,8},{8,4},{12,0},{16,28},{20,24},{24,20},{28,16},{1,13},{... | collective-permute-start | bytes 884744 | tf_op jit(solution)/shard_map/ppermute | solution.py:206
  22.4 20.0 %collective-permute-start.7 = (bf16[192,768]{1,0:T(8,128)(2,1)S(1)}, bf16[192,768]{1,0:T(8,128)(2,1)S(1)}, u32[]{:S(2)}, u32[]{:S(2)}) collective-permute-start(bf16[192,768]{1,0:T(8,128)(2,1)S(1)} %collective-permute-done.rest_4_), channel_id=1, source_target_pairs={{0,2},{1,3},{2,0},{3,1},{4,6},{5,7},{6,4},{7,5},{8,10},{9,11},{10,... | collective-permute-start | bytes 884744 | tf_op jit(solution)/shard_map/ppermute | solution.py:206
  23.9 18.5 %collective-permute-start.23 = (bf16[192,768]{1,0:T(8,128)(2,1)S(1)}, bf16[192,768]{1,0:T(8,128)(2,1)S(1)}, u32[]{:S(2)}, u32[]{:S(2)}) collective-permute-start(bf16[192,768]{1,0:T(8,128)(2,1)S(1)} %get-tuple-element.61.rest_0_), channel_id=1, source_target_pairs={{0,1},{1,0},{2,3},{3,2},{4,5},{5,4},{6,7},{7,6},{8,9},{9,8},{10,11... | collective-permute-start | bytes 884744 | tf_op jit(solution)/shard_map/ppermute | solution.py:206
  30.5 22.4 %collective-permute-start.5 = (bf16[192,768]{1,0:T(8,128)(2,1)S(1)}, bf16[192,768]{1,0:T(8,128)(2,1)S(1)}, u32[]{:S(2)}, u32[]{:S(2)}) collective-permute-start(bf16[192,768]{1,0:T(8,128)(2,1)S(1)} %get-tuple-element.54), channel_id=1, source_target_pairs={{0,20},{4,16},{8,28},{12,24},{16,4},{20,0},{24,12},{28,8},{1,21},{... | collective-permute-start | bytes 884744 | tf_op jit(solution)/shard_map/ppermute | solution.py:206
  31.4 21.5 %collective-permute-start.15 = (bf16[192,768]{1,0:T(8,128)(2,1)S(1)}, bf16[192,768]{1,0:T(8,128)(2,1)S(1)}, u32[]{:S(2)}, u32[]{:S(2)}) collective-permute-start(bf16[192,768]{1,0:T(8,128)(2,1)S(1)} %collective-permute-done.13.rest_8_), channel_id=1, source_target_pairs={{0,2},{1,3},{2,0},{3,1},{4,6},{5,7},{6,4},{7,5},{8,10},{9,11},{10,... | collective-permute-start | bytes 884744 | tf_op jit(solution)/shard_map/ppermute | solution.py:206
  39.7 13.8 %collective-permute-start.2 = (bf16[192,768]{1,0:T(8,128)(2,1)S(1)}, bf16[192,768]{1,0:T(8,128)(2,1)S(1)}, u32[]{:S(2)}, u32[]{:S(2)}) collective-permute-start(bf16[192,768]{1,0:T(8,128)(2,1)S(1)} %get-tuple-element.52), channel_id=1, source_target_pairs={{0,24},{4,28},{8,16},{12,20},{16,8},{20,12},{24,0},{28,4},{1,25},{... | collective-permute-start | bytes 884744 | tf_op jit(solution)/shard_map/ppermute | solution.py:206
  42.4 11.0 %collective-permute-start.24 = (bf16[192,768]{1,0:T(8,128)(2,1)S(1)}, bf16[192,768]{1,0:T(8,128)(2,1)S(1)}, u32[]{:S(2)}, u32[]{:S(2)}) collective-permute-start(bf16[192,768]{1,0:T(8,128)(2,1)S(1)} %collective-permute-done.14.rest_2_), channel_id=1, source_target_pairs={{0,1},{1,0},{2,3},{3,2},{4,5},{5,4},{6,7},{7,6},{8,9},{9,8},{10,11... | collective-permute-start | bytes 884744 | tf_op jit(solution)/shard_map/ppermute | solution.py:206
  42.4 11.5 %collective-permute-start.8 = (bf16[192,768]{1,0:T(8,128)(2,1)S(1)}, bf16[192,768]{1,0:T(8,128)(2,1)S(1)}, u32[]{:S(2)}, u32[]{:S(2)}) collective-permute-start(bf16[192,768]{1,0:T(8,128)(2,1)S(1)} %collective-permute-done.6.rest_12_), channel_id=1, source_target_pairs={{0,2},{1,3},{2,0},{3,1},{4,6},{5,7},{6,4},{7,5},{8,10},{9,11},{10,... | collective-permute-start | bytes 884744 | tf_op jit(solution)/shard_map/ppermute | solution.py:206
  53.9 9.9 %collective-permute-start.16 = (bf16[192,768]{1,0:T(8,128)(2,1)S(1)}, bf16[192,768]{1,0:T(8,128)(2,1)S(1)}, u32[]{:S(2)}, u32[]{:S(2)}) collective-permute-start(bf16[192,768]{1,0:T(8,128)(2,1)S(1)} %collective-permute-done.1.rest_0_), channel_id=1, source_target_pairs={{0,2},{1,3},{2,0},{3,1},{4,6},{5,7},{6,4},{7,5},{8,10},{9,11},{10,... | collective-permute-start | bytes 884744 | tf_op jit(solution)/shard_map/ppermute | solution.py:206
  54.4 11.8 %collective-permute-start.3 = (bf16[192,768]{1,0:T(8,128)(2,1)S(1)}, bf16[192,768]{1,0:T(8,128)(2,1)S(1)}, u32[]{:S(2)}, u32[]{:S(2)}) collective-permute-start(bf16[192,768]{1,0:T(8,128)(2,1)S(1)} %get-tuple-element.53), channel_id=1, source_target_pairs={{0,28},{4,24},{8,20},{12,16},{16,12},{20,8},{24,4},{28,0},{1,29},{... | collective-permute-start | bytes 884744 | tf_op jit(solution)/shard_map/ppermute | solution.py:206
  57.4 11.8 %collective-permute-start.9 = (bf16[192,768]{1,0:T(8,128)(2,1)S(1)}, bf16[192,768]{1,0:T(8,128)(2,1)S(1)}, u32[]{:S(2)}, u32[]{:S(2)}) collective-permute-start(bf16[192,768]{1,0:T(8,128)(2,1)S(1)} %collective-permute-done.5.rest_4_), channel_id=1, source_target_pairs={{0,2},{1,3},{2,0},{3,1},{4,6},{5,7},{6,4},{7,5},{8,10},{9,11},{10,... | collective-permute-start | bytes 884744 | tf_op jit(solution)/shard_map/ppermute | solution.py:206
  58.9 10.7 %collective-permute-start.28 = (bf16[192,768]{1,0:T(8,128)(2,1)S(1)}, bf16[192,768]{1,0:T(8,128)(2,1)S(1)}, u32[]{:S(2)}, u32[]{:S(2)}) collective-permute-start(bf16[192,768]{1,0:T(8,128)(2,1)S(1)} %collective-permute-done.15.rest_10_), channel_id=1, source_target_pairs={{0,1},{1,0},{2,3},{3,2},{4,5},{5,4},{6,7},{7,6},{8,9},{9,8},{10,11... | collective-permute-start | bytes 884744 | tf_op jit(solution)/shard_map/ppermute | solution.py:206
  58.9 10.7 %collective-permute-start.29 = (bf16[192,768]{1,0:T(8,128)(2,1)S(1)}, bf16[192,768]{1,0:T(8,128)(2,1)S(1)}, u32[]{:S(2)}, u32[]{:S(2)}) collective-permute-start(bf16[192,768]{1,0:T(8,128)(2,1)S(1)} %collective-permute-done.6.rest_12_), channel_id=1, source_target_pairs={{0,1},{1,0},{2,3},{3,2},{4,5},{5,4},{6,7},{7,6},{8,9},{9,8},{10,11... | collective-permute-start | bytes 884744 | tf_op jit(solution)/shard_map/ppermute | solution.py:206
  63.8 7.5 %collective-permute-start.26 = (bf16[192,768]{1,0:T(8,128)(2,1)S(1)}, bf16[192,768]{1,0:T(8,128)(2,1)S(1)}, u32[]{:S(2)}, u32[]{:S(2)}) collective-permute-start(bf16[192,768]{1,0:T(8,128)(2,1)S(1)} %collective-permute-done.7.rest_6_), channel_id=1, source_target_pairs={{0,1},{1,0},{2,3},{3,2},{4,5},{5,4},{6,7},{7,6},{8,9},{9,8},{10,11... | collective-permute-start | bytes 884744 | tf_op jit(solution)/shard_map/ppermute | solution.py:206
  66.3 26.1 %collective-permute-start.30 = (bf16[192,768]{1,0:T(8,128)(2,1)S(1)}, bf16[192,768]{1,0:T(8,128)(2,1)S(1)}, u32[]{:S(2)}, u32[]{:S(2)}) collective-permute-start(bf16[192,768]{1,0:T(8,128)(2,1)S(1)} %collective-permute-done.8.rest_14_), channel_id=1, source_target_pairs={{0,1},{1,0},{2,3},{3,2},{4,5},{5,4},{6,7},{7,6},{8,9},{9,8},{10,11... | collective-permute-start | bytes 884744 | tf_op jit(solution)/shard_map/ppermute | solution.py:206
  69.2 23.3 %collective-permute-start.17 = (bf16[192,768]{1,0:T(8,128)(2,1)S(1)}, bf16[192,768]{1,0:T(8,128)(2,1)S(1)}, u32[]{:S(2)}, u32[]{:S(2)}) collective-permute-start(bf16[192,768]{1,0:T(8,128)(2,1)S(1)} %collective-permute-done.2.rest_0_), channel_id=1, source_target_pairs={{0,2},{1,3},{2,0},{3,1},{4,6},{5,7},{6,4},{7,5},{8,10},{9,11},{10,... | collective-permute-start | bytes 884744 | tf_op jit(solution)/shard_map/ppermute | solution.py:206
  69.7 29.1 %collective-permute-start.20 = (bf16[192,768]{1,0:T(8,128)(2,1)S(1)}, bf16[192,768]{1,0:T(8,128)(2,1)S(1)}, u32[]{:S(2)}, u32[]{:S(2)}) collective-permute-start(bf16[192,768]{1,0:T(8,128)(2,1)S(1)} %collective-permute-done.16.rest_2_), channel_id=1, source_target_pairs={{0,1},{1,0},{2,3},{3,2},{4,5},{5,4},{6,7},{7,6},{8,9},{9,8},{10,11... | collective-permute-start | bytes 884744 | tf_op jit(solution)/shard_map/ppermute | solution.py:206
  69.7 29.3 %collective-permute-start.10 = (bf16[192,768]{1,0:T(8,128)(2,1)S(1)}, bf16[192,768]{1,0:T(8,128)(2,1)S(1)}, u32[]{:S(2)}, u32[]{:S(2)}) collective-permute-start(bf16[192,768]{1,0:T(8,128)(2,1)S(1)} %collective-permute-done.3.rest_0_), channel_id=1, source_target_pairs={{0,2},{1,3},{2,0},{3,1},{4,6},{5,7},{6,4},{7,5},{8,10},{9,11},{10,... | collective-permute-start | bytes 884744 | tf_op jit(solution)/shard_map/ppermute | solution.py:206
  71.3 28.1 %collective-permute-start.22 = (bf16[192,768]{1,0:T(8,128)(2,1)S(1)}, bf16[192,768]{1,0:T(8,128)(2,1)S(1)}, u32[]{:S(2)}, u32[]{:S(2)}) collective-permute-start(bf16[192,768]{1,0:T(8,128)(2,1)S(1)} %collective-permute-done.9.rest_6_), channel_id=1, source_target_pairs={{0,1},{1,0},{2,3},{3,2},{4,5},{5,4},{6,7},{7,6},{8,9},{9,8},{10,11... | collective-permute-start | bytes 884744 | tf_op jit(solution)/shard_map/ppermute | solution.py:206
  92.4 13.2 %collective-permute-start.12 = (bf16[192,768]{1,0:T(8,128)(2,1)S(1)}, bf16[192,768]{1,0:T(8,128)(2,1)S(1)}, u32[]{:S(2)}, u32[]{:S(2)}) collective-permute-start(bf16[192,768]{1,0:T(8,128)(2,1)S(1)} %collective-permute-done.2.rest_0_), channel_id=1, source_target_pairs={{0,1},{1,0},{2,3},{3,2},{4,5},{5,4},{6,7},{7,6},{8,9},{9,8},{10,11... | collective-permute-start | bytes 884744 | tf_op jit(solution)/shard_map/ppermute | solution.py:206
  92.6 13.0 %collective-permute-start.18 = (bf16[192,768]{1,0:T(8,128)(2,1)S(1)}, bf16[192,768]{1,0:T(8,128)(2,1)S(1)}, u32[]{:S(2)}, u32[]{:S(2)}) collective-permute-start(bf16[192,768]{1,0:T(8,128)(2,1)S(1)} %collective-permute-done.17.rest_2_), channel_id=1, source_target_pairs={{0,1},{1,0},{2,3},{3,2},{4,5},{5,4},{6,7},{7,6},{8,9},{9,8},{10,11... | collective-permute-start | bytes 884744 | tf_op jit(solution)/shard_map/ppermute | solution.py:206
  98.8 10.9 %collective-permute-start.4 = (bf16[192,768]{1,0:T(8,128)(2,1)S(1)}, bf16[192,768]{1,0:T(8,128)(2,1)S(1)}, u32[]{:S(2)}, u32[]{:S(2)}) collective-permute-start(bf16[192,768]{1,0:T(8,128)(2,1)S(1)} %collective-permute-done.3.rest_0_), channel_id=1, source_target_pairs={{0,1},{1,0},{2,3},{3,2},{4,5},{5,4},{6,7},{7,6},{8,9},{9,8},{10,11... | collective-permute-start | bytes 884744 | tf_op jit(solution)/shard_map/ppermute | solution.py:206
  99.0 10.7 %collective-permute-start.11 = (bf16[192,768]{1,0:T(8,128)(2,1)S(1)}, bf16[192,768]{1,0:T(8,128)(2,1)S(1)}, u32[]{:S(2)}, u32[]{:S(2)}) collective-permute-start(bf16[192,768]{1,0:T(8,128)(2,1)S(1)} %collective-permute-done.10.rest_2_), channel_id=1, source_target_pairs={{0,1},{1,0},{2,3},{3,2},{4,5},{5,4},{6,7},{7,6},{8,9},{9,8},{10,11... | collective-permute-start | bytes 884744 | tf_op jit(solution)/shard_map/ppermute | solution.py:206
  114.4 9.3 %collective-permute-start.31 = (f32[1,192]{1,0:T(1,128)S(1)}, f32[1,192]{1,0:T(1,128)S(1)}, u32[]{:S(2)}, u32[]{:S(2)}) collective-permute-start(f32[1,192]{1,0:T(1,128)S(1)} %get-tuple-element.72), channel_id=1, source_target_pairs={{0,4},{4,0},{8,12},{12,8},{16,20},{20,16},{24,28},{28,24},{1,5},{5... | collective-permute-start | bytes 2312 | tf_op jit(solution)/shard_map/ppermute | solution.py:206
  115.0 11.0 %collective-permute-start.32 = (f32[1,192]{1,0:T(1,128)S(1)}, f32[1,192]{1,0:T(1,128)S(1)}, u32[]{:S(2)}, u32[]{:S(2)}) collective-permute-start(f32[1,192]{1,0:T(1,128)S(1)} %get-tuple-element.73), channel_id=1, source_target_pairs={{0,8},{4,12},{8,0},{12,4},{16,24},{20,28},{24,16},{28,20},{1,9},{5... | collective-permute-start | bytes 2312 | tf_op jit(solution)/shard_map/ppermute | solution.py:206
  119.2 9.2 %collective-permute-start.33 = (f32[1,192]{1,0:T(1,128)S(1)}, f32[1,192]{1,0:T(1,128)S(1)}, u32[]{:S(2)}, u32[]{:S(2)}) collective-permute-start(f32[1,192]{1,0:T(1,128)S(1)} %get-tuple-element.74), channel_id=1, source_target_pairs={{0,12},{4,8},{8,4},{12,0},{16,28},{20,24},{24,20},{28,16},{1,13},{... | collective-permute-start | bytes 2312 | tf_op jit(solution)/shard_map/ppermute | solution.py:206
  120.0 8.4 %collective-permute-start.34 = (f32[1,192]{1,0:T(1,128)S(1)}, f32[1,192]{1,0:T(1,128)S(1)}, u32[]{:S(2)}, u32[]{:S(2)}) collective-permute-start(f32[1,192]{1,0:T(1,128)S(1)} %get-tuple-element.75), channel_id=1, source_target_pairs={{0,16},{4,20},{8,24},{12,28},{16,0},{20,4},{24,8},{28,12},{1,17},{... | collective-permute-start | bytes 2312 | tf_op jit(solution)/shard_map/ppermute | solution.py:206
  126.0 6.3 %collective-permute-start.37 = (f32[1,192]{1,0:T(1,128)S(1)}, f32[1,192]{1,0:T(1,128)S(1)}, u32[]{:S(2)}, u32[]{:S(2)}) collective-permute-start(f32[1,192]{1,0:T(1,128)S(1)} %get-tuple-element.78), channel_id=1, source_target_pairs={{0,28},{4,24},{8,20},{12,16},{16,12},{20,8},{24,4},{28,0},{1,29},{... | collective-permute-start | bytes 2312 | tf_op jit(solution)/shard_map/ppermute | solution.py:206
  (8 other events, 30.3 us)

commit v3 on v1

v3 whole, which is shorter than its diff:
```python
import functools

import jax
import jax.numpy as jnp
from jax import lax
from jax.experimental import pallas as pl
from jax.experimental.pallas import tpu as pltpu
from jax.sharding import PartitionSpec as P

BF16, F32, I32 = jnp.bfloat16, jnp.float32, jnp.int32
LANES = 128
CLUSTERS = 4
NOTE = 8
VMEM = pl.BlockSpec(memory_space=pltpu.VMEM)
SMEM = pl.BlockSpec(memory_space=pltpu.SMEM)
ANY = pl.BlockSpec(memory_space=pl.ANY)
MIB = 1 << 20


def dot_nt(a, b):
    return lax.dot_general(a, b, (((1,), (1,)), ((), ())), preferred_element_type=F32)


def iota(shape, dim):
    return lax.broadcasted_iota(I32, shape, dim)


def one_hot(match):
    return jnp.where(match, 1.0, 0.0).astype(BF16)


def digits(x):
    return [(x >> 6).astype(F32), (x & 63).astype(F32)]


def places(n, family_rows, route):
    blocks = route.shape[0]
    fam = jnp.zeros_like(route)
    for f in range(1, n):
        fam = fam + jnp.where(route >= f * family_rows, 1, 0)
    rel = route - fam * family_rows
    pad = -blocks % 16
    tall = blocks + pad
    fam_pad = jnp.concatenate([fam, jnp.full((pad, LANES), -1, I32)], axis=0) if pad else fam
    member = jnp.concatenate([jnp.where(fam_pad == f, 1.0, 0.0) for f in range(n)], axis=0)
    member_low = member.astype(BF16)
    before = one_hot(iota((LANES, LANES), 0) < iota((LANES, LANES), 1))
    within = jnp.dot(member_low, before, preferred_element_type=F32)
    totals = jnp.dot(member_low, jnp.ones((LANES, LANES), BF16), preferred_element_type=F32)
    size = n * tall
    shift = tall.bit_length() - 1
    row, col = iota((size, size), 0), iota((size, size), 1)
    above = one_hot(((row >> shift) == (col >> shift)) & (col < row))
    ranks = within + jnp.dot(above, totals.astype(BF16), preferred_element_type=F32)
    ranks = ranks * member
    rank = jnp.zeros((tall, LANES), F32)
    for f in range(n):
        rank = rank + ranks[f * tall:(f + 1) * tall]
    rank = rank.astype(I32)

    def as_row(x):
        return jnp.concatenate([x[i:i + 1] for i in range(blocks)], axis=1)

    return as_row(fam), as_row(rank), as_row(rel)


def pack(n, piece, which, grp, unit_ref, fam_row, rank_row, note_ref, outs):
    rows, width = unit_ref.shape
    pos = (fam_row ^ grp) * piece + rank_row
    for d, out in zip(which, outs):
        select = one_hot(iota((piece, rows), 0) + d * piece == pos)
        got = jnp.dot(select, unit_ref[...], preferred_element_type=F32)
        note = note_ref[grp ^ d]
        note = jnp.concatenate([note, jnp.zeros((NOTE, width - note.shape[1]), F32)], axis=1)
        out[...] = jnp.concatenate([got, note], axis=0).astype(BF16)


def first_kernel(n, piece, family_rows, which, here_ref, route_ref, cluster_ref, emb_ref, *rest):
    fam_ref, rank_ref, note_ref, unit_ref = rest[:4]
    outs = rest[4:4 + len(which)]
    rows = emb_ref.shape[0]
    fam_row, rank_row, rel_row = places(n, family_rows, route_ref[...])
    fam_ref[...] = fam_row
    rank_ref[...] = rank_row
    mine = iota((n, rows), 0) == fam_row
    high, low = [jnp.where(mine, x, 0.0) for x in digits(rel_row)]
    at_rank = one_hot(iota((piece, rows), 0) == rank_row)
    slots = dot_nt(jnp.concatenate([high, low], axis=0).astype(BF16), at_rank)
    cluster = cluster_ref[...]
    counts = []
    for c in range(CLUSTERS - 1):
        total = jnp.sum(jnp.where(cluster <= c, 1.0, 0.0), axis=1, keepdims=True)
        counts += digits(jnp.broadcast_to(total, (1, piece)).astype(I32))
    counts = jnp.concatenate(counts, axis=0)
    spare = note_ref.shape[-1] - piece
    for f in range(n):
        note = jnp.concatenate([slots[f:f + 1], slots[n + f:n + f + 1], counts], axis=0)
        if spare:
            note = jnp.concatenate([note, jnp.zeros((NOTE, spare), F32)], axis=1)
        note_ref[f] = note

    @pl.loop(0, rows // 128)
    def _(i):
        at = pl.ds(pl.multiple_of(i * 128, 128), 128)
        x = emb_ref[at, :].astype(F32)
        total = jnp.sum(x * x, axis=1, keepdims=True)
        unit_ref[at, :] = (x * lax.rsqrt(total + 1e-06)).astype(BF16)

    pack(n, piece, which, here_ref[0], unit_ref, fam_row, rank_row, note_ref, outs)


def second_kernel(n, piece, which, here_ref, fam_ref, rank_ref, note_ref, unit_ref, *outs):
    pack(n, piece, which, here_ref[0], unit_ref, fam_ref[...], rank_ref[...], note_ref, outs)


def stage_kernel(n, nb, piece, lo, hi, here_ref, *rest):
    count = hi - lo
    home = rest[:nb]
    pieces = [rest[(1 + i) * nb:(2 + i) * nb] for i in range(count)]
    rest = rest[(1 + count) * nb + (4 if lo else 0):]
    out_ref, keys, best, key_kinds, query_kinds = rest
    grp, blk = here_ref[0], here_ref[1]
    width = keys.shape[-1]
    span = nb * piece
    wide = -(-piece // LANES) * LANES

    def note_of(ref):
        return ref[piece:, :wide].astype(F32)

    bounds = [jnp.zeros((1, piece), F32)] * (CLUSTERS - 1)
    for e in range(nb):
        note = note_of(home[e])[:, :piece]
        bounds = [
            b + note[2 + 2 * c:3 + 2 * c] * 64.0 + note[3 + 2 * c:4 + 2 * c]
            for c, b in enumerate(bounds)
        ]
    first = iota((8, piece), 0) == 0
    ones = jnp.where(iota((8, LANES), 0) == 0, 1.0, 0.0).astype(BF16)
    if not lo:
        best[...] = jnp.full(best.shape, -1.0, F32)
    for i in range(count):
        column = grp ^ (lo + i)
        for e in range(nb):
            ref = pieces[i][e]
            keys[column, blk ^ e] = ref[:piece]
            note = note_of(ref)[:, :piece]
            slots = note[0:1] * 64.0 + note[1:2]
            kinds = jnp.zeros((1, piece), F32)
            for bound in bounds:
                kinds = kinds + jnp.where(slots >= bound, 1.0, 0.0)
            if not e:
                query_kinds[column] = kinds
            key_kinds[column * nb + (blk ^ e)] = lax.dot_general(
                jnp.where(first, kinds, 0.0).astype(BF16),
                ones,
                (((0,), (0,)), ((), ())),
                preferred_element_type=F32,
            )

    def fold(query, key, causal):
        q = keys[query, blk]
        for half in range(2):
            rows = span // 2
            k = keys[key, half * nb // 2:(half + 1) * nb // 2].reshape(rows, width)
            scores = dot_nt(k, q)
            kinds = key_kinds[pl.ds(key * nb + half * nb // 2, nb // 2)].reshape(rows, LANES)
            parts = []
            for at in range(0, piece, LANES):
                w = min(LANES, piece - at)
                match = kinds[:, :w] == query_kinds[query][:, at:at + w]
                if causal:
                    early = iota((rows, w), 0) - iota((rows, w), 1) < blk * piece + (at - half * rows)
                    match = match & early
                part = jnp.where(match, scores[:, at:at + w], -1.0)
                parts.append(jnp.max(part.reshape(rows // 8, 8, w), axis=0))
            folded = jnp.concatenate(parts, axis=1) if len(parts) > 1 else parts[0]
            best[query] = jnp.maximum(best[query], folded)

    @pl.loop(lo, hi)
    def _(a):
        one = grp ^ a
        fold(one, one, True)

        @pl.loop(0, a)
        def _(b):
            two = grp ^ b
            fold(jnp.maximum(one, two), jnp.minimum(one, two), False)

    if hi == n:
        for f in range(n):
            out_ref[f] = jnp.max(best[f], axis=0, keepdims=True)
    else:
        out_ref[...] = jnp.zeros(out_ref.shape, F32)


def unpack_kernel(n, piece, fam_ref, rank_ref, score_ref, out_ref):
    x = jnp.concatenate([score_ref[f] for f in range(n)], axis=0)
    high = x.astype(BF16)
    rest = x - high.astype(F32)
    mid = rest.astype(BF16)
    low = (rest - mid.astype(F32)).astype(BF16)
    rows = fam_ref.shape[1]
    at_rank = one_hot(iota((piece, rows), 0) == rank_ref[...])
    got = jnp.dot(jnp.concatenate([high, mid, low], axis=0), at_rank, preferred_element_type=F32)
    value = got[:n] + got[n:2 * n] + got[2 * n:]
    value = jnp.where(iota((n, rows), 0) == fam_ref[...], value, 0.0)
    value = jnp.sum(value, axis=0, keepdims=True)
    for i in range(out_ref.shape[0]):
        out_ref[i:i + 1] = value[:, i * LANES:(i + 1) * LANES]


def shape(*dims, kind=F32):
    return jax.ShapeDtypeStruct(dims, kind)


def send(x, axis, by):
    return lax.ppermute(x, axis, [(i, i ^ by) for i in range(lax.axis_size(axis))])


def after(x, *deps):
    return pl.pallas_call(
        lambda *refs: None,
        out_shape=jax.ShapeDtypeStruct(x.shape, x.dtype),
        in_specs=[ANY] * (1 + len(deps)),
        out_specs=ANY,
        input_output_aliases={0: 0},
        cost_estimate=cost(0),
        name="after",
    )(x, *deps)


def limit(mib):
    return pltpu.CompilerParams(vmem_limit_bytes=mib * MIB)


def cost(flops):
    return pl.CostEstimate(flops=flops, bytes_accessed=0, transcendentals=0)


def on_device(embeddings, route, cluster):
    rows, width = embeddings.shape
    n, nb = lax.axis_size("grp"), lax.axis_size("blk")
    piece = rows // n
    half = n // 2
    grp, blk = lax.axis_index("grp"), lax.axis_index("blk")
    here = jnp.stack([grp, blk]).astype(I32)
    blocks = rows // LANES
    wide = -(-piece // LANES) * LANES
    one_piece = shape(piece + NOTE, width, kind=BF16)

    early = [half, half + 1, 0, 1]
    late = [d for d in range(n) if d not in early]
    fam, rank, note, unit, *packed = pl.pallas_call(
        functools.partial(first_kernel, n, piece, rows * nb, early),
        out_shape=[shape(1, rows, kind=I32)] * 2
        + [shape(n, NOTE, wide), shape(rows, width, kind=BF16)]
        + [one_piece] * len(early),
        in_specs=[SMEM, VMEM, VMEM, VMEM],
        out_specs=[VMEM] * (4 + len(early)),
        compiler_params=limit(16),
        name="first",
    )(here, route.reshape(blocks, LANES), cluster, embeddings)
    others = pl.pallas_call(
        functools.partial(second_kernel, n, piece, late),
        out_shape=[one_piece] * len(late),
        in_specs=[SMEM] + [VMEM] * 4,
        out_specs=[VMEM] * len(late),
        compiler_params=limit(16),
        cost_estimate=cost(8 * rows * rows * width),
        name="second",
    )(here, fam, rank, note, unit)
    sent = dict(zip(early + late, packed + list(others)))

    cuts = [0, half, half + 2, half + 3, n] if n == 8 else list(range(0, n + 1, 8))
    own, across, held = [None] * n, [None] * n, [None] * n

    own[0] = sent[0]
    across[0] = send(own[0], "blk", 2)
    for d in [half, half + 1] + list(range(1, half)) + list(range(half + 2, n)):
        dep = None if d in (1, half, half + 1) else across[0] if d < half else own[d - 2]
        own[d] = send(sent[d] if dep is None else after(sent[d], dep), "grp", d)
    state, tokens = [], []
    for lo, hi in zip(cuts, cuts[1:]):
        for d in range(lo, hi):
            x = own[d]
            across[d] = send(x, "blk", 2) if d else across[0]
            held[d] = [x, send(x, "blk", 1), across[d], send(across[d], "blk", 1)]
        kept = [
            shape(n, nb, piece, width, kind=BF16),
            shape(n, 8, piece),
            shape(n * nb, piece, LANES),
            shape(n, 1, piece),
        ]
        folds = sum(d + 1 for d in range(lo, hi))
        args = [here] + held[0] + [p for d in range(lo, hi) for p in held[d]] + list(state)
        token, *state = pl.pallas_call(
            functools.partial(stage_kernel, n, nb, piece, lo, hi),
            out_shape=[shape(n, 1, piece) if hi == n else shape(8, LANES)] + kept,
            in_specs=[SMEM] + [VMEM] * (len(args) - 1),
            out_specs=[VMEM] * 5,
            input_output_aliases={len(args) - 4 + i: 1 + i for i in range(4)} if lo else {},
            compiler_params=limit(12),
            cost_estimate=cost(folds * 2 * piece * piece * nb * width),
            name="stage",
        )(*args)
        tokens.append(token)

    home = lax.all_to_all(token, "grp", split_axis=0, concat_axis=0, tiled=True)
    out = pl.pallas_call(
        functools.partial(unpack_kernel, n, piece),
        out_shape=shape(blocks, LANES),
        in_specs=[VMEM] * 3,
        out_specs=VMEM,
        compiler_params=limit(16),
        name="unpack",
    )(fam, rank, home)
    return out.reshape(rows)


def solution(mesh):
    in_specs = (P(("grp", "blk"), None), P(("grp", "blk")), P("grp", "blk"))
    return jax.shard_map(
        on_device, mesh=mesh, in_specs=in_specs, out_specs=P(("grp", "blk")), check_vma=False
    )
```

time: 208 us -> 129 us (0.62)
  blocking collectives: 54.9 us -> 20.5 us
  waiting for transfers between devices: 67.9 us -> 43.4 us
  local copies, waits for them, and re-layouts: 21 us -> 7.62 us
  starting transfers between devices: 29.1 us -> 24 us
  other arithmetic: 4.61 us -> 0.07 us
  Pallas kernels: 29.7 us -> 32.7 us
    all_gather x1 -> x0, blocking collectives: 46.1 us -> none  [on_device(): everyone = lax.all_gather(meta, ('grp', 'blk'))]
    ppermute x31, waiting for transfers between devices: 67.9 us -> 43.4 us  [send(): lax.ppermute(x, axis, [(i, i ^ by) for i in range(lax.axis_size(axis))])]
    all_to_all x1, blocking collectives: 8.88 us -> 20.5 us  [on_device(): home = lax.all_to_all(token, 'grp', split_axis=0, concat_axis=0, tiled=True)]
    add x2 -> x0, local copies, waits for them, and re-layouts: 5.9 us -> none  [on_device(): kinds = kinds + (slots >= bounds[c]).astype(I32)]
    ppermute x31, starting transfers between devices: 29.1 us -> 24 us  [send(): lax.ppermute(x, axis, [(i, i ^ by) for i in range(lax.axis_size(axis))])]
    slice x3 -> x0, local copies, waits for them, and re-layouts: 3.8 us -> none  [the longest x1 1.67 us: on_device(): slots = lax.dynamic_index_in_dim(everyone[:, :n], grp, 1, keepdims=False)]
    add x1 -> x0, other arithmetic: 2.52 us -> none  [on_device(): kinds = kinds + (slots >= bounds[c]).astype(I32)]
    pallas_call x3 -> x10, Pallas kernels: 29.5 us -> 31.9 us  [the longest x4 24.6 us: on_device(): pl.pallas_call(functools.partial(stage_kernel, n, nb, piece, lo, hi), out...]
  transfers between devices with their start and end apart: 31 -> 31, of which waited for: 10 -> 9; matrix products, arithmetic and copies ran while one was open for 7% -> 0% of each run, Pallas kernels for 0% -> 18%
where the time goes in v3:
time: 129 us; the launch traced here: 128 us
  waiting for transfers between devices  43.4 us (34%)
  Pallas kernels  32.7 us (25%)
  starting transfers between devices  24 us (19%)
  blocking collectives  20.5 us (16%)
  local copies, waits for them, and re-layouts  7.62 us (6%)
    ppermute x31, waiting for transfers between devices, send(): lax.ppermute(x, axis, [(i, i ^ by) for i in range(lax.axis_size(axis))])  43.4 us
    pallas_call x4, Pallas kernels, on_device(): pl.pallas_call(functools.partial(stage_kernel, n, nb, piece, lo, hi), out...  24.6 us
    ppermute x31, starting transfers between devices, send(): lax.ppermute(x, axis, [(i, i ^ by) for i in range(lax.axis_size(axis))])  24 us
    all_to_all x1, blocking collectives, on_device(): home = lax.all_to_all(token, 'grp', split_axis=0, concat_axis=0, tiled=True)  20.5 us
    unnamed x24, local copies, waits for them, and re-layouts  7.62 us
    pallas_call x1, Pallas kernels, on_device(): pl.pallas_call(functools.partial(first_kernel, n, piece, rows * nb, early...  4.76 us
  transfers between devices with their start and end apart: 31, of which 9 were waited for; matrix products, arithmetic and copies ran while one was open for 0% of the time, Pallas kernels for 18%

profile of v3, /device:TPU:0, one launch (start us, length us, event | category | flops | bytes accessed | tf_op | source)
XLA Modules:
  0.0 128.4 jit_solution(10907793004095165029)
XLA Ops:
  0.1 1.7 %copy-done.3 = bf16[1536,768]{1,0:T(8,128)(2,1)S(1)} copy-done((bf16[1536,768]{1,0:T(8,128)(2,1)S(1)}, bf16[1536,768]{1,0:T(8,128)(2,1)}, u32[]{:S(2)}) %copy-start.3) | copy-done | bytes 2359320
  3.1 4.8 %first.1 = (s32[1,1536]{1,0:T(1,128)S(1)}, s32[1,1536]{1,0:T(1,128)S(1)}, f32[8,8,256]{2,1,0:T(8,128)S(1)}, bf16[1536,768]{1,0:T(8,128)(2,1)S(1)}, bf16[200,768]...) custom-call(s32[2]{0:T(128)S(1)} %pad_add_fusion.here_ref, ...), custom_call_target="tpu_custom_call" | custom-call | tf_op jit(solution)/shard_map/first/pallas_call | solution.py:253
  7.9 3.0 %collective-permute-start.1 = (bf16[200,768]{1,0:T(8,128)(2,1)S(1)}, bf16[200,768]{1,0:T(8,128)(2,1)S(1)}, u32[]{:S(2)}, u32[]{:S(2)}) collective-permute-start(bf16[200,768]{1,0:T(8,128)(2,1)S(1)} %get-tuple-element.32.rest_0_.rest_4_), channel_id=1, source_target_pairs={{0,2},{1,3},{2,0},{3,1},{4,6},{5,7},{6,4},{7,5},{8,10},{9,11},{10,... | collective-permute-start | bytes 921608 | tf_op jit(solution)/shard_map/ppermute | solution.py:217
  10.9 1.5 %collective-permute-start.19 = (bf16[200,768]{1,0:T(8,128)(2,1)S(1)}, bf16[200,768]{1,0:T(8,128)(2,1)S(1)}, u32[]{:S(2)}, u32[]{:S(2)}) collective-permute-start(bf16[200,768]{1,0:T(8,128)(2,1)S(1)} %get-tuple-element.39), channel_id=1, source_target_pairs={{0,4},{4,0},{8,12},{12,8},{16,20},{20,16},{24,28},{28,24},{1,5},{5... | collective-permute-start | bytes 921608 | tf_op jit(solution)/shard_map/ppermute | solution.py:217
  12.4 2.6 %collective-permute-start.8 = (bf16[200,768]{1,0:T(8,128)(2,1)S(1)}, bf16[200,768]{1,0:T(8,128)(2,1)}, u32[]{:S(2)}, u32[]{:S(2)}) collective-permute-start(bf16[200,768]{1,0:T(8,128)(2,1)S(1)} %get-tuple-element.38), channel_id=1, source_target_pairs={{0,16},{4,20},{8,24},{12,28},{16,0},{20,4},{24,8},{28,12},{1,17},{... | collective-permute-start | bytes 921608 | tf_op jit(solution)/shard_map/ppermute | solution.py:217
  15.3 2.6 %second.1 = (bf16[200,768]{1,0:T(8,128)(2,1)S(1)}, bf16[200,768]{1,0:T(8,128)(2,1)S(1)}, bf16[200,768]{1,0:T(8,128)(2,1)S(1)}, bf16[200,768]{1,0:T(8,128)(2,1)S(1)}) custom-call(s32[2]{0:T(128)S(1)} %pad_add_fusion.here_ref, s32[1,1536]{1,0:T(1,128)S(1)} %get-tuple-element.30.fam_ref, s32[1,1536]{1,0:T(1,128)S(1)} %get-tuple-element.31.rank_ref, ...), custom_call_target="tpu_custom_call" | custom-call | flops 14495514624 | tf_op jit(solution)/shard_map/second/pallas_call | solution.py:263
  18.6 0.7 copy-done.7
  19.3 0.7 copy-done.8
  20.1 0.7 copy-done.9
  20.8 0.7 copy-done
  21.5 1.6 %collective-permute-start.23 = (bf16[200,768]{1,0:T(8,128)(2,1)}, bf16[200,768]{1,0:T(8,128)(2,1)S(1)}, u32[]{:S(2)}, u32[]{:S(2)}) collective-permute-start(bf16[200,768]{1,0:T(8,128)(2,1)} %after.6), channel_id=1, source_target_pairs={{0,8},{4,12},{8,0},{12,4},{16,24},{20,28},{24,16},{28,20},{1,9},{5... | collective-permute-start | bytes 921608 | tf_op jit(solution)/shard_map/ppermute | solution.py:217
  23.1 1.4 %collective-permute-start.27 = (bf16[200,768]{1,0:T(8,128)(2,1)}, bf16[200,768]{1,0:T(8,128)(2,1)}, u32[]{:S(2)}, u32[]{:S(2)}) collective-permute-start(bf16[200,768]{1,0:T(8,128)(2,1)} %after.7), channel_id=1, source_target_pairs={{0,12},{4,8},{8,4},{12,0},{16,28},{20,24},{24,20},{28,16},{1,13},{... | collective-permute-start | bytes 921608 | tf_op jit(solution)/shard_map/ppermute | solution.py:217
  24.5 12.3 %collective-permute-done.8.refs_1_.rest_4_ = bf16[200,768]{1,0:T(8,128)(2,1)} collective-permute-done((bf16[200,768]{1,0:T(8,128)(2,1)S(1)}, bf16[200,768]{1,0:T(8,128)(2,1)}, u32[]{:S(2)}, u32[]{:S(2)}) %collective-permute-start.8) | collective-permute-done | bytes 307232 | tf_op jit(solution)/shard_map/ppermute | solution.py:217
  37.3 5.2 %collective-permute-done.3.refs_1_.rest_8_ = bf16[200,768]{1,0:T(8,128)(2,1)S(1)} collective-permute-done((bf16[200,768]{1,0:T(8,128)(2,1)S(1)}, bf16[200,768]{1,0:T(8,128)(2,1)S(1)}, u32[]{:S(2)}, u32[]{:S(2)}) %collective-permute-start.3) | collective-permute-done | bytes 307232 | tf_op jit(solution)/shard_map/ppermute | solution.py:217
  42.6 1.4 %collective-permute-done.23.rest_12_ = bf16[200,768]{1,0:T(8,128)(2,1)S(1)} collective-permute-done((bf16[200,768]{1,0:T(8,128)(2,1)}, bf16[200,768]{1,0:T(8,128)(2,1)S(1)}, u32[]{:S(2)}, u32[]{:S(2)}) %collective-permute-start.23) | collective-permute-done | bytes 307232 | tf_op jit(solution)/shard_map/ppermute | solution.py:217
  44.1 6.1 %collective-permute-done.27.rest_16_ = bf16[200,768]{1,0:T(8,128)(2,1)} collective-permute-done((bf16[200,768]{1,0:T(8,128)(2,1)}, bf16[200,768]{1,0:T(8,128)(2,1)}, u32[]{:S(2)}, u32[]{:S(2)}) %collective-permute-start.27) | collective-permute-done | bytes 307232 | tf_op jit(solution)/shard_map/ppermute | solution.py:217
  51.2 4.7 %collective-permute-start.9 = (bf16[200,768]{1,0:T(8,128)(2,1)}, bf16[200,768]{1,0:T(8,128)(2,1)S(1)}, u32[]{:S(2)}, u32[]{:S(2)}) collective-permute-start(bf16[200,768]{1,0:T(8,128)(2,1)} %after.5), channel_id=1, source_target_pairs={{0,24},{4,28},{8,16},{12,20},{16,8},{20,12},{24,0},{28,4},{1,25},{... | collective-permute-start | bytes 921608 | tf_op jit(solution)/shard_map/ppermute | solution.py:217
  56.0 1.5 %collective-permute-start.4 = (bf16[200,768]{1,0:T(8,128)(2,1)}, bf16[200,768]{1,0:T(8,128)(2,1)S(1)}, u32[]{:S(2)}, u32[]{:S(2)}) collective-permute-start(bf16[200,768]{1,0:T(8,128)(2,1)} %after.4), channel_id=1, source_target_pairs={{0,28},{4,24},{8,20},{12,16},{16,12},{20,8},{24,4},{28,0},{1,29},{... | collective-permute-start | bytes 921608 | tf_op jit(solution)/shard_map/ppermute | solution.py:217
  57.5 1.5 %collective-permute-done.17.rest_10_ = bf16[200,768]{1,0:T(8,128)(2,1)S(1)} collective-permute-done((bf16[200,768]{1,0:T(8,128)(2,1)S(1)}, bf16[200,768]{1,0:T(8,128)(2,1)S(1)}, u32[]{:S(2)}, u32[]{:S(2)}) %collective-permute-start.17) | collective-permute-done | bytes 307232 | tf_op jit(solution)/shard_map/ppermute | solution.py:217
  59.5 1.6 %collective-permute-start.29 = (bf16[200,768]{1,0:T(8,128)(2,1)}, bf16[200,768]{1,0:T(8,128)(2,1)S(1)}, u32[]{:S(2)}, u32[]{:S(2)}) collective-permute-start(bf16[200,768]{1,0:T(8,128)(2,1)} %collective-permute-done.27.rest_16_), channel_id=1, source_target_pairs={{0,2},{1,3},{2,0},{3,1},{4,6},{5,7},{6,4},{7,5},{8,10},{9,11},{10,... | collective-permute-start | bytes 921608 | tf_op jit(solution)/shard_map/ppermute | solution.py:217
  61.1 3.3 %collective-permute-done.9.rest_4_ = bf16[200,768]{1,0:T(8,128)(2,1)S(1)} collective-permute-done((bf16[200,768]{1,0:T(8,128)(2,1)}, bf16[200,768]{1,0:T(8,128)(2,1)S(1)}, u32[]{:S(2)}, u32[]{:S(2)}) %collective-permute-start.9) | collective-permute-done | bytes 307232 | tf_op jit(solution)/shard_map/ppermute | solution.py:217
  64.3 6.0 %collective-permute-done.4.rest_4_ = bf16[200,768]{1,0:T(8,128)(2,1)S(1)} collective-permute-done((bf16[200,768]{1,0:T(8,128)(2,1)}, bf16[200,768]{1,0:T(8,128)(2,1)S(1)}, u32[]{:S(2)}, u32[]{:S(2)}) %collective-permute-start.4) | collective-permute-done | bytes 307232 | tf_op jit(solution)/shard_map/ppermute | solution.py:217
  70.3 1.5 %collective-permute-start.11 = (bf16[200,768]{1,0:T(8,128)(2,1)S(1)}, bf16[200,768]{1,0:T(8,128)(2,1)S(1)}, u32[]{:S(2)}, u32[]{:S(2)}) collective-permute-start(bf16[200,768]{1,0:T(8,128)(2,1)S(1)} %collective-permute-done.9.rest_4_), channel_id=1, source_target_pairs={{0,2},{1,3},{2,0},{3,1},{4,6},{5,7},{6,4},{7,5},{8,10},{9,11},{10,... | collective-permute-start | bytes 921608 | tf_op jit(solution)/shard_map/ppermute | solution.py:217
  71.9 1.6 %collective-permute-done.29.rest_18_ = bf16[200,768]{1,0:T(8,128)(2,1)S(1)} collective-permute-done((bf16[200,768]{1,0:T(8,128)(2,1)}, bf16[200,768]{1,0:T(8,128)(2,1)S(1)}, u32[]{:S(2)}, u32[]{:S(2)}) %collective-permute-start.29) | collective-permute-done | bytes 307232 | tf_op jit(solution)/shard_map/ppermute | solution.py:217
  74.6 5.9 %collective-permute-done.11.rest_6_ = bf16[200,768]{1,0:T(8,128)(2,1)S(1)} collective-permute-done((bf16[200,768]{1,0:T(8,128)(2,1)S(1)}, bf16[200,768]{1,0:T(8,128)(2,1)S(1)}, u32[]{:S(2)}, u32[]{:S(2)}) %collective-permute-start.11) | collective-permute-done | bytes 307232 | tf_op jit(solution)/shard_map/ppermute | solution.py:217
  81.0 1.0 copy-done.1
  82.0 7.6 %stage.4 = (f32[8,128]{1,0:T(8,128)}, bf16[8,4,192,768]{3,2,1,0:T(8,128)(2,1)S(1)}, f32[8,8,192]{2,1,0:T(8,128)S(1)}, f32[32,192,128]{2,1,0:T(8,128)S(1)}, f32[8,1,192]{2,1,0:T(1,128)S(1)}) custom-call(s32[2]{0:T(128)S(1)} %pad_add_fusion.here_ref, bf16[200,768]{1,0:T(8,128)(2,1)S(1)} %get-tuple-element.32.rest_0_.rest_4_, ...), custom_call_target="tpu_custom_call" | custom-call | flops 2264924160 | tf_op jit(solution)/shard_map/stage/pallas_call | solution.py:296
  90.1 7.6 %stage.5 = (f32[8,128]{1,0:T(8,128)}, bf16[8,4,192,768]{3,2,1,0:T(8,128)(2,1)S(1)}, f32[8,8,192]{2,1,0:T(8,128)S(1)}, f32[32,192,128]{2,1,0:T(8,128)S(1)}, f32[8,1,192]{2,1,0:T(1,128)S(1)}) custom-call(s32[2]{0:T(128)S(1)} %pad_add_fusion.here_ref, ...), custom_call_target="tpu_custom_call", output_to_operand_aliasing={{1}: (13, {}), {2}: (14, {}), {3}: (15, {}), {4}: (16, {})} | custom-call | flops 2491416576 | tf_op jit(solution)/shard_map/stage/pallas_call | solution.py:296
  97.7 4.8 %stage.6 = (f32[8,128]{1,0:T(8,128)}, bf16[8,4,192,768]{3,2,1,0:T(8,128)(2,1)S(1)}, f32[8,8,192]{2,1,0:T(8,128)S(1)}, f32[32,192,128]{2,1,0:T(8,128)S(1)}, f32[8,1,192]{2,1,0:T(1,128)S(1)}) custom-call(s32[2]{0:T(128)S(1)} %pad_add_fusion.here_ref, ...), custom_call_target="tpu_custom_call", output_to_operand_aliasing={{1}: (9, {}), {2}: (10, {}), {3}: (11, {}), {4}: (12, {})} | custom-call | flops 1585446912 | tf_op jit(solution)/shard_map/stage/pallas_call | solution.py:296
  102.4 4.6 %stage.7 = (f32[8,1,192]{2,1,0:T(1,128)S(1)}, bf16[8,4,192,768]{3,2,1,0:T(8,128)(2,1)S(1)}, f32[8,8,192]{2,1,0:T(8,128)S(1)}, f32[32,192,128]{2,1,0:T(8,128)S(1)}, f32[8,1,192]{2,1,0:T(1,128)S(1)}) custom-call(s32[2]{0:T(128)S(1)} %pad_add_fusion.here_ref, ...), custom_call_target="tpu_custom_call", output_to_operand_aliasing={{1}: (9, {}), {2}: (10, {}), {3}: (11, {}), {4}: (12, {})} | custom-call | flops 1811939328 | tf_op jit(solution)/shard_map/stage/pallas_call | solution.py:296
  107.1 20.5 %all_to_all.5.score_ref = f32[8,1,192]{2,1,0:T(1,128)S(1)} all-to-all(f32[8,1,192]{2,1,0:T(1,128)S(1)} %get-tuple-element.54), channel_id=1, replica_groups=mesh['grp'=8,'blk'=4] {'grp'}, dimensions={0} | all-to-all | bytes 12288 | tf_op jit(solution)/shard_map/all_to_all | solution.py:308
  127.6 0.8 unpack.1
  (67 shorter events, 6.8 us)
Async XLA Ops:
  7.9 12.9 %collective-permute-start.1 = (bf16[200,768]{1,0:T(8,128)(2,1)S(1)}, bf16[200,768]{1,0:T(8,128)(2,1)S(1)}, u32[]{:S(2)}, u32[]{:S(2)}) collective-permute-start(bf16[200,768]{1,0:T(8,128)(2,1)S(1)} %get-tuple-element.32.rest_0_.rest_4_), channel_id=1, source_target_pairs={{0,2},{1,3},{2,0},{3,1},{4,6},{5,7},{6,4},{7,5},{8,10},{9,11},{10,... | collective-permute-start | bytes 921608 | tf_op jit(solution)/shard_map/ppermute | solution.py:217
  10.9 12.2 %collective-permute-start = (bf16[200,768]{1,0:T(8,128)(2,1)S(1)}, bf16[200,768]{1,0:T(8,128)(2,1)S(1)}, u32[]{:S(2)}, u32[]{:S(2)}) collective-permute-start(bf16[200,768]{1,0:T(8,128)(2,1)S(1)} %get-tuple-element.32.rest_0_.rest_4_), channel_id=1, source_target_pairs={{0,1},{1,0},{2,3},{3,2},{4,5},{5,4},{6,7},{7,6},{8,9},{9,8},{10,11... | collective-permute-start | bytes 921608 | tf_op jit(solution)/shard_map/ppermute | solution.py:217
  10.9 13.5 %collective-permute-start.19 = (bf16[200,768]{1,0:T(8,128)(2,1)S(1)}, bf16[200,768]{1,0:T(8,128)(2,1)S(1)}, u32[]{:S(2)}, u32[]{:S(2)}) collective-permute-start(bf16[200,768]{1,0:T(8,128)(2,1)S(1)} %get-tuple-element.39), channel_id=1, source_target_pairs={{0,4},{4,0},{8,12},{12,8},{16,20},{20,16},{24,28},{28,24},{1,5},{5... | collective-permute-start | bytes 921608 | tf_op jit(solution)/shard_map/ppermute | solution.py:217
  12.4 24.4 %collective-permute-start.8 = (bf16[200,768]{1,0:T(8,128)(2,1)S(1)}, bf16[200,768]{1,0:T(8,128)(2,1)}, u32[]{:S(2)}, u32[]{:S(2)}) collective-permute-start(bf16[200,768]{1,0:T(8,128)(2,1)S(1)} %get-tuple-element.38), channel_id=1, source_target_pairs={{0,16},{4,20},{8,24},{12,28},{16,0},{20,4},{24,8},{28,12},{1,17},{... | collective-permute-start | bytes 921608 | tf_op jit(solution)/shard_map/ppermute | solution.py:217
  15.0 27.5 %collective-permute-start.3 = (bf16[200,768]{1,0:T(8,128)(2,1)S(1)}, bf16[200,768]{1,0:T(8,128)(2,1)S(1)}, u32[]{:S(2)}, u32[]{:S(2)}) collective-permute-start(bf16[200,768]{1,0:T(8,128)(2,1)S(1)} %get-tuple-element.36), channel_id=1, source_target_pairs={{0,20},{4,16},{8,28},{12,24},{16,4},{20,0},{24,12},{28,8},{1,21},{... | collective-permute-start | bytes 921608 | tf_op jit(solution)/shard_map/ppermute | solution.py:217
  21.5 22.5 %collective-permute-start.23 = (bf16[200,768]{1,0:T(8,128)(2,1)}, bf16[200,768]{1,0:T(8,128)(2,1)S(1)}, u32[]{:S(2)}, u32[]{:S(2)}) collective-permute-start(bf16[200,768]{1,0:T(8,128)(2,1)} %after.6), channel_id=1, source_target_pairs={{0,8},{4,12},{8,0},{12,4},{16,24},{20,28},{24,16},{28,20},{1,9},{5... | collective-permute-start | bytes 921608 | tf_op jit(solution)/shard_map/ppermute | solution.py:217
  23.1 27.1 %collective-permute-start.27 = (bf16[200,768]{1,0:T(8,128)(2,1)}, bf16[200,768]{1,0:T(8,128)(2,1)}, u32[]{:S(2)}, u32[]{:S(2)}) collective-permute-start(bf16[200,768]{1,0:T(8,128)(2,1)} %after.7), channel_id=1, source_target_pairs={{0,12},{4,8},{8,4},{12,0},{16,28},{20,24},{24,20},{28,16},{1,13},{... | collective-permute-start | bytes 921608 | tf_op jit(solution)/shard_map/ppermute | solution.py:217
  24.5 26.2 %collective-permute-start.2 = (bf16[200,768]{1,0:T(8,128)(2,1)}, bf16[200,768]{1,0:T(8,128)(2,1)S(1)}, u32[]{:S(2)}, u32[]{:S(2)}) collective-permute-start(bf16[200,768]{1,0:T(8,128)(2,1)} %copy-done), channel_id=1, source_target_pairs={{0,1},{1,0},{2,3},{3,2},{4,5},{5,4},{6,7},{7,6},{8,9},{9,8},{10,11... | collective-permute-start | bytes 921608 | tf_op jit(solution)/shard_map/ppermute | solution.py:217
  36.8 13.9 %collective-permute-start.21 = (bf16[200,768]{1,0:T(8,128)(2,1)S(1)}, bf16[200,768]{1,0:T(8,128)(2,1)}, u32[]{:S(2)}, u32[]{:S(2)}) collective-permute-start(bf16[200,768]{1,0:T(8,128)(2,1)S(1)} %collective-permute-done.19.rest_8_), channel_id=1, source_target_pairs={{0,2},{1,3},{2,0},{3,1},{4,6},{5,7},{6,4},{7,5},{8,10},{9,11},{10,... | collective-permute-start | bytes 921608 | tf_op jit(solution)/shard_map/ppermute | solution.py:217
  42.6 8.7 %collective-permute-start.20 = (bf16[200,768]{1,0:T(8,128)(2,1)S(1)}, bf16[200,768]{1,0:T(8,128)(2,1)}, u32[]{:S(2)}, u32[]{:S(2)}) collective-permute-start(bf16[200,768]{1,0:T(8,128)(2,1)S(1)} %collective-permute-done.19.rest_8_), channel_id=1, source_target_pairs={{0,1},{1,0},{2,3},{3,2},{4,5},{5,4},{6,7},{7,6},{8,9},{9,8},{10,11... | collective-permute-start | bytes 921608 | tf_op jit(solution)/shard_map/ppermute | solution.py:217
  44.0 12.0 %collective-permute-start.14 = (bf16[200,768]{1,0:T(8,128)(2,1)}, bf16[200,768]{1,0:T(8,128)(2,1)S(1)}, u32[]{:S(2)}, u32[]{:S(2)}) collective-permute-start(bf16[200,768]{1,0:T(8,128)(2,1)} %collective-permute-done.8.refs_1_.rest_4_), channel_id=1, source_target_pairs={{0,2},{1,3},{2,0},{3,1},{4,6},{5,7},{6,4},{7,5},{8,10},{9,11},{10,... | collective-permute-start | bytes 921608 | tf_op jit(solution)/shard_map/ppermute | solution.py:217
  50.2 8.8 %collective-permute-start.17 = (bf16[200,768]{1,0:T(8,128)(2,1)S(1)}, bf16[200,768]{1,0:T(8,128)(2,1)S(1)}, u32[]{:S(2)}, u32[]{:S(2)}) collective-permute-start(bf16[200,768]{1,0:T(8,128)(2,1)S(1)} %collective-permute-done.3.refs_1_.rest_8_), channel_id=1, source_target_pairs={{0,2},{1,3},{2,0},{3,1},{4,6},{5,7},{6,4},{7,5},{8,10},{9,11},{10,... | collective-permute-start | bytes 921608 | tf_op jit(solution)/shard_map/ppermute | solution.py:217
  50.7 8.8 %collective-permute-start.13 = (bf16[200,768]{1,0:T(8,128)(2,1)}, bf16[200,768]{1,0:T(8,128)(2,1)S(1)}, u32[]{:S(2)}, u32[]{:S(2)}) collective-permute-start(bf16[200,768]{1,0:T(8,128)(2,1)} %collective-permute-done.8.refs_1_.rest_4_), channel_id=1, source_target_pairs={{0,1},{1,0},{2,3},{3,2},{4,5},{5,4},{6,7},{7,6},{8,9},{9,8},{10,11... | collective-permute-start | bytes 921608 | tf_op jit(solution)/shard_map/ppermute | solution.py:217
  50.7 10.4 %collective-permute-start.16 = (bf16[200,768]{1,0:T(8,128)(2,1)S(1)}, bf16[200,768]{1,0:T(8,128)(2,1)S(1)}, u32[]{:S(2)}, u32[]{:S(2)}) collective-permute-start(bf16[200,768]{1,0:T(8,128)(2,1)S(1)} %collective-permute-done.3.refs_1_.rest_8_), channel_id=1, source_target_pairs={{0,1},{1,0},{2,3},{3,2},{4,5},{5,4},{6,7},{7,6},{8,9},{9,8},{10,11... | collective-permute-start | bytes 921608 | tf_op jit(solution)/shard_map/ppermute | solution.py:217
  51.2 38.9 %copy-start.2 = (bf16[200,768]{1,0:T(8,128)(2,1)S(1)}, bf16[200,768]{1,0:T(8,128)(2,1)}, u32[]{:S(2)}) copy-start(bf16[200,768]{1,0:T(8,128)(2,1)} %copy-done) | copy-start | bytes 921604
  51.2 13.1 %collective-permute-start.9 = (bf16[200,768]{1,0:T(8,128)(2,1)}, bf16[200,768]{1,0:T(8,128)(2,1)S(1)}, u32[]{:S(2)}, u32[]{:S(2)}) collective-permute-start(bf16[200,768]{1,0:T(8,128)(2,1)} %after.5), channel_id=1, source_target_pairs={{0,24},{4,28},{8,16},{12,20},{16,8},{20,12},{24,0},{28,4},{1,25},{... | collective-permute-start | bytes 921608 | tf_op jit(solution)/shard_map/ppermute | solution.py:217
  56.0 14.4 %collective-permute-start.4 = (bf16[200,768]{1,0:T(8,128)(2,1)}, bf16[200,768]{1,0:T(8,128)(2,1)S(1)}, u32[]{:S(2)}, u32[]{:S(2)}) collective-permute-start(bf16[200,768]{1,0:T(8,128)(2,1)} %after.4), channel_id=1, source_target_pairs={{0,28},{4,24},{8,20},{12,16},{16,12},{20,8},{24,4},{28,0},{1,29},{... | collective-permute-start | bytes 921608 | tf_op jit(solution)/shard_map/ppermute | solution.py:217
  59.0 11.3 %collective-permute-start.25 = (bf16[200,768]{1,0:T(8,128)(2,1)S(1)}, bf16[200,768]{1,0:T(8,128)(2,1)S(1)}, u32[]{:S(2)}, u32[]{:S(2)}) collective-permute-start(bf16[200,768]{1,0:T(8,128)(2,1)S(1)} %collective-permute-done.23.rest_12_), channel_id=1, source_target_pairs={{0,2},{1,3},{2,0},{3,1},{4,6},{5,7},{6,4},{7,5},{8,10},{9,11},{10,... | collective-permute-start | bytes 921608 | tf_op jit(solution)/shard_map/ppermute | solution.py:217
  59.5 14.0 %collective-permute-start.29 = (bf16[200,768]{1,0:T(8,128)(2,1)}, bf16[200,768]{1,0:T(8,128)(2,1)S(1)}, u32[]{:S(2)}, u32[]{:S(2)}) collective-permute-start(bf16[200,768]{1,0:T(8,128)(2,1)} %collective-permute-done.27.rest_16_), channel_id=1, source_target_pairs={{0,2},{1,3},{2,0},{3,1},{4,6},{5,7},{6,4},{7,5},{8,10},{9,11},{10,... | collective-permute-start | bytes 921608 | tf_op jit(solution)/shard_map/ppermute | solution.py:217
  61.1 12.4 %collective-permute-start.24 = (bf16[200,768]{1,0:T(8,128)(2,1)S(1)}, bf16[200,768]{1,0:T(8,128)(2,1)S(1)}, u32[]{:S(2)}, u32[]{:S(2)}) collective-permute-start(bf16[200,768]{1,0:T(8,128)(2,1)S(1)} %collective-permute-done.23.rest_12_), channel_id=1, source_target_pairs={{0,1},{1,0},{2,3},{3,2},{4,5},{5,4},{6,7},{7,6},{8,9},{9,8},{10,11... | collective-permute-start | bytes 921608 | tf_op jit(solution)/shard_map/ppermute | solution.py:217
  64.3 9.7 %collective-permute-start.28 = (bf16[200,768]{1,0:T(8,128)(2,1)}, bf16[200,768]{1,0:T(8,128)(2,1)S(1)}, u32[]{:S(2)}, u32[]{:S(2)}) collective-permute-start(bf16[200,768]{1,0:T(8,128)(2,1)} %collective-permute-done.27.rest_16_), channel_id=1, source_target_pairs={{0,1},{1,0},{2,3},{3,2},{4,5},{5,4},{6,7},{7,6},{8,9},{9,8},{10,11... | collective-permute-start | bytes 921608 | tf_op jit(solution)/shard_map/ppermute | solution.py:217
  70.3 3.8 %collective-permute-start.22 = (bf16[200,768]{1,0:T(8,128)(2,1)}, bf16[200,768]{1,0:T(8,128)(2,1)S(1)}, u32[]{:S(2)}, u32[]{:S(2)}) collective-permute-start(bf16[200,768]{1,0:T(8,128)(2,1)} %collective-permute-done.21.rest_10_), channel_id=1, source_target_pairs={{0,1},{1,0},{2,3},{3,2},{4,5},{5,4},{6,7},{7,6},{8,9},{9,8},{10,11... | collective-permute-start | bytes 921608 | tf_op jit(solution)/shard_map/ppermute | solution.py:217
  70.3 10.1 %collective-permute-start.11 = (bf16[200,768]{1,0:T(8,128)(2,1)S(1)}, bf16[200,768]{1,0:T(8,128)(2,1)S(1)}, u32[]{:S(2)}, u32[]{:S(2)}) collective-permute-start(bf16[200,768]{1,0:T(8,128)(2,1)S(1)} %collective-permute-done.9.rest_4_), channel_id=1, source_target_pairs={{0,2},{1,3},{2,0},{3,1},{4,6},{5,7},{6,4},{7,5},{8,10},{9,11},{10,... | collective-permute-start | bytes 921608 | tf_op jit(solution)/shard_map/ppermute | solution.py:217
  73.5 6.9 %collective-permute-start.26 = (bf16[200,768]{1,0:T(8,128)(2,1)S(1)}, bf16[200,768]{1,0:T(8,128)(2,1)S(1)}, u32[]{:S(2)}, u32[]{:S(2)}) collective-permute-start(bf16[200,768]{1,0:T(8,128)(2,1)S(1)} %collective-permute-done.25.rest_14_), channel_id=1, source_target_pairs={{0,1},{1,0},{2,3},{3,2},{4,5},{5,4},{6,7},{7,6},{8,9},{9,8},{10,11... | collective-permute-start | bytes 921608 | tf_op jit(solution)/shard_map/ppermute | solution.py:217
  73.5 7.4 %collective-permute-start.30 = (bf16[200,768]{1,0:T(8,128)(2,1)S(1)}, bf16[200,768]{1,0:T(8,128)(2,1)S(1)}, u32[]{:S(2)}, u32[]{:S(2)}) collective-permute-start(bf16[200,768]{1,0:T(8,128)(2,1)S(1)} %collective-permute-done.29.rest_18_), channel_id=1, source_target_pairs={{0,1},{1,0},{2,3},{3,2},{4,5},{5,4},{6,7},{7,6},{8,9},{9,8},{10,11... | collective-permute-start | bytes 921608 | tf_op jit(solution)/shard_map/ppermute | solution.py:217
  74.0 15.6 %collective-permute-start.15 = (bf16[200,768]{1,0:T(8,128)(2,1)S(1)}, bf16[200,768]{1,0:T(8,128)(2,1)S(1)}, u32[]{:S(2)}, u32[]{:S(2)}) collective-permute-start(bf16[200,768]{1,0:T(8,128)(2,1)S(1)} %collective-permute-done.14.rest_6_), channel_id=1, source_target_pairs={{0,1},{1,0},{2,3},{3,2},{4,5},{5,4},{6,7},{7,6},{8,9},{9,8},{10,11... | collective-permute-start | bytes 921608 | tf_op jit(solution)/shard_map/ppermute | solution.py:217
  74.1 15.9 %collective-permute-start.6 = (bf16[200,768]{1,0:T(8,128)(2,1)S(1)}, bf16[200,768]{1,0:T(8,128)(2,1)S(1)}, u32[]{:S(2)}, u32[]{:S(2)}) collective-permute-start(bf16[200,768]{1,0:T(8,128)(2,1)S(1)} %collective-permute-done.4.rest_4_), channel_id=1, source_target_pairs={{0,2},{1,3},{2,0},{3,1},{4,6},{5,7},{6,4},{7,5},{8,10},{9,11},{10,... | collective-permute-start | bytes 921608 | tf_op jit(solution)/shard_map/ppermute | solution.py:217
  80.4 9.7 %collective-permute-start.18 = (bf16[200,768]{1,0:T(8,128)(2,1)S(1)}, bf16[200,768]{1,0:T(8,128)(2,1)S(1)}, u32[]{:S(2)}, u32[]{:S(2)}) collective-permute-start(bf16[200,768]{1,0:T(8,128)(2,1)S(1)} %collective-permute-done.17.rest_10_), channel_id=1, source_target_pairs={{0,1},{1,0},{2,3},{3,2},{4,5},{5,4},{6,7},{7,6},{8,9},{9,8},{10,11... | collective-permute-start | bytes 921608 | tf_op jit(solution)/shard_map/ppermute | solution.py:217
  80.4 17.3 %collective-permute-start.10 = (bf16[200,768]{1,0:T(8,128)(2,1)S(1)}, bf16[200,768]{1,0:T(8,128)(2,1)S(1)}, u32[]{:S(2)}, u32[]{:S(2)}) collective-permute-start(bf16[200,768]{1,0:T(8,128)(2,1)S(1)} %collective-permute-done.9.rest_4_), channel_id=1, source_target_pairs={{0,1},{1,0},{2,3},{3,2},{4,5},{5,4},{6,7},{7,6},{8,9},{9,8},{10,11... | collective-permute-start | bytes 921608 | tf_op jit(solution)/shard_map/ppermute | solution.py:217
  80.9 16.7 %collective-permute-start.12 = (bf16[200,768]{1,0:T(8,128)(2,1)S(1)}, bf16[200,768]{1,0:T(8,128)(2,1)S(1)}, u32[]{:S(2)}, u32[]{:S(2)}) collective-permute-start(bf16[200,768]{1,0:T(8,128)(2,1)S(1)} %collective-permute-done.11.rest_6_), channel_id=1, source_target_pairs={{0,1},{1,0},{2,3},{3,2},{4,5},{5,4},{6,7},{7,6},{8,9},{9,8},{10,11... | collective-permute-start | bytes 921608 | tf_op jit(solution)/shard_map/ppermute | solution.py:217
  89.6 12.9 %collective-permute-start.5 = (bf16[200,768]{1,0:T(8,128)(2,1)S(1)}, bf16[200,768]{1,0:T(8,128)(2,1)S(1)}, u32[]{:S(2)}, u32[]{:S(2)}) collective-permute-start(bf16[200,768]{1,0:T(8,128)(2,1)S(1)} %collective-permute-done.4.rest_4_), channel_id=1, source_target_pairs={{0,1},{1,0},{2,3},{3,2},{4,5},{5,4},{6,7},{7,6},{8,9},{9,8},{10,11... | collective-permute-start | bytes 921608 | tf_op jit(solution)/shard_map/ppermute | solution.py:217
  90.0 12.4 %collective-permute-start.7 = (bf16[200,768]{1,0:T(8,128)(2,1)S(1)}, bf16[200,768]{1,0:T(8,128)(2,1)S(1)}, u32[]{:S(2)}, u32[]{:S(2)}) collective-permute-start(bf16[200,768]{1,0:T(8,128)(2,1)S(1)} %collective-permute-done.6.rest_6_), channel_id=1, source_target_pairs={{0,1},{1,0},{2,3},{3,2},{4,5},{5,4},{6,7},{7,6},{8,9},{9,8},{10,11... | collective-permute-start | bytes 921608 | tf_op jit(solution)/shard_map/ppermute | solution.py:217
  (11 other events, 24.4 us)

commit v4 on v3

--- a/solution.py
+++ b/solution.py
@@ -13,7 +13,6 @@
 NOTE = 8
 VMEM = pl.BlockSpec(memory_space=pltpu.VMEM)
 SMEM = pl.BlockSpec(memory_space=pltpu.SMEM)
-ANY = pl.BlockSpec(memory_space=pl.ANY)
 MIB = 1 << 20
 
 
@@ -109,16 +108,26 @@
     pack(n, piece, which, here_ref[0], unit_ref, fam_row, rank_row, note_ref, outs)
 
 
-def second_kernel(n, piece, which, here_ref, fam_ref, rank_ref, note_ref, unit_ref, *outs):
+def second_kernel(n, piece, which, here_ref, fam_ref, rank_ref, note_ref, unit_ref, *rest):
+    *outs, token_ref = rest
+    token_ref[...] = jnp.zeros(token_ref.shape, F32)
     pack(n, piece, which, here_ref[0], unit_ref, fam_ref[...], rank_ref[...], note_ref, outs)
 
 
-def stage_kernel(n, nb, piece, lo, hi, here_ref, *rest):
-    count = hi - lo
-    home = rest[:nb]
-    pieces = [rest[(1 + i) * nb:(2 + i) * nb] for i in range(count)]
-    rest = rest[(1 + count) * nb + (4 if lo else 0):]
-    out_ref, keys, best, key_kinds, query_kinds = rest
+def join_kernel(count, *refs):
+    out_ref = refs[-1]
+    for i in range(count):
+        out_ref[i] = refs[i][...]
+
+
+def stage_kernel(n, nb, piece, old, groups, here_ref, token_ref, *rest):
+    new = [d for group in groups for d in group]
+    pieces = [
+        [rest[i * nb + e].at[j] for e in range(nb)]
+        for i, group in enumerate(groups)
+        for j in range(len(group))
+    ]
+    out_ref, keys, best, key_kinds, query_kinds, bounds_ref = rest[-6:]
     grp, blk = here_ref[0], here_ref[1]
     width = keys.shape[-1]
     span = nb * piece
@@ -127,21 +136,24 @@
     def note_of(ref):
         return ref[piece:, :wide].astype(F32)
 
-    bounds = [jnp.zeros((1, piece), F32)] * (CLUSTERS - 1)
-    for e in range(nb):
-        note = note_of(home[e])[:, :piece]
-        bounds = [
-            b + note[2 + 2 * c:3 + 2 * c] * 64.0 + note[3 + 2 * c:4 + 2 * c]
-            for c, b in enumerate(bounds)
-        ]
+    if not old:
+        bounds = [jnp.zeros((1, piece), F32)] * (CLUSTERS - 1)
+        for ref in pieces[0]:
+            note = note_of(ref)[:, :piece]
+            bounds = [
+                b + note[2 + 2 * c:3 + 2 * c] * 64.0 + note[3 + 2 * c:4 + 2 * c]
+                for c, b in enumerate(bounds)
+            ]
+        for c, bound in enumerate(bounds):
+            bounds_ref[c] = bound
+    bounds = [bounds_ref[c] for c in range(CLUSTERS - 1)]
     first = iota((8, piece), 0) == 0
     ones = jnp.where(iota((8, LANES), 0) == 0, 1.0, 0.0).astype(BF16)
-    if not lo:
+    if not old:
         best[...] = jnp.full(best.shape, -1.0, F32)
-    for i in range(count):
-        column = grp ^ (lo + i)
-        for e in range(nb):
-            ref = pieces[i][e]
+    for d, refs in zip(new, pieces):
+        column = grp ^ d
+        for e, ref in enumerate(refs):
             keys[column, blk ^ e] = ref[:piece]
             note = note_of(ref)[:, :piece]
             slots = note[0:1] * 64.0 + note[1:2]
@@ -158,39 +170,41 @@
             )
 
     def fold(query, key, causal):
-        q = keys[query, blk]
-        for half in range(2):
-            rows = span // 2
-            k = keys[key, half * nb // 2:(half + 1) * nb // 2].reshape(rows, width)
-            scores = dot_nt(k, q)
-            kinds = key_kinds[pl.ds(key * nb + half * nb // 2, nb // 2)].reshape(rows, LANES)
-            parts = []
-            for at in range(0, piece, LANES):
-                w = min(LANES, piece - at)
-                match = kinds[:, :w] == query_kinds[query][:, at:at + w]
-                if causal:
-                    early = iota((rows, w), 0) - iota((rows, w), 1) < blk * piece + (at - half * rows)
-                    match = match & early
-                part = jnp.where(match, scores[:, at:at + w], -1.0)
-                parts.append(jnp.max(part.reshape(rows // 8, 8, w), axis=0))
-            folded = jnp.concatenate(parts, axis=1) if len(parts) > 1 else parts[0]
-            best[query] = jnp.maximum(best[query], folded)
-
-    @pl.loop(lo, hi)
-    def _(a):
-        one = grp ^ a
-        fold(one, one, True)
-
-        @pl.loop(0, a)
-        def _(b):
-            two = grp ^ b
-            fold(jnp.maximum(one, two), jnp.minimum(one, two), False)
-
-    if hi == n:
+        scores = dot_nt(keys[key].reshape(span, width), keys[query, blk])
+        kinds = key_kinds[pl.ds(key * nb, nb)].reshape(span, LANES)
+        parts = []
+        for at in range(0, piece, LANES):
+            w = min(LANES, piece - at)
+            match = kinds[:, :w] == query_kinds[query][:, at:at + w]
+            if causal:
+                early = iota((span, w), 0) - iota((span, w), 1) < blk * piece + at
+                match = match & early
+            part = jnp.where(match, scores[:, at:at + w], -1.0)
+            parts.append(jnp.max(part.reshape(span // 8, 8, w), axis=0))
+        folded = jnp.concatenate(parts, axis=1) if len(parts) > 1 else parts[0]
+        best[query] = jnp.maximum(best[query], folded)
+
+    def pair(a, b):
+        one, two = grp ^ a, grp ^ b
+        fold(jnp.maximum(one, two), jnp.minimum(one, two), False)
+
+    if n <= 8:
+        for i, a in enumerate(new):
+            fold(grp ^ a, grp ^ a, True)
+            for b in old + new[:i]:
+                pair(a, b)
+    else:
+        @pl.loop(len(old), len(old) + len(new))
+        def _(a):
+            fold(grp ^ a, grp ^ a, True)
+
+            @pl.loop(0, a)
+            def _(b):
+                pair(a, b)
+
+    if len(old) + len(new) == n:
         for f in range(n):
             out_ref[f] = jnp.max(best[f], axis=0, keepdims=True)
-    else:
-        out_ref[...] = jnp.zeros(out_ref.shape, F32)
 
 
 def unpack_kernel(n, piece, fam_ref, rank_ref, score_ref, out_ref):
@@ -217,18 +231,6 @@
     return lax.ppermute(x, axis, [(i, i ^ by) for i in range(lax.axis_size(axis))])
 
 
-def after(x, *deps):
-    return pl.pallas_call(
-        lambda *refs: None,
-        out_shape=jax.ShapeDtypeStruct(x.shape, x.dtype),
-        in_specs=[ANY] * (1 + len(deps)),
-        out_specs=ANY,
-        input_output_aliases={0: 0},
-        cost_estimate=cost(0),
-        name="after",
-    )(x, *deps)
-
-
 def limit(mib):
     return pltpu.CompilerParams(vmem_limit_bytes=mib * MIB)
 
@@ -248,7 +250,7 @@
     wide = -(-piece // LANES) * LANES
     one_piece = shape(piece + NOTE, width, kind=BF16)
 
-    early = [half, half + 1, 0, 1]
+    early = [half, 0, 1]
     late = [d for d in range(n) if d not in early]
     fam, rank, note, unit, *packed = pl.pallas_call(
         functools.partial(first_kernel, n, piece, rows * nb, early),
@@ -260,52 +262,100 @@
         compiler_params=limit(16),
         name="first",
     )(here, route.reshape(blocks, LANES), cluster, embeddings)
-    others = pl.pallas_call(
+    *others, token = pl.pallas_call(
         functools.partial(second_kernel, n, piece, late),
-        out_shape=[one_piece] * len(late),
+        out_shape=[one_piece] * len(late) + [shape(8, LANES)],
         in_specs=[SMEM] + [VMEM] * 4,
-        out_specs=[VMEM] * len(late),
+        out_specs=[VMEM] * (len(late) + 1),
         compiler_params=limit(16),
         cost_estimate=cost(8 * rows * rows * width),
         name="second",
     )(here, fam, rank, note, unit)
-    sent = dict(zip(early + late, packed + list(others)))
-
-    cuts = [0, half, half + 2, half + 3, n] if n == 8 else list(range(0, n + 1, 8))
-    own, across, held = [None] * n, [None] * n, [None] * n
-
-    own[0] = sent[0]
-    across[0] = send(own[0], "blk", 2)
-    for d in [half, half + 1] + list(range(1, half)) + list(range(half + 2, n)):
-        dep = None if d in (1, half, half + 1) else across[0] if d < half else own[d - 2]
-        own[d] = send(sent[d] if dep is None else after(sent[d], dep), "grp", d)
-    state, tokens = [], []
-    for lo, hi in zip(cuts, cuts[1:]):
-        for d in range(lo, hi):
-            x = own[d]
-            across[d] = send(x, "blk", 2) if d else across[0]
-            held[d] = [x, send(x, "blk", 1), across[d], send(across[d], "blk", 1)]
+    sent = dict(zip(early + late, packed + others))
+    own, seen, state = {0: sent[0]}, [], []
+
+    def to_columns(*ds):
+        for d in ds:
+            own[d] = send(sent[d], "grp", d)
+
+    def join(ds, later=()):
+        nonlocal token
+        ins = [own[d] for d in ds]
+        kept = [token, *later]
+        token, *later, joined = pl.pallas_call(
+            functools.partial(join_kernel, len(ins)),
+            out_shape=[jax.ShapeDtypeStruct(x.shape, x.dtype) for x in kept]
+            + [shape(len(ins), *one_piece.shape, kind=BF16)],
+            in_specs=[VMEM] * (len(ins) + len(kept)),
+            out_specs=[VMEM] * (len(kept) + 1),
+            input_output_aliases={len(ins) + i: i for i in range(len(kept))},
+            compiler_params=limit(4),
+            cost_estimate=cost(0),
+            name="join",
+        )(*ins, *kept)
+        return [joined, *later]
+
+    def stage(*groups):
+        nonlocal token, seen, state
         kept = [
             shape(n, nb, piece, width, kind=BF16),
             shape(n, 8, piece),
             shape(n * nb, piece, LANES),
             shape(n, 1, piece),
+            shape(CLUSTERS - 1, 1, piece),
         ]
-        folds = sum(d + 1 for d in range(lo, hi))
-        args = [here] + held[0] + [p for d in range(lo, hi) for p in held[d]] + list(state)
+        args = [here, token]
+        for _, mine, across in groups:
+            args += [mine, send(mine, "blk", 1), across, send(across, "blk", 1)]
+        args += list(state)
+        ds = [list(group[0]) for group in groups]
+        now = seen + sum(ds, [])
+        outs = [shape(8, LANES)] + ([shape(n, 1, piece)] if len(now) == n else []) + kept
+        alias = {1: 0}
+        if seen:
+            alias |= {len(args) - 5 + i: len(outs) - 5 + i for i in range(5)}
+        folds = sum(range(len(seen) + 1, len(now) + 1))
         token, *state = pl.pallas_call(
-            functools.partial(stage_kernel, n, nb, piece, lo, hi),
-            out_shape=[shape(n, 1, piece) if hi == n else shape(8, LANES)] + kept,
+            functools.partial(stage_kernel, n, nb, piece, seen, ds),
+            out_shape=outs,
             in_specs=[SMEM] + [VMEM] * (len(args) - 1),
-            out_specs=[VMEM] * 5,
-            input_output_aliases={len(args) - 4 + i: 1 + i for i in range(4)} if lo else {},
+            out_specs=[VMEM] * len(outs),
+            input_output_aliases=alias,
             compiler_params=limit(12),
-            cost_estimate=cost(folds * 2 * piece * piece * nb * width),
+            cost_estimate=cost(folds * 4 * piece * piece * nb * width),
             name="stage",
         )(*args)
-        tokens.append(token)
-
-    home = lax.all_to_all(token, "grp", split_axis=0, concat_axis=0, tiled=True)
+        seen = now
+
+    if n == 8:
+        to_columns(4, 1)
+        one = own[0].reshape(1, *one_piece.shape)
+        one_across = send(one, "blk", 2)
+        two, one_across, sent[5], sent[2], sent[3] = join(
+            (1, 4), [one_across, sent[5], sent[2], sent[3]]
+        )
+        two_across = send(two, "blk", 2)
+        to_columns(5, 2, 3)
+        three, two, two_across, sent[6] = join((2, 5), [two, two_across, sent[6]])
+        three_across = send(three, "blk", 2)
+        to_columns(6)
+        four, three, three_across, sent[7] = join((3, 6), [three, three_across, sent[7]])
+        four_across = send(four, "blk", 2)
+        to_columns(7)
+        stage(((0,), one, one_across), ((1, 4), two, two_across), ((2, 5), three, three_across))
+        five, four, four_across = join((7,), [four, four_across])
+        five_across = send(five, "blk", 2)
+        stage(((3, 6), four, four_across))
+        stage(((7,), five, five_across))
+    else:
+        to_columns(*range(1, n))
+        for lo in range(0, n, 8):
+            ds = range(lo, lo + 8)
+            (joined,) = join(ds)
+            stage((ds, joined, send(joined, "blk", 2)))
+    scores = state[0]
+
+    home = lax.all_to_all(scores, "grp", split_axis=0, concat_axis=0, tiled=True)
     out = pl.pallas_call(
         functools.partial(unpack_kernel, n, piece),
         out_shape=shape(blocks, LANES),

time: 129 us -> 114 us (0.88)
  waiting for transfers between devices: 43.4 us -> 55 us
  blocking collectives: 20.5 us -> 11.3 us
  Pallas kernels: 32.7 us -> 23.6 us
  local copies, waits for them, and re-layouts: 7.62 us -> 3.05 us
  starting transfers between devices: 24 us -> 20.8 us
    ppermute x31 -> x22, waiting for transfers between devices: 43.4 us -> 55 us  [send(): lax.ppermute(x, axis, [(i, i ^ by) for i in range(lax.axis_size(axis))])]
    pallas_call x8 -> x7, Pallas kernels: 24.6 us -> 15.2 us  [the longest x3 15.1 us: stage(): pl.pallas_call(functools.partial(stage_kernel, n, nb, piece, seen, ds), o...]
    all_to_all x1, blocking collectives: 20.5 us -> 11.3 us  [on_device(): lax.all_to_all(scores, 'grp', split_axis=0, concat_axis=0, tiled=True)]
    unnamed x24 -> x6, local copies, waits for them, and re-layouts: 7.62 us -> 3.05 us
    ppermute x31 -> x22, starting transfers between devices: 24 us -> 20.8 us  [send(): lax.ppermute(x, axis, [(i, i ^ by) for i in range(lax.axis_size(axis))])]
  transfers between devices with their start and end apart: 31 -> 22, of which waited for: 9 -> 11; matrix products, arithmetic and copies ran while one was open for 0% -> 0% of each run, Pallas kernels for 18% -> 13%
where the time goes in v4:
time: 114 us
  waiting for transfers between devices  55 us (48%)
  Pallas kernels  23.6 us (21%)
  starting transfers between devices  20.8 us (18%)
  blocking collectives  11.3 us (10%)
  local copies, waits for them, and re-layouts  3.05 us (3%)
    ppermute x22, waiting for transfers between devices, send(): lax.ppermute(x, axis, [(i, i ^ by) for i in range(lax.axis_size(axis))])  55 us
    ppermute x22, starting transfers between devices, send(): lax.ppermute(x, axis, [(i, i ^ by) for i in range(lax.axis_size(axis))])  20.8 us
    pallas_call x3, Pallas kernels, stage(): pl.pallas_call(functools.partial(stage_kernel, n, nb, piece, seen, ds), o...  15.1 us
    all_to_all x1, blocking collectives, on_device(): lax.all_to_all(scores, 'grp', split_axis=0, concat_axis=0, tiled=True)  11.3 us
    pallas_call x1, Pallas kernels, on_device(): pl.pallas_call(functools.partial(first_kernel, n, piece, rows * nb, early...  4.5 us
    pallas_call x1, Pallas kernels, on_device(): pl.pallas_call(functools.partial(second_kernel, n, piece, late), out_shap...  3.07 us
    unnamed x6, local copies, waits for them, and re-layouts  3.05 us
  transfers between devices with their start and end apart: 22, of which 11 were waited for; matrix products, arithmetic and copies ran while one was open for 0% of the time, Pallas kernels for 13%

profile of v4, /device:TPU:0, one launch (start us, length us, event | category | flops | bytes accessed | tf_op | source)
XLA Modules:
  0.0 114.0 jit_solution(15848824689667345733)
XLA Ops:
  0.1 1.7 %copy-done = bf16[1536,768]{1,0:T(8,128)(2,1)S(1)} copy-done((bf16[1536,768]{1,0:T(8,128)(2,1)S(1)}, bf16[1536,768]{1,0:T(8,128)(2,1)}, u32[]{:S(2)}) %copy-start) | copy-done | bytes 2359320
  1.7 0.7 copy-done.1
  2.4 0.7 copy-done.2
  3.1 4.5 %first.1 = (s32[1,1536]{1,0:T(1,128)S(1)}, s32[1,1536]{1,0:T(1,128)S(1)}, f32[8,8,256]{2,1,0:T(8,128)S(1)}, bf16[1536,768]{1,0:T(8,128)(2,1)S(1)}, bf16[200,768]...) custom-call(s32[2]{0:T(128)S(1)} %pad_add_fusion.here_ref, s32[12,128]{1,0:T(8,128)S(1)} %bitcast.5, ...), custom_call_target="tpu_custom_call" | custom-call | tf_op jit(solution)/shard_map/first/pallas_call | solution.py:255
  7.6 3.0 %collective-permute-start.2 = (bf16[1,200,768]{2,1,0:T(8,128)(2,1)S(1)}, bf16[1,200,768]{2,1,0:T(8,128)(2,1)S(1)}, u32[]{:S(2)}, u32[]{:S(2)}) collective-permute-start(bf16[1,200,768]{2,1,0:T(8,128)(2,1)S(1)} %bitcast.6), channel_id=1, source_target_pairs={{0,2},{1,3},{2,0},{3,1},{4,6},{5,7},{6,4},{7,5},{8,10},{9,11},{10,... | collective-permute-start | bytes 921608 | tf_op jit(solution)/shard_map/ppermute | solution.py:231
  10.7 1.5 %collective-permute-start = (bf16[200,768]{1,0:T(8,128)(2,1)S(1)}, bf16[200,768]{1,0:T(8,128)(2,1)S(1)}, u32[]{:S(2)}, u32[]{:S(2)}) collective-permute-start(bf16[200,768]{1,0:T(8,128)(2,1)S(1)} %get-tuple-element.53), channel_id=1, source_target_pairs={{0,4},{4,0},{8,12},{12,8},{16,20},{20,16},{24,28},{28,24},{1,5},{5... | collective-permute-start | bytes 921608 | tf_op jit(solution)/shard_map/ppermute | solution.py:231
  12.2 2.6 %collective-permute-start.1 = (bf16[200,768]{1,0:T(8,128)(2,1)S(1)}, bf16[200,768]{1,0:T(8,128)(2,1)S(1)}, u32[]{:S(2)}, u32[]{:S(2)}) collective-permute-start(bf16[200,768]{1,0:T(8,128)(2,1)S(1)} %get-tuple-element.54), channel_id=1, source_target_pairs={{0,16},{4,20},{8,24},{12,28},{16,0},{20,4},{24,8},{28,12},{1,17},{... | collective-permute-start | bytes 921608 | tf_op jit(solution)/shard_map/ppermute | solution.py:231
  14.7 3.1 %second.1 = (bf16[200,768]{1,0:T(8,128)(2,1)S(1)}, bf16[200,768]{1,0:T(8,128)(2,1)S(1)}, bf16[200,768]{1,0:T(8,128)(2,1)S(1)}, bf16[200,768]{1,0:T(8,128)(2,1)S(...) custom-call(s32[2]{0:T(128)S(1)} %pad_add_fusion.here_ref, s32[1,1536]{1,0:T(1,128)S(1)} %get-tuple-element.51.fam_ref, ...), custom_call_target="tpu_custom_call" | custom-call | flops 14495514624 | tf_op jit(solution)/shard_map/second/pallas_call | solution.py:265
  17.9 1.5 %collective-permute-done.refs_0_ = bf16[200,768]{1,0:T(8,128)(2,1)S(1)} collective-permute-done((bf16[200,768]{1,0:T(8,128)(2,1)S(1)}, bf16[200,768]{1,0:T(8,128)(2,1)S(1)}, u32[]{:S(2)}, u32[]{:S(2)}) %collective-permute-start) | collective-permute-done | bytes 307232 | tf_op jit(solution)/shard_map/ppermute | solution.py:231
  19.4 8.7 %collective-permute-done.1.refs_1_ = bf16[200,768]{1,0:T(8,128)(2,1)S(1)} collective-permute-done((bf16[200,768]{1,0:T(8,128)(2,1)S(1)}, bf16[200,768]{1,0:T(8,128)(2,1)S(1)}, u32[]{:S(2)}, u32[]{:S(2)}) %collective-permute-start.1) | collective-permute-done | bytes 307232 | tf_op jit(solution)/shard_map/ppermute | solution.py:231
  28.1 0.6 collective-permute-start.6
  28.7 0.7 collective-permute-start.4
  29.4 3.4 %collective-permute-start.5 = (bf16[200,768]{1,0:T(8,128)(2,1)S(1)}, bf16[200,768]{1,0:T(8,128)(2,1)S(1)}, u32[]{:S(2)}, u32[]{:S(2)}) collective-permute-start(bf16[200,768]{1,0:T(8,128)(2,1)S(1)} %get-tuple-element.64), channel_id=1, source_target_pairs={{0,20},{4,16},{8,28},{12,24},{16,4},{20,0},{24,12},{28,8},{1,21},{... | collective-permute-start | bytes 921608 | tf_op jit(solution)/shard_map/ppermute | solution.py:231
  32.7 10.2 %collective-permute-done.4.refs_0_ = bf16[200,768]{1,0:T(8,128)(2,1)S(1)} collective-permute-done((bf16[200,768]{1,0:T(8,128)(2,1)S(1)}, bf16[200,768]{1,0:T(8,128)(2,1)S(1)}, u32[]{:S(2)}, u32[]{:S(2)}) %collective-permute-start.4) | collective-permute-done | bytes 307232 | tf_op jit(solution)/shard_map/ppermute | solution.py:231
  42.9 3.5 %collective-permute-done.5.refs_1_ = bf16[200,768]{1,0:T(8,128)(2,1)S(1)} collective-permute-done((bf16[200,768]{1,0:T(8,128)(2,1)S(1)}, bf16[200,768]{1,0:T(8,128)(2,1)S(1)}, u32[]{:S(2)}, u32[]{:S(2)}) %collective-permute-start.5) | collective-permute-done | bytes 307232 | tf_op jit(solution)/shard_map/ppermute | solution.py:231
  46.5 1.6 %collective-permute-start.8 = (bf16[2,200,768]{2,1,0:T(8,128)(2,1)S(1)}, bf16[2,200,768]{2,1,0:T(8,128)(2,1)S(1)}, u32[]{:S(2)}, u32[]{:S(2)}) collective-permute-start(bf16[2,200,768]{2,1,0:T(8,128)(2,1)S(1)} %get-tuple-element.70.refs_3_), channel_id=1, source_target_pairs={{0,2},{1,3},{2,0},{3,1},{4,6},{5,7},{6,4},{7,5},{8,10},{9,11},{10,... | collective-permute-start | bytes 1843208 | tf_op jit(solution)/shard_map/ppermute | solution.py:231
  48.1 1.1 collective-permute-start.3
  49.1 2.0 %collective-permute-start.7 = (bf16[200,768]{1,0:T(8,128)(2,1)S(1)}, bf16[200,768]{1,0:T(8,128)(2,1)S(1)}, u32[]{:S(2)}, u32[]{:S(2)}) collective-permute-start(bf16[200,768]{1,0:T(8,128)(2,1)S(1)} %get-tuple-element.68), channel_id=1, source_target_pairs={{0,24},{4,28},{8,16},{12,20},{16,8},{20,12},{24,0},{28,4},{1,25},{... | collective-permute-start | bytes 921608 | tf_op jit(solution)/shard_map/ppermute | solution.py:231
  51.7 5.2 %collective-permute-done.3.refs_0_ = bf16[200,768]{1,0:T(8,128)(2,1)S(1)} collective-permute-done((bf16[200,768]{1,0:T(8,128)(2,1)S(1)}, bf16[200,768]{1,0:T(8,128)(2,1)S(1)}, u32[]{:S(2)}, u32[]{:S(2)}) %collective-permute-start.3) | collective-permute-done | bytes 307232 | tf_op jit(solution)/shard_map/ppermute | solution.py:231
  56.9 7.0 %collective-permute-done.7.refs_1_ = bf16[200,768]{1,0:T(8,128)(2,1)S(1)} collective-permute-done((bf16[200,768]{1,0:T(8,128)(2,1)S(1)}, bf16[200,768]{1,0:T(8,128)(2,1)S(1)}, u32[]{:S(2)}, u32[]{:S(2)}) %collective-permute-start.7) | collective-permute-done | bytes 307232 | tf_op jit(solution)/shard_map/ppermute | solution.py:231
  64.6 2.8 %collective-permute-done.11.rest_3_ = bf16[1,200,768]{2,1,0:T(8,128)(2,1)S(1)} collective-permute-done((bf16[1,200,768]{2,1,0:T(8,128)(2,1)S(1)}, bf16[1,200,768]{2,1,0:T(8,128)(2,1)S(1)}, u32[]{:S(2)}, u32[]{:S(2)}) %collective-permute-start.11) | collective-permute-done | bytes 307232 | tf_op jit(solution)/shard_map/ppermute | solution.py:231
  67.4 0.5 collective-permute-start.16
  67.9 1.7 %collective-permute-start.9 = (bf16[200,768]{1,0:T(8,128)(2,1)S(1)}, bf16[200,768]{1,0:T(8,128)(2,1)S(1)}, u32[]{:S(2)}, u32[]{:S(2)}) collective-permute-start(bf16[200,768]{1,0:T(8,128)(2,1)S(1)} %get-tuple-element.72), channel_id=1, source_target_pairs={{0,28},{4,24},{8,20},{12,16},{16,12},{20,8},{24,4},{28,0},{1,29},{... | collective-permute-start | bytes 921608 | tf_op jit(solution)/shard_map/ppermute | solution.py:231
  69.6 6.4 %stage.3 = (f32[8,128]{1,0:T(8,128)S(1)}, bf16[8,4,192,768]{3,2,1,0:T(8,128)(2,1)S(1)}, f32[8,8,192]{2,1,0:T(8,128)S(1)}, f32[32,192,128]{2,1,0:T(8,128)S(1)}, f...) custom-call(s32[2]{0:T(128)S(1)} %pad_add_fusion.here_ref, ...), custom_call_target="tpu_custom_call", output_to_operand_aliasing={{0}: (1, {})} | custom-call | flops 6794772480 | tf_op jit(solution)/shard_map/stage/pallas_call | solution.py:318
  76.0 3.7 %collective-permute-done.9.refs_0_ = bf16[200,768]{1,0:T(8,128)(2,1)S(1)} collective-permute-done((bf16[200,768]{1,0:T(8,128)(2,1)S(1)}, bf16[200,768]{1,0:T(8,128)(2,1)S(1)}, u32[]{:S(2)}, u32[]{:S(2)}) %collective-permute-start.9) | collective-permute-done | bytes 307232 | tf_op jit(solution)/shard_map/ppermute | solution.py:231
  79.7 3.6 %collective-permute-done.16.refs_3_ = bf16[2,200,768]{2,1,0:T(8,128)(2,1)S(1)} collective-permute-done((bf16[2,200,768]{2,1,0:T(8,128)(2,1)S(1)}, bf16[2,200,768]{2,1,0:T(8,128)(2,1)S(1)}, u32[]{:S(2)}, u32[]{:S(2)}) %collective-permute-start.16) | collective-permute-done | bytes 614432 | tf_op jit(solution)/shard_map/ppermute | solution.py:231
  83.9 0.5 collective-permute-start.20
  84.4 8.7 %collective-permute-done.20.rest_2_ = bf16[1,200,768]{2,1,0:T(8,128)(2,1)S(1)} collective-permute-done((bf16[1,200,768]{2,1,0:T(8,128)(2,1)S(1)}, bf16[1,200,768]{2,1,0:T(8,128)(2,1)S(1)}, u32[]{:S(2)}, u32[]{:S(2)}) %collective-permute-start.20) | collective-permute-done | bytes 307232 | tf_op jit(solution)/shard_map/ppermute | solution.py:231
  93.1 5.3 %stage.4 = (f32[8,128]{1,0:T(8,128)S(1)}, bf16[8,4,192,768]{3,2,1,0:T(8,128)(2,1)S(1)}, f32[8,8,192]{2,1,0:T(8,128)S(1)}, f32[32,192,128]{2,1,0:T(8,128)S(1)}, f...) custom-call(s32[2]{0:T(128)S(1)} %pad_add_fusion.here_ref, ...), custom_call_target="tpu_custom_call", output_to_operand_aliasing={{0}: (1, {}), {1}: (6, {}), {2}: (7, {}), {3}: (8, {}), {4}... | custom-call | flops 5888802816 | tf_op jit(solution)/shard_map/stage/pallas_call | solution.py:318
  98.4 3.4 %stage.5 = (f32[8,128]{1,0:T(8,128)S(1)}, f32[8,1,192]{2,1,0:T(1,128)S(1)}, bf16[8,4,192,768]{3,2,1,0:T(8,128)(2,1)S(1)}, f32[8,8,192]{2,1,0:T(8,128)S(1)}, f32[...) custom-call(s32[2]{0:T(128)S(1)} %pad_add_fusion.here_ref, ...), custom_call_target="tpu_custom_call", output_to_operand_aliasing={{0}: (1, {}), {2}: (6, {}), {3}: (7, {}), {4}: (8, {}), {5}... | custom-call | flops 3623878656 | tf_op jit(solution)/shard_map/stage/pallas_call | solution.py:318
  101.8 11.3 %all_to_all.5.score_ref = f32[8,1,192]{2,1,0:T(1,128)S(1)} all-to-all(f32[8,1,192]{2,1,0:T(1,128)S(1)} %get-tuple-element.96), channel_id=1, replica_groups=mesh['grp'=8,'blk'=4] {'grp'}, dimensions={0} | all-to-all | bytes 12288 | tf_op jit(solution)/shard_map/all_to_all | solution.py:358
  113.2 0.8 unpack.1
  (30 shorter events, 2.1 us)
Async XLA Ops:
  0.1 1.7 %copy-start = (bf16[1536,768]{1,0:T(8,128)(2,1)S(1)}, bf16[1536,768]{1,0:T(8,128)(2,1)}, u32[]{:S(2)}) copy-start(bf16[1536,768]{1,0:T(8,128)(2,1)} %emb_ref.1) | copy-start | bytes 7077892
  1.7 0.7 copy-start.1
  2.4 0.7 copy-start.2
  7.6 10.3 %collective-permute-start.2 = (bf16[1,200,768]{2,1,0:T(8,128)(2,1)S(1)}, bf16[1,200,768]{2,1,0:T(8,128)(2,1)S(1)}, u32[]{:S(2)}, u32[]{:S(2)}) collective-permute-start(bf16[1,200,768]{2,1,0:T(8,128)(2,1)S(1)} %bitcast.6), channel_id=1, source_target_pairs={{0,2},{1,3},{2,0},{3,1},{4,6},{5,7},{6,4},{7,5},{8,10},{9,11},{10,... | collective-permute-start | bytes 921608 | tf_op jit(solution)/shard_map/ppermute | solution.py:231
  10.7 8.7 %collective-permute-start = (bf16[200,768]{1,0:T(8,128)(2,1)S(1)}, bf16[200,768]{1,0:T(8,128)(2,1)S(1)}, u32[]{:S(2)}, u32[]{:S(2)}) collective-permute-start(bf16[200,768]{1,0:T(8,128)(2,1)S(1)} %get-tuple-element.53), channel_id=1, source_target_pairs={{0,4},{4,0},{8,12},{12,8},{16,20},{20,16},{24,28},{28,24},{1,5},{5... | collective-permute-start | bytes 921608 | tf_op jit(solution)/shard_map/ppermute | solution.py:231
  12.2 15.9 %collective-permute-start.1 = (bf16[200,768]{1,0:T(8,128)(2,1)S(1)}, bf16[200,768]{1,0:T(8,128)(2,1)S(1)}, u32[]{:S(2)}, u32[]{:S(2)}) collective-permute-start(bf16[200,768]{1,0:T(8,128)(2,1)S(1)} %get-tuple-element.54), channel_id=1, source_target_pairs={{0,16},{4,20},{8,24},{12,28},{16,0},{20,4},{24,8},{28,12},{1,17},{... | collective-permute-start | bytes 921608 | tf_op jit(solution)/shard_map/ppermute | solution.py:231
  28.1 18.3 %collective-permute-start.6 = (bf16[2,200,768]{2,1,0:T(8,128)(2,1)S(1)}, bf16[2,200,768]{2,1,0:T(8,128)(2,1)S(1)}, u32[]{:S(2)}, u32[]{:S(2)}) collective-permute-start(bf16[2,200,768]{2,1,0:T(8,128)(2,1)S(1)} %get-tuple-element.66.refs_3_), channel_id=1, source_target_pairs={{0,2},{1,3},{2,0},{3,1},{4,6},{5,7},{6,4},{7,5},{8,10},{9,11},{10,... | collective-permute-start | bytes 1843208 | tf_op jit(solution)/shard_map/ppermute | solution.py:231
  28.7 14.2 %collective-permute-start.4 = (bf16[200,768]{1,0:T(8,128)(2,1)S(1)}, bf16[200,768]{1,0:T(8,128)(2,1)S(1)}, u32[]{:S(2)}, u32[]{:S(2)}) collective-permute-start(bf16[200,768]{1,0:T(8,128)(2,1)S(1)} %get-tuple-element.63), channel_id=1, source_target_pairs={{0,8},{4,12},{8,0},{12,4},{16,24},{20,28},{24,16},{28,20},{1,9},{5... | collective-permute-start | bytes 921608 | tf_op jit(solution)/shard_map/ppermute | solution.py:231
  29.4 17.1 %collective-permute-start.5 = (bf16[200,768]{1,0:T(8,128)(2,1)S(1)}, bf16[200,768]{1,0:T(8,128)(2,1)S(1)}, u32[]{:S(2)}, u32[]{:S(2)}) collective-permute-start(bf16[200,768]{1,0:T(8,128)(2,1)S(1)} %get-tuple-element.64), channel_id=1, source_target_pairs={{0,20},{4,16},{8,28},{12,24},{16,4},{20,0},{24,12},{28,8},{1,21},{... | collective-permute-start | bytes 921608 | tf_op jit(solution)/shard_map/ppermute | solution.py:231
  46.5 17.4 %collective-permute-start.8 = (bf16[2,200,768]{2,1,0:T(8,128)(2,1)S(1)}, bf16[2,200,768]{2,1,0:T(8,128)(2,1)S(1)}, u32[]{:S(2)}, u32[]{:S(2)}) collective-permute-start(bf16[2,200,768]{2,1,0:T(8,128)(2,1)S(1)} %get-tuple-element.70.refs_3_), channel_id=1, source_target_pairs={{0,2},{1,3},{2,0},{3,1},{4,6},{5,7},{6,4},{7,5},{8,10},{9,11},{10,... | collective-permute-start | bytes 1843208 | tf_op jit(solution)/shard_map/ppermute | solution.py:231
  48.1 8.8 %collective-permute-start.3 = (bf16[200,768]{1,0:T(8,128)(2,1)S(1)}, bf16[200,768]{1,0:T(8,128)(2,1)S(1)}, u32[]{:S(2)}, u32[]{:S(2)}) collective-permute-start(bf16[200,768]{1,0:T(8,128)(2,1)S(1)} %get-tuple-element.62), channel_id=1, source_target_pairs={{0,12},{4,8},{8,4},{12,0},{16,28},{20,24},{24,20},{28,16},{1,13},{... | collective-permute-start | bytes 921608 | tf_op jit(solution)/shard_map/ppermute | solution.py:231
  49.1 14.8 %collective-permute-start.7 = (bf16[200,768]{1,0:T(8,128)(2,1)S(1)}, bf16[200,768]{1,0:T(8,128)(2,1)S(1)}, u32[]{:S(2)}, u32[]{:S(2)}) collective-permute-start(bf16[200,768]{1,0:T(8,128)(2,1)S(1)} %get-tuple-element.68), channel_id=1, source_target_pairs={{0,24},{4,28},{8,16},{12,20},{16,8},{20,12},{24,0},{28,4},{1,25},{... | collective-permute-start | bytes 921608 | tf_op jit(solution)/shard_map/ppermute | solution.py:231
  51.2 13.4 %collective-permute-start.10 = (bf16[1,200,768]{2,1,0:T(8,128)(2,1)S(1)}, bf16[1,200,768]{2,1,0:T(8,128)(2,1)S(1)}, u32[]{:S(2)}, u32[]{:S(2)}) collective-permute-start(bf16[1,200,768]{2,1,0:T(8,128)(2,1)S(1)} %bitcast.7), channel_id=1, source_target_pairs={{0,1},{1,0},{2,3},{3,2},{4,5},{5,4},{6,7},{7,6},{8,9},{9,8},{10,11... | collective-permute-start | bytes 921608 | tf_op jit(solution)/shard_map/ppermute | solution.py:231
  51.2 16.7 %collective-permute-start.12 = (bf16[2,200,768]{2,1,0:T(8,128)(2,1)S(1)}, bf16[2,200,768]{2,1,0:T(8,128)(2,1)S(1)}, u32[]{:S(2)}, u32[]{:S(2)}) collective-permute-start(bf16[2,200,768]{2,1,0:T(8,128)(2,1)S(1)} %get-tuple-element.75.rest_4_), channel_id=1, source_target_pairs={{0,1},{1,0},{2,3},{3,2},{4,5},{5,4},{6,7},{7,6},{8,9},{9,8},{10,11... | collective-permute-start | bytes 1843208 | tf_op jit(solution)/shard_map/ppermute | solution.py:231
  56.9 12.7 %collective-permute-start.13 = (bf16[2,200,768]{2,1,0:T(8,128)(2,1)S(1)}, bf16[2,200,768]{2,1,0:T(8,128)(2,1)S(1)}, u32[]{:S(2)}, u32[]{:S(2)}) collective-permute-start(bf16[2,200,768]{2,1,0:T(8,128)(2,1)S(1)} %get-tuple-element.76.rest_6_), channel_id=1, source_target_pairs={{0,1},{1,0},{2,3},{3,2},{4,5},{5,4},{6,7},{7,6},{8,9},{9,8},{10,11... | collective-permute-start | bytes 1843208 | tf_op jit(solution)/shard_map/ppermute | solution.py:231
  64.0 5.7 %collective-permute-start.14 = (bf16[2,200,768]{2,1,0:T(8,128)(2,1)S(1)}, bf16[2,200,768]{2,1,0:T(8,128)(2,1)S(1)}, u32[]{:S(2)}, u32[]{:S(2)}) collective-permute-start(bf16[2,200,768]{2,1,0:T(8,128)(2,1)S(1)} %get-tuple-element.77.rest_8_), channel_id=1, source_target_pairs={{0,1},{1,0},{2,3},{3,2},{4,5},{5,4},{6,7},{7,6},{8,9},{9,8},{10,11... | collective-permute-start | bytes 1843208 | tf_op jit(solution)/shard_map/ppermute | solution.py:231
  64.0 5.6 %collective-permute-start.15 = (bf16[2,200,768]{2,1,0:T(8,128)(2,1)S(1)}, bf16[2,200,768]{2,1,0:T(8,128)(2,1)S(1)}, u32[]{:S(2)}, u32[]{:S(2)}) collective-permute-start(bf16[2,200,768]{2,1,0:T(8,128)(2,1)S(1)} %get-tuple-element.78.rest_10_), channel_id=1, source_target_pairs={{0,1},{1,0},{2,3},{3,2},{4,5},{5,4},{6,7},{7,6},{8,9},{9,8},{10,11... | collective-permute-start | bytes 1843208 | tf_op jit(solution)/shard_map/ppermute | solution.py:231
  64.5 2.8 %collective-permute-start.11 = (bf16[1,200,768]{2,1,0:T(8,128)(2,1)S(1)}, bf16[1,200,768]{2,1,0:T(8,128)(2,1)S(1)}, u32[]{:S(2)}, u32[]{:S(2)}) collective-permute-start(bf16[1,200,768]{2,1,0:T(8,128)(2,1)S(1)} %get-tuple-element.74.rest_2_), channel_id=1, source_target_pairs={{0,1},{1,0},{2,3},{3,2},{4,5},{5,4},{6,7},{7,6},{8,9},{9,8},{10,11... | collective-permute-start | bytes 921608 | tf_op jit(solution)/shard_map/ppermute | solution.py:231
  67.4 15.9 %collective-permute-start.16 = (bf16[2,200,768]{2,1,0:T(8,128)(2,1)S(1)}, bf16[2,200,768]{2,1,0:T(8,128)(2,1)S(1)}, u32[]{:S(2)}, u32[]{:S(2)}) collective-permute-start(bf16[2,200,768]{2,1,0:T(8,128)(2,1)S(1)} %get-tuple-element.80.refs_2_), channel_id=1, source_target_pairs={{0,2},{1,3},{2,0},{3,1},{4,6},{5,7},{6,4},{7,5},{8,10},{9,11},{10,... | collective-permute-start | bytes 1843208 | tf_op jit(solution)/shard_map/ppermute | solution.py:231
  67.9 11.8 %collective-permute-start.9 = (bf16[200,768]{1,0:T(8,128)(2,1)S(1)}, bf16[200,768]{1,0:T(8,128)(2,1)S(1)}, u32[]{:S(2)}, u32[]{:S(2)}) collective-permute-start(bf16[200,768]{1,0:T(8,128)(2,1)S(1)} %get-tuple-element.72), channel_id=1, source_target_pairs={{0,28},{4,24},{8,20},{12,16},{16,12},{20,8},{24,4},{28,0},{1,29},{... | collective-permute-start | bytes 921608 | tf_op jit(solution)/shard_map/ppermute | solution.py:231
  83.3 9.8 %collective-permute-start.17 = (bf16[2,200,768]{2,1,0:T(8,128)(2,1)S(1)}, bf16[2,200,768]{2,1,0:T(8,128)(2,1)S(1)}, u32[]{:S(2)}, u32[]{:S(2)}) collective-permute-start(bf16[2,200,768]{2,1,0:T(8,128)(2,1)S(1)} %get-tuple-element.82.rest_0_), channel_id=1, source_target_pairs={{0,1},{1,0},{2,3},{3,2},{4,5},{5,4},{6,7},{7,6},{8,9},{9,8},{10,11... | collective-permute-start | bytes 1843208 | tf_op jit(solution)/shard_map/ppermute | solution.py:231
  83.4 9.8 %collective-permute-start.18 = (bf16[2,200,768]{2,1,0:T(8,128)(2,1)S(1)}, bf16[2,200,768]{2,1,0:T(8,128)(2,1)S(1)}, u32[]{:S(2)}, u32[]{:S(2)}) collective-permute-start(bf16[2,200,768]{2,1,0:T(8,128)(2,1)S(1)} %get-tuple-element.83.rest_2_), channel_id=1, source_target_pairs={{0,1},{1,0},{2,3},{3,2},{4,5},{5,4},{6,7},{7,6},{8,9},{9,8},{10,11... | collective-permute-start | bytes 1843208 | tf_op jit(solution)/shard_map/ppermute | solution.py:231
  83.9 9.3 %collective-permute-start.20 = (bf16[1,200,768]{2,1,0:T(8,128)(2,1)S(1)}, bf16[1,200,768]{2,1,0:T(8,128)(2,1)S(1)}, u32[]{:S(2)}, u32[]{:S(2)}) collective-permute-start(bf16[1,200,768]{2,1,0:T(8,128)(2,1)S(1)} %get-tuple-element.90.rest_0_), channel_id=1, source_target_pairs={{0,2},{1,3},{2,0},{3,1},{4,6},{5,7},{6,4},{7,5},{8,10},{9,11},{10,... | collective-permute-start | bytes 921608 | tf_op jit(solution)/shard_map/ppermute | solution.py:231
  84.4 14.0 %collective-permute-start.19 = (bf16[1,200,768]{2,1,0:T(8,128)(2,1)S(1)}, bf16[1,200,768]{2,1,0:T(8,128)(2,1)S(1)}, u32[]{:S(2)}, u32[]{:S(2)}) collective-permute-start(bf16[1,200,768]{2,1,0:T(8,128)(2,1)S(1)} %get-tuple-element.90.rest_0_), channel_id=1, source_target_pairs={{0,1},{1,0},{2,3},{3,2},{4,5},{5,4},{6,7},{7,6},{8,9},{9,8},{10,11... | collective-permute-start | bytes 921608 | tf_op jit(solution)/shard_map/ppermute | solution.py:231
  93.1 5.3 %collective-permute-start.21 = (bf16[1,200,768]{2,1,0:T(8,128)(2,1)S(1)}, bf16[1,200,768]{2,1,0:T(8,128)(2,1)S(1)}, u32[]{:S(2)}, u32[]{:S(2)}) collective-permute-start(bf16[1,200,768]{2,1,0:T(8,128)(2,1)S(1)} %collective-permute-done.20.rest_2_), channel_id=1, source_target_pairs={{0,1},{1,0},{2,3},{3,2},{4,5},{5,4},{6,7},{7,6},{8,9},{9,8},{10,11... | collective-permute-start | bytes 921608 | tf_op jit(solution)/shard_map/ppermute | solution.py:231

commit v5 on v4

--- a/solution.py
+++ b/solution.py
@@ -71,7 +71,9 @@
         got = jnp.dot(select, unit_ref[...], preferred_element_type=F32)
         note = note_ref[grp ^ d]
         note = jnp.concatenate([note, jnp.zeros((NOTE, width - note.shape[1]), F32)], axis=1)
-        out[...] = jnp.concatenate([got, note], axis=0).astype(BF16)
+        out[:piece + NOTE] = jnp.concatenate([got, note], axis=0).astype(BF16)
+        if out.shape[0] > piece + NOTE:
+            out[piece + NOTE:] = jnp.zeros((out.shape[0] - piece - NOTE, width), BF16)
 
 
 def first_kernel(n, piece, family_rows, which, here_ref, route_ref, cluster_ref, emb_ref, *rest):
@@ -117,7 +119,7 @@
 def join_kernel(count, *refs):
     out_ref = refs[-1]
     for i in range(count):
-        out_ref[i] = refs[i][...]
+        out_ref[i] = refs[i][:out_ref.shape[1]]
 
 
 def stage_kernel(n, nb, piece, old, groups, here_ref, token_ref, *rest):
@@ -249,6 +251,8 @@
     blocks = rows // LANES
     wide = -(-piece // LANES) * LANES
     one_piece = shape(piece + NOTE, width, kind=BF16)
+    longer = shape(piece + 2 * NOTE, width, kind=BF16)
+    kind_of = {d: longer if n == 8 and d in (4, 6) else one_piece for d in range(n)}
 
     early = [half, 0, 1]
     late = [d for d in range(n) if d not in early]
@@ -256,7 +260,7 @@
         functools.partial(first_kernel, n, piece, rows * nb, early),
         out_shape=[shape(1, rows, kind=I32)] * 2
         + [shape(n, NOTE, wide), shape(rows, width, kind=BF16)]
-        + [one_piece] * len(early),
+        + [kind_of[d] for d in early],
         in_specs=[SMEM, VMEM, VMEM, VMEM],
         out_specs=[VMEM] * (4 + len(early)),
         compiler_params=limit(16),
@@ -264,7 +268,7 @@
     )(here, route.reshape(blocks, LANES), cluster, embeddings)
     *others, token = pl.pallas_call(
         functools.partial(second_kernel, n, piece, late),
-        out_shape=[one_piece] * len(late) + [shape(8, LANES)],
+        out_shape=[kind_of[d] for d in late] + [shape(8, LANES)],
         in_specs=[SMEM] + [VMEM] * 4,
         out_specs=[VMEM] * (len(late) + 1),
         compiler_params=limit(16),
@@ -282,18 +286,18 @@
         nonlocal token
         ins = [own[d] for d in ds]
         kept = [token, *later]
-        token, *later, joined = pl.pallas_call(
+        joined = [shape(len(ins), *one_piece.shape, kind=BF16)] if ins else []
+        token, *rest = pl.pallas_call(
             functools.partial(join_kernel, len(ins)),
-            out_shape=[jax.ShapeDtypeStruct(x.shape, x.dtype) for x in kept]
-            + [shape(len(ins), *one_piece.shape, kind=BF16)],
+            out_shape=[jax.ShapeDtypeStruct(x.shape, x.dtype) for x in kept] + joined,
             in_specs=[VMEM] * (len(ins) + len(kept)),
-            out_specs=[VMEM] * (len(kept) + 1),
+            out_specs=[VMEM] * (len(kept) + len(joined)),
             input_output_aliases={len(ins) + i: i for i in range(len(kept))},
             compiler_params=limit(4),
             cost_estimate=cost(0),
             name="join",
         )(*ins, *kept)
-        return [joined, *later]
+        return rest[len(later):] + rest[:len(later)]
 
     def stage(*groups):
         nonlocal token, seen, state
@@ -305,8 +309,8 @@
             shape(CLUSTERS - 1, 1, piece),
         ]
         args = [here, token]
-        for _, mine, across in groups:
-            args += [mine, send(mine, "blk", 1), across, send(across, "blk", 1)]
+        for _, *four in groups:
+            args += four
         args += list(state)
         ds = [list(group[0]) for group in groups]
         now = seen + sum(ds, [])
@@ -329,30 +333,30 @@
 
     if n == 8:
         to_columns(4, 1)
-        one = own[0].reshape(1, *one_piece.shape)
-        one_across = send(one, "blk", 2)
-        two, one_across, sent[5], sent[2], sent[3] = join(
-            (1, 4), [one_across, sent[5], sent[2], sent[3]]
-        )
-        two_across = send(two, "blk", 2)
-        to_columns(5, 2, 3)
-        three, two, two_across, sent[6] = join((2, 5), [two, two_across, sent[6]])
-        three_across = send(three, "blk", 2)
-        to_columns(6)
-        four, three, three_across, sent[7] = join((3, 6), [three, three_across, sent[7]])
-        four_across = send(four, "blk", 2)
+        m0 = own[0].reshape(1, *one_piece.shape)
+        y0, c0 = send(m0, "blk", 2), send(m0, "blk", 1)
+        m1, y0, c0, sent[5], sent[2] = join((4, 1), [y0, c0, sent[5], sent[2]])
+        to_columns(5, 2)
+        y1, c1, x0 = send(m1, "blk", 2), send(m1, "blk", 1), send(y0, "blk", 1)
+        m2, y1, c1, x0, sent[6], sent[3] = join((5, 2), [y1, c1, x0, sent[6], sent[3]])
+        to_columns(6, 3)
+        y2, c2, x1 = send(m2, "blk", 2), send(m2, "blk", 1), send(y1, "blk", 1)
+        m3, y2, c2, x1, sent[7] = join((6, 3), [y2, c2, x1, sent[7]])
         to_columns(7)
-        stage(((0,), one, one_across), ((1, 4), two, two_across), ((2, 5), three, three_across))
-        five, four, four_across = join((7,), [four, four_across])
-        five_across = send(five, "blk", 2)
-        stage(((3, 6), four, four_across))
-        stage(((7,), five, five_across))
+        y3, c3, x2 = send(m3, "blk", 2), send(m3, "blk", 1), send(y2, "blk", 1)
+        stage(((0,), m0, c0, y0, x0), ((4, 1), m1, c1, y1, x1), ((5, 2), m2, c2, y2, x2))
+        m4, y3, c3 = join((7,), [y3, c3])
+        y4, c4, x3 = send(m4, "blk", 2), send(m4, "blk", 1), send(y3, "blk", 1)
+        stage(((6, 3), m3, c3, y3, x3))
+        (y4,) = join((), [y4])
+        stage(((7,), m4, c4, y4, send(y4, "blk", 1)))
     else:
         to_columns(*range(1, n))
         for lo in range(0, n, 8):
             ds = range(lo, lo + 8)
-            (joined,) = join(ds)
-            stage((ds, joined, send(joined, "blk", 2)))
+            (m,) = join(ds)
+            y = send(m, "blk", 2)
+            stage((ds, m, send(m, "blk", 1), y, send(y, "blk", 1)))
     scores = state[0]
 
     home = lax.all_to_all(scores, "grp", split_axis=0, concat_axis=0, tiled=True)

time: 114 us -> 111 us (0.974)
  waiting for transfers between devices: 55 us -> 53.3 us
    ppermute x22, waiting for transfers between devices: 55 us -> 53.3 us  [send(): lax.ppermute(x, axis, [(i, i ^ by) for i in range(lax.axis_size(axis))])]
    ppermute x22, starting transfers between devices: 20.8 us -> 19.7 us  [send(): lax.ppermute(x, axis, [(i, i ^ by) for i in range(lax.axis_size(axis))])]
where the time goes in v5:
time: 111 us
  waiting for transfers between devices  53.3 us (48%)
  Pallas kernels  23.5 us (21%)
  starting transfers between devices  19.7 us (18%)
  blocking collectives  10.8 us (10%)
  local copies, waits for them, and re-layouts  3.05 us (3%)
    ppermute x22, waiting for transfers between devices, send(): lax.ppermute(x, axis, [(i, i ^ by) for i in range(lax.axis_size(axis))])  53.3 us
    ppermute x22, starting transfers between devices, send(): lax.ppermute(x, axis, [(i, i ^ by) for i in range(lax.axis_size(axis))])  19.7 us
    pallas_call x3, Pallas kernels, stage(): pl.pallas_call(functools.partial(stage_kernel, n, nb, piece, seen, ds), o...  15 us
    all_to_all x1, blocking collectives, on_device(): lax.all_to_all(scores, 'grp', split_axis=0, concat_axis=0, tiled=True)  10.8 us
    pallas_call x1, Pallas kernels, on_device(): pl.pallas_call(functools.partial(first_kernel, n, piece, rows * nb, early...  4.48 us
    unnamed x6, local copies, waits for them, and re-layouts  3.05 us
    pallas_call x1, Pallas kernels, on_device(): pl.pallas_call(functools.partial(second_kernel, n, piece, late), out_shap...  3.03 us
  transfers between devices with their start and end apart: 22, of which 11 were waited for; matrix products, arithmetic and copies ran while one was open for 0% of the time, Pallas kernels for 13%

profile of v5, /device:TPU:0, one launch (start us, length us, event | category | flops | bytes accessed | tf_op | source)
XLA Modules:
  0.0 110.6 jit_solution(2911803307467845618)
XLA Ops:
  0.1 1.7 %copy-done = bf16[1536,768]{1,0:T(8,128)(2,1)S(1)} copy-done((bf16[1536,768]{1,0:T(8,128)(2,1)S(1)}, bf16[1536,768]{1,0:T(8,128)(2,1)}, u32[]{:S(2)}) %copy-start) | copy-done | bytes 2359320
  1.7 0.7 copy-done.1
  2.4 0.7 copy-done.2
  3.1 4.5 %first.1 = (s32[1,1536]{1,0:T(1,128)S(1)}, s32[1,1536]{1,0:T(1,128)S(1)}, f32[8,8,256]{2,1,0:T(8,128)S(1)}, bf16[1536,768]{1,0:T(8,128)(2,1)S(1)}, bf16[208,768]...) custom-call(s32[2]{0:T(128)S(1)} %pad_add_fusion.here_ref, s32[12,128]{1,0:T(8,128)S(1)} %bitcast.5, ...), custom_call_target="tpu_custom_call" | custom-call | tf_op jit(solution)/shard_map/first/pallas_call | solution.py:259
  7.6 3.0 %collective-permute-start.2 = (bf16[1,200,768]{2,1,0:T(8,128)(2,1)S(1)}, bf16[1,200,768]{2,1,0:T(8,128)(2,1)S(1)}, u32[]{:S(2)}, u32[]{:S(2)}) collective-permute-start(bf16[1,200,768]{2,1,0:T(8,128)(2,1)S(1)} %bitcast.6), channel_id=1, source_target_pairs={{0,2},{1,3},{2,0},{3,1},{4,6},{5,7},{6,4},{7,5},{8,10},{9,11},{10,... | collective-permute-start | bytes 921608 | tf_op jit(solution)/shard_map/ppermute | solution.py:233
  10.7 2.6 %collective-permute-start = (bf16[208,768]{1,0:T(8,128)(2,1)S(1)}, bf16[208,768]{1,0:T(8,128)(2,1)S(1)}, u32[]{:S(2)}, u32[]{:S(2)}) collective-permute-start(bf16[208,768]{1,0:T(8,128)(2,1)S(1)} %get-tuple-element.58), channel_id=1, source_target_pairs={{0,16},{4,20},{8,24},{12,28},{16,0},{20,4},{24,8},{28,12},{1,17},{... | collective-permute-start | bytes 958472 | tf_op jit(solution)/shard_map/ppermute | solution.py:233
  13.2 1.5 %collective-permute-start.1 = (bf16[200,768]{1,0:T(8,128)(2,1)S(1)}, bf16[200,768]{1,0:T(8,128)(2,1)S(1)}, u32[]{:S(2)}, u32[]{:S(2)}) collective-permute-start(bf16[200,768]{1,0:T(8,128)(2,1)S(1)} %get-tuple-element.59), channel_id=1, source_target_pairs={{0,4},{4,0},{8,12},{12,8},{16,20},{20,16},{24,28},{28,24},{1,5},{5... | collective-permute-start | bytes 921608 | tf_op jit(solution)/shard_map/ppermute | solution.py:233
  14.7 3.0 %second.1 = (bf16[200,768]{1,0:T(8,128)(2,1)S(1)}, bf16[200,768]{1,0:T(8,128)(2,1)S(1)}, bf16[200,768]{1,0:T(8,128)(2,1)S(1)}, bf16[208,768]{1,0:T(8,128)(2,1)S(...) custom-call(s32[2]{0:T(128)S(1)} %pad_add_fusion.here_ref, s32[1,1536]{1,0:T(1,128)S(1)} %get-tuple-element.56.fam_ref, ...), custom_call_target="tpu_custom_call" | custom-call | flops 14495514624 | tf_op jit(solution)/shard_map/second/pallas_call | solution.py:269
  17.9 4.7 %collective-permute-done.1.refs_1_ = bf16[200,768]{1,0:T(8,128)(2,1)S(1)} collective-permute-done((bf16[200,768]{1,0:T(8,128)(2,1)S(1)}, bf16[200,768]{1,0:T(8,128)(2,1)S(1)}, u32[]{:S(2)}, u32[]{:S(2)}) %collective-permute-start.1) | collective-permute-done | bytes 307232 | tf_op jit(solution)/shard_map/ppermute | solution.py:233
  22.6 5.7 %collective-permute-done.refs_0_ = bf16[208,768]{1,0:T(8,128)(2,1)S(1)} collective-permute-done((bf16[208,768]{1,0:T(8,128)(2,1)S(1)}, bf16[208,768]{1,0:T(8,128)(2,1)S(1)}, u32[]{:S(2)}, u32[]{:S(2)}) %collective-permute-start) | collective-permute-done | bytes 319520 | tf_op jit(solution)/shard_map/ppermute | solution.py:233
  28.4 0.5 collective-permute-start.6
  28.9 0.5 collective-permute-start.4
  29.4 4.5 %collective-permute-start.5 = (bf16[200,768]{1,0:T(8,128)(2,1)S(1)}, bf16[200,768]{1,0:T(8,128)(2,1)S(1)}, u32[]{:S(2)}, u32[]{:S(2)}) collective-permute-start(bf16[200,768]{1,0:T(8,128)(2,1)S(1)} %get-tuple-element.67), channel_id=1, source_target_pairs={{0,8},{4,12},{8,0},{12,4},{16,24},{20,28},{24,16},{28,20},{1,9},{5... | collective-permute-start | bytes 921608 | tf_op jit(solution)/shard_map/ppermute | solution.py:233
  34.0 13.1 %collective-permute-done.4.refs_0_ = bf16[200,768]{1,0:T(8,128)(2,1)S(1)} collective-permute-done((bf16[200,768]{1,0:T(8,128)(2,1)S(1)}, bf16[200,768]{1,0:T(8,128)(2,1)S(1)}, u32[]{:S(2)}, u32[]{:S(2)}) %collective-permute-start.4) | collective-permute-done | bytes 307232 | tf_op jit(solution)/shard_map/ppermute | solution.py:233
  47.1 0.9 collective-permute-done.5.refs_1_
  48.0 1.6 %collective-permute-start.11 = (bf16[2,200,768]{2,1,0:T(8,128)(2,1)S(1)}, bf16[2,200,768]{2,1,0:T(8,128)(2,1)S(1)}, u32[]{:S(2)}, u32[]{:S(2)}) collective-permute-start(bf16[2,200,768]{2,1,0:T(8,128)(2,1)S(1)} %get-tuple-element.76.rest_8_), channel_id=1, source_target_pairs={{0,2},{1,3},{2,0},{3,1},{4,6},{5,7},{6,4},{7,5},{8,10},{9,11},{10,... | collective-permute-start | bytes 1843208 | tf_op jit(solution)/shard_map/ppermute | solution.py:233
  49.6 0.5 collective-permute-start.13
  50.1 1.0 collective-permute-start.9
  51.2 16.5 %collective-permute-done.10.refs_1_ = bf16[200,768]{1,0:T(8,128)(2,1)S(1)} collective-permute-done((bf16[200,768]{1,0:T(8,128)(2,1)S(1)}, bf16[200,768]{1,0:T(8,128)(2,1)S(1)}, u32[]{:S(2)}, u32[]{:S(2)}) %collective-permute-start.10) | collective-permute-done | bytes 307232 | tf_op jit(solution)/shard_map/ppermute | solution.py:233
  67.9 0.6 collective-permute-start.16
  68.6 2.2 %collective-permute-start.14 = (bf16[200,768]{1,0:T(8,128)(2,1)S(1)}, bf16[200,768]{1,0:T(8,128)(2,1)S(1)}, u32[]{:S(2)}, u32[]{:S(2)}) collective-permute-start(bf16[200,768]{1,0:T(8,128)(2,1)S(1)} %get-tuple-element.79), channel_id=1, source_target_pairs={{0,28},{4,24},{8,20},{12,16},{16,12},{20,8},{24,4},{28,0},{1,29},{... | collective-permute-start | bytes 921608 | tf_op jit(solution)/shard_map/ppermute | solution.py:233
  70.8 6.4 %stage.3 = (f32[8,128]{1,0:T(8,128)S(1)}, bf16[8,4,192,768]{3,2,1,0:T(8,128)(2,1)S(1)}, f32[8,8,192]{2,1,0:T(8,128)S(1)}, f32[32,192,128]{2,1,0:T(8,128)S(1)}, f...) custom-call(s32[2]{0:T(128)S(1)} %pad_add_fusion.here_ref, ...), custom_call_target="tpu_custom_call", output_to_operand_aliasing={{0}: (1, {})} | custom-call | flops 6794772480 | tf_op jit(solution)/shard_map/stage/pallas_call | solution.py:322
  77.2 3.8 %collective-permute-done.14.refs_0_ = bf16[200,768]{1,0:T(8,128)(2,1)S(1)} collective-permute-done((bf16[200,768]{1,0:T(8,128)(2,1)S(1)}, bf16[200,768]{1,0:T(8,128)(2,1)S(1)}, u32[]{:S(2)}, u32[]{:S(2)}) %collective-permute-start.14) | collective-permute-done | bytes 307232 | tf_op jit(solution)/shard_map/ppermute | solution.py:233
  81.0 3.2 %collective-permute-done.16.refs_2_ = bf16[2,200,768]{2,1,0:T(8,128)(2,1)S(1)} collective-permute-done((bf16[2,200,768]{2,1,0:T(8,128)(2,1)S(1)}, bf16[2,200,768]{2,1,0:T(8,128)(2,1)S(1)}, u32[]{:S(2)}, u32[]{:S(2)}) %collective-permute-start.16) | collective-permute-done | bytes 614432 | tf_op jit(solution)/shard_map/ppermute | solution.py:233
  84.3 0.6 collective-permute-start.19
  85.0 1.3 %collective-permute-done.18.rest_3_ = bf16[2,200,768]{2,1,0:T(8,128)(2,1)S(1)} collective-permute-done((bf16[2,200,768]{2,1,0:T(8,128)(2,1)S(1)}, bf16[2,200,768]{2,1,0:T(8,128)(2,1)S(1)}, u32[]{:S(2)}, u32[]{:S(2)}) %collective-permute-start.18) | collective-permute-done | bytes 614432 | tf_op jit(solution)/shard_map/ppermute | solution.py:233
  86.3 5.2 %stage.4 = (f32[8,128]{1,0:T(8,128)S(1)}, bf16[8,4,192,768]{3,2,1,0:T(8,128)(2,1)S(1)}, f32[8,8,192]{2,1,0:T(8,128)S(1)}, f32[32,192,128]{2,1,0:T(8,128)S(1)}, f...) custom-call(s32[2]{0:T(128)S(1)} %pad_add_fusion.here_ref, ...), custom_call_target="tpu_custom_call", output_to_operand_aliasing={{0}: (1, {}), {1}: (6, {}), {2}: (7, {}), {3}: (8, {}), {4}... | custom-call | flops 5888802816 | tf_op jit(solution)/shard_map/stage/pallas_call | solution.py:322
  91.6 2.4 %collective-permute-done.19.refs_1_ = bf16[1,200,768]{2,1,0:T(8,128)(2,1)S(1)} collective-permute-done((bf16[1,200,768]{2,1,0:T(8,128)(2,1)S(1)}, bf16[1,200,768]{2,1,0:T(8,128)(2,1)S(1)}, u32[]{:S(2)}, u32[]{:S(2)}) %collective-permute-start.19) | collective-permute-done | bytes 307232 | tf_op jit(solution)/shard_map/ppermute | solution.py:233
  94.0 1.6 %collective-permute-done.21.rest_3_ = bf16[1,200,768]{2,1,0:T(8,128)(2,1)S(1)} collective-permute-done((bf16[1,200,768]{2,1,0:T(8,128)(2,1)S(1)}, bf16[1,200,768]{2,1,0:T(8,128)(2,1)S(1)}, u32[]{:S(2)}, u32[]{:S(2)}) %collective-permute-start.21) | collective-permute-done | bytes 307232 | tf_op jit(solution)/shard_map/ppermute | solution.py:233
  95.6 3.4 %stage.5 = (f32[8,128]{1,0:T(8,128)S(1)}, f32[8,1,192]{2,1,0:T(1,128)S(1)}, bf16[8,4,192,768]{3,2,1,0:T(8,128)(2,1)S(1)}, f32[8,8,192]{2,1,0:T(8,128)S(1)}, f32[...) custom-call(s32[2]{0:T(128)S(1)} %pad_add_fusion.here_ref, ...), custom_call_target="tpu_custom_call", output_to_operand_aliasing={{0}: (1, {}), {2}: (6, {}), {3}: (7, {}), {4}: (8, {}), {5}... | custom-call | flops 3623878656 | tf_op jit(solution)/shard_map/stage/pallas_call | solution.py:322
  99.0 10.8 %all_to_all.5.score_ref = f32[8,1,192]{2,1,0:T(1,128)S(1)} all-to-all(f32[8,1,192]{2,1,0:T(1,128)S(1)} %get-tuple-element.106), channel_id=1, replica_groups=mesh['grp'=8,'blk'=4] {'grp'}, dimensions={0} | all-to-all | bytes 12288 | tf_op jit(solution)/shard_map/all_to_all | solution.py:362
  109.7 0.8 unpack.1
  (31 shorter events, 1.0 us)
Async XLA Ops:
  0.1 1.7 %copy-start = (bf16[1536,768]{1,0:T(8,128)(2,1)S(1)}, bf16[1536,768]{1,0:T(8,128)(2,1)}, u32[]{:S(2)}) copy-start(bf16[1536,768]{1,0:T(8,128)(2,1)} %emb_ref.1) | copy-start | bytes 7077892
  1.7 0.7 copy-start.1
  2.4 0.7 copy-start.2
  7.6 10.3 %collective-permute-start.2 = (bf16[1,200,768]{2,1,0:T(8,128)(2,1)S(1)}, bf16[1,200,768]{2,1,0:T(8,128)(2,1)S(1)}, u32[]{:S(2)}, u32[]{:S(2)}) collective-permute-start(bf16[1,200,768]{2,1,0:T(8,128)(2,1)S(1)} %bitcast.6), channel_id=1, source_target_pairs={{0,2},{1,3},{2,0},{3,1},{4,6},{5,7},{6,4},{7,5},{8,10},{9,11},{10,... | collective-permute-start | bytes 921608 | tf_op jit(solution)/shard_map/ppermute | solution.py:233
  10.7 7.3 %collective-permute-start.3 = (bf16[1,200,768]{2,1,0:T(8,128)(2,1)S(1)}, bf16[1,200,768]{2,1,0:T(8,128)(2,1)S(1)}, u32[]{:S(2)}, u32[]{:S(2)}) collective-permute-start(bf16[1,200,768]{2,1,0:T(8,128)(2,1)S(1)} %bitcast.7), channel_id=1, source_target_pairs={{0,1},{1,0},{2,3},{3,2},{4,5},{5,4},{6,7},{7,6},{8,9},{9,8},{10,11... | collective-permute-start | bytes 921608 | tf_op jit(solution)/shard_map/ppermute | solution.py:233
  10.7 17.7 %collective-permute-start = (bf16[208,768]{1,0:T(8,128)(2,1)S(1)}, bf16[208,768]{1,0:T(8,128)(2,1)S(1)}, u32[]{:S(2)}, u32[]{:S(2)}) collective-permute-start(bf16[208,768]{1,0:T(8,128)(2,1)S(1)} %get-tuple-element.58), channel_id=1, source_target_pairs={{0,16},{4,20},{8,24},{12,28},{16,0},{20,4},{24,8},{28,12},{1,17},{... | collective-permute-start | bytes 958472 | tf_op jit(solution)/shard_map/ppermute | solution.py:233
  13.2 9.4 %collective-permute-start.1 = (bf16[200,768]{1,0:T(8,128)(2,1)S(1)}, bf16[200,768]{1,0:T(8,128)(2,1)S(1)}, u32[]{:S(2)}, u32[]{:S(2)}) collective-permute-start(bf16[200,768]{1,0:T(8,128)(2,1)S(1)} %get-tuple-element.59), channel_id=1, source_target_pairs={{0,4},{4,0},{8,12},{12,8},{16,20},{20,16},{24,28},{28,24},{1,5},{5... | collective-permute-start | bytes 921608 | tf_op jit(solution)/shard_map/ppermute | solution.py:233
  28.4 19.6 %collective-permute-start.6 = (bf16[2,200,768]{2,1,0:T(8,128)(2,1)S(1)}, bf16[2,200,768]{2,1,0:T(8,128)(2,1)S(1)}, u32[]{:S(2)}, u32[]{:S(2)}) collective-permute-start(bf16[2,200,768]{2,1,0:T(8,128)(2,1)S(1)} %get-tuple-element.69.rest_4_), channel_id=1, source_target_pairs={{0,2},{1,3},{2,0},{3,1},{4,6},{5,7},{6,4},{7,5},{8,10},{9,11},{10,... | collective-permute-start | bytes 1843208 | tf_op jit(solution)/shard_map/ppermute | solution.py:233
  28.9 19.1 %collective-permute-start.7 = (bf16[2,200,768]{2,1,0:T(8,128)(2,1)S(1)}, bf16[2,200,768]{2,1,0:T(8,128)(2,1)S(1)}, u32[]{:S(2)}, u32[]{:S(2)}) collective-permute-start(bf16[2,200,768]{2,1,0:T(8,128)(2,1)S(1)} %get-tuple-element.69.rest_4_), channel_id=1, source_target_pairs={{0,1},{1,0},{2,3},{3,2},{4,5},{5,4},{6,7},{7,6},{8,9},{9,8},{10,11... | collective-permute-start | bytes 1843208 | tf_op jit(solution)/shard_map/ppermute | solution.py:233
  28.9 18.2 %collective-permute-start.4 = (bf16[200,768]{1,0:T(8,128)(2,1)S(1)}, bf16[200,768]{1,0:T(8,128)(2,1)S(1)}, u32[]{:S(2)}, u32[]{:S(2)}) collective-permute-start(bf16[200,768]{1,0:T(8,128)(2,1)S(1)} %get-tuple-element.66), channel_id=1, source_target_pairs={{0,20},{4,16},{8,28},{12,24},{16,4},{20,0},{24,12},{28,8},{1,21},{... | collective-permute-start | bytes 921608 | tf_op jit(solution)/shard_map/ppermute | solution.py:233
  29.4 18.5 %collective-permute-start.5 = (bf16[200,768]{1,0:T(8,128)(2,1)S(1)}, bf16[200,768]{1,0:T(8,128)(2,1)S(1)}, u32[]{:S(2)}, u32[]{:S(2)}) collective-permute-start(bf16[200,768]{1,0:T(8,128)(2,1)S(1)} %get-tuple-element.67), channel_id=1, source_target_pairs={{0,8},{4,12},{8,0},{12,4},{16,24},{20,28},{24,16},{28,20},{1,9},{5... | collective-permute-start | bytes 921608 | tf_op jit(solution)/shard_map/ppermute | solution.py:233
  33.9 14.0 %collective-permute-start.8 = (bf16[1,200,768]{2,1,0:T(8,128)(2,1)S(1)}, bf16[1,200,768]{2,1,0:T(8,128)(2,1)S(1)}, u32[]{:S(2)}, u32[]{:S(2)}) collective-permute-start(bf16[1,200,768]{2,1,0:T(8,128)(2,1)S(1)} %get-tuple-element.70.rest_2_), channel_id=1, source_target_pairs={{0,1},{1,0},{2,3},{3,2},{4,5},{5,4},{6,7},{7,6},{8,9},{9,8},{10,11... | collective-permute-start | bytes 921608 | tf_op jit(solution)/shard_map/ppermute | solution.py:233
  48.0 19.7 %collective-permute-start.11 = (bf16[2,200,768]{2,1,0:T(8,128)(2,1)S(1)}, bf16[2,200,768]{2,1,0:T(8,128)(2,1)S(1)}, u32[]{:S(2)}, u32[]{:S(2)}) collective-permute-start(bf16[2,200,768]{2,1,0:T(8,128)(2,1)S(1)} %get-tuple-element.76.rest_8_), channel_id=1, source_target_pairs={{0,2},{1,3},{2,0},{3,1},{4,6},{5,7},{6,4},{7,5},{8,10},{9,11},{10,... | collective-permute-start | bytes 1843208 | tf_op jit(solution)/shard_map/ppermute | solution.py:233
  49.6 18.2 %collective-permute-start.12 = (bf16[2,200,768]{2,1,0:T(8,128)(2,1)S(1)}, bf16[2,200,768]{2,1,0:T(8,128)(2,1)S(1)}, u32[]{:S(2)}, u32[]{:S(2)}) collective-permute-start(bf16[2,200,768]{2,1,0:T(8,128)(2,1)S(1)} %get-tuple-element.76.rest_8_), channel_id=1, source_target_pairs={{0,1},{1,0},{2,3},{3,2},{4,5},{5,4},{6,7},{7,6},{8,9},{9,8},{10,11... | collective-permute-start | bytes 1843208 | tf_op jit(solution)/shard_map/ppermute | solution.py:233
  49.6 18.2 %collective-permute-start.13 = (bf16[2,200,768]{2,1,0:T(8,128)(2,1)S(1)}, bf16[2,200,768]{2,1,0:T(8,128)(2,1)S(1)}, u32[]{:S(2)}, u32[]{:S(2)}) collective-permute-start(bf16[2,200,768]{2,1,0:T(8,128)(2,1)S(1)} %get-tuple-element.77.rest_6_), channel_id=1, source_target_pairs={{0,1},{1,0},{2,3},{3,2},{4,5},{5,4},{6,7},{7,6},{8,9},{9,8},{10,11... | collective-permute-start | bytes 1843208 | tf_op jit(solution)/shard_map/ppermute | solution.py:233
  50.1 17.6 %collective-permute-start.9 = (bf16[208,768]{1,0:T(8,128)(2,1)S(1)}, bf16[208,768]{1,0:T(8,128)(2,1)S(1)}, u32[]{:S(2)}, u32[]{:S(2)}) collective-permute-start(bf16[208,768]{1,0:T(8,128)(2,1)S(1)} %get-tuple-element.73), channel_id=1, source_target_pairs={{0,24},{4,28},{8,16},{12,20},{16,8},{20,12},{24,0},{28,4},{1,25},{... | collective-permute-start | bytes 958472 | tf_op jit(solution)/shard_map/ppermute | solution.py:233
  51.1 16.6 %collective-permute-start.10 = (bf16[200,768]{1,0:T(8,128)(2,1)S(1)}, bf16[200,768]{1,0:T(8,128)(2,1)S(1)}, u32[]{:S(2)}, u32[]{:S(2)}) collective-permute-start(bf16[200,768]{1,0:T(8,128)(2,1)S(1)} %get-tuple-element.74), channel_id=1, source_target_pairs={{0,12},{4,8},{8,4},{12,0},{16,28},{20,24},{24,20},{28,16},{1,13},{... | collective-permute-start | bytes 921608 | tf_op jit(solution)/shard_map/ppermute | solution.py:233
  67.8 3.0 %collective-permute-start.15 = (bf16[2,200,768]{2,1,0:T(8,128)(2,1)S(1)}, bf16[2,200,768]{2,1,0:T(8,128)(2,1)S(1)}, u32[]{:S(2)}, u32[]{:S(2)}) collective-permute-start(bf16[2,200,768]{2,1,0:T(8,128)(2,1)S(1)} %get-tuple-element.86.rest_10_), channel_id=1, source_target_pairs={{0,1},{1,0},{2,3},{3,2},{4,5},{5,4},{6,7},{7,6},{8,9},{9,8},{10,11... | collective-permute-start | bytes 1843208 | tf_op jit(solution)/shard_map/ppermute | solution.py:233
  67.9 16.3 %collective-permute-start.16 = (bf16[2,200,768]{2,1,0:T(8,128)(2,1)S(1)}, bf16[2,200,768]{2,1,0:T(8,128)(2,1)S(1)}, u32[]{:S(2)}, u32[]{:S(2)}) collective-permute-start(bf16[2,200,768]{2,1,0:T(8,128)(2,1)S(1)} %get-tuple-element.88.rest_0_), channel_id=1, source_target_pairs={{0,2},{1,3},{2,0},{3,1},{4,6},{5,7},{6,4},{7,5},{8,10},{9,11},{10,... | collective-permute-start | bytes 1843208 | tf_op jit(solution)/shard_map/ppermute | solution.py:233
  68.5 15.7 %collective-permute-start.17 = (bf16[2,200,768]{2,1,0:T(8,128)(2,1)S(1)}, bf16[2,200,768]{2,1,0:T(8,128)(2,1)S(1)}, u32[]{:S(2)}, u32[]{:S(2)}) collective-permute-start(bf16[2,200,768]{2,1,0:T(8,128)(2,1)S(1)} %get-tuple-element.88.rest_0_), channel_id=1, source_target_pairs={{0,1},{1,0},{2,3},{3,2},{4,5},{5,4},{6,7},{7,6},{8,9},{9,8},{10,11... | collective-permute-start | bytes 1843208 | tf_op jit(solution)/shard_map/ppermute | solution.py:233
  68.6 12.3 %collective-permute-start.14 = (bf16[200,768]{1,0:T(8,128)(2,1)S(1)}, bf16[200,768]{1,0:T(8,128)(2,1)S(1)}, u32[]{:S(2)}, u32[]{:S(2)}) collective-permute-start(bf16[200,768]{1,0:T(8,128)(2,1)S(1)} %get-tuple-element.79), channel_id=1, source_target_pairs={{0,28},{4,24},{8,20},{12,16},{16,12},{20,8},{24,4},{28,0},{1,29},{... | collective-permute-start | bytes 921608 | tf_op jit(solution)/shard_map/ppermute | solution.py:233
  84.2 2.1 %collective-permute-start.18 = (bf16[2,200,768]{2,1,0:T(8,128)(2,1)S(1)}, bf16[2,200,768]{2,1,0:T(8,128)(2,1)S(1)}, u32[]{:S(2)}, u32[]{:S(2)}) collective-permute-start(bf16[2,200,768]{2,1,0:T(8,128)(2,1)S(1)} %get-tuple-element.91.rest_2_), channel_id=1, source_target_pairs={{0,1},{1,0},{2,3},{3,2},{4,5},{5,4},{6,7},{7,6},{8,9},{9,8},{10,11... | collective-permute-start | bytes 1843208 | tf_op jit(solution)/shard_map/ppermute | solution.py:233
  84.3 9.7 %collective-permute-start.19 = (bf16[1,200,768]{2,1,0:T(8,128)(2,1)S(1)}, bf16[1,200,768]{2,1,0:T(8,128)(2,1)S(1)}, u32[]{:S(2)}, u32[]{:S(2)}) collective-permute-start(bf16[1,200,768]{2,1,0:T(8,128)(2,1)S(1)} %get-tuple-element.98.rest_0_), channel_id=1, source_target_pairs={{0,2},{1,3},{2,0},{3,1},{4,6},{5,7},{6,4},{7,5},{8,10},{9,11},{10,... | collective-permute-start | bytes 921608 | tf_op jit(solution)/shard_map/ppermute | solution.py:233
  84.9 9.1 %collective-permute-start.20 = (bf16[1,200,768]{2,1,0:T(8,128)(2,1)S(1)}, bf16[1,200,768]{2,1,0:T(8,128)(2,1)S(1)}, u32[]{:S(2)}, u32[]{:S(2)}) collective-permute-start(bf16[1,200,768]{2,1,0:T(8,128)(2,1)S(1)} %get-tuple-element.98.rest_0_), channel_id=1, source_target_pairs={{0,1},{1,0},{2,3},{3,2},{4,5},{5,4},{6,7},{7,6},{8,9},{9,8},{10,11... | collective-permute-start | bytes 921608 | tf_op jit(solution)/shard_map/ppermute | solution.py:233
  94.0 1.6 %collective-permute-start.21 = (bf16[1,200,768]{2,1,0:T(8,128)(2,1)S(1)}, bf16[1,200,768]{2,1,0:T(8,128)(2,1)S(1)}, u32[]{:S(2)}, u32[]{:S(2)}) collective-permute-start(bf16[1,200,768]{2,1,0:T(8,128)(2,1)S(1)} %get-tuple-element.100.rest_2_), channel_id=1, source_target_pairs={{0,1},{1,0},{2,3},{3,2},{4,5},{5,4},{6,7},{7,6},{8,9},{9,8},{10,11... | collective-permute-start | bytes 921608 | tf_op jit(solution)/shard_map/ppermute | solution.py:233

commit v6 on v5

--- a/solution.py
+++ b/solution.py
@@ -252,9 +252,9 @@
     wide = -(-piece // LANES) * LANES
     one_piece = shape(piece + NOTE, width, kind=BF16)
     longer = shape(piece + 2 * NOTE, width, kind=BF16)
-    kind_of = {d: longer if n == 8 and d in (4, 6) else one_piece for d in range(n)}
-
-    early = [half, 0, 1]
+    kind_of = {d: longer if n == 8 and d in (2, 4, 6) else one_piece for d in range(n)}
+
+    early = [half, 2]
     late = [d for d in range(n) if d not in early]
     fam, rank, note, unit, *packed = pl.pallas_call(
         functools.partial(first_kernel, n, piece, rows * nb, early),
@@ -332,22 +332,22 @@
         seen = now
 
     if n == 8:
-        to_columns(4, 1)
+        to_columns(4, 2)
         m0 = own[0].reshape(1, *one_piece.shape)
         y0, c0 = send(m0, "blk", 2), send(m0, "blk", 1)
-        m1, y0, c0, sent[5], sent[2] = join((4, 1), [y0, c0, sent[5], sent[2]])
-        to_columns(5, 2)
+        m1, y0, c0, sent[5], sent[3] = join((4, 2), [y0, c0, sent[5], sent[3]])
+        to_columns(5, 3)
         y1, c1, x0 = send(m1, "blk", 2), send(m1, "blk", 1), send(y0, "blk", 1)
-        m2, y1, c1, x0, sent[6], sent[3] = join((5, 2), [y1, c1, x0, sent[6], sent[3]])
-        to_columns(6, 3)
+        m2, y1, c1, x0, sent[6], sent[1] = join((5, 3), [y1, c1, x0, sent[6], sent[1]])
+        to_columns(6, 1)
         y2, c2, x1 = send(m2, "blk", 2), send(m2, "blk", 1), send(y1, "blk", 1)
-        m3, y2, c2, x1, sent[7] = join((6, 3), [y2, c2, x1, sent[7]])
+        m3, y2, c2, x1, sent[7] = join((6, 1), [y2, c2, x1, sent[7]])
         to_columns(7)
         y3, c3, x2 = send(m3, "blk", 2), send(m3, "blk", 1), send(y2, "blk", 1)
-        stage(((0,), m0, c0, y0, x0), ((4, 1), m1, c1, y1, x1), ((5, 2), m2, c2, y2, x2))
+        stage(((0,), m0, c0, y0, x0), ((4, 2), m1, c1, y1, x1), ((5, 3), m2, c2, y2, x2))
         m4, y3, c3 = join((7,), [y3, c3])
         y4, c4, x3 = send(m4, "blk", 2), send(m4, "blk", 1), send(y3, "blk", 1)
-        stage(((6, 3), m3, c3, y3, x3))
+        stage(((6, 1), m3, c3, y3, x3))
         (y4,) = join((), [y4])
         stage(((7,), m4, c4, y4, send(y4, "blk", 1)))
     else:

time: 111 us -> 107 us (0.964)
  waiting for transfers between devices: 53.3 us -> 43 us
  starting transfers between devices: 19.7 us -> 23.7 us
  blocking collectives: 10.8 us -> 13.4 us
    ppermute x22, waiting for transfers between devices: 53.3 us -> 43 us  [send(): lax.ppermute(x, axis, [(i, i ^ by) for i in range(lax.axis_size(axis))])]
    ppermute x22, starting transfers between devices: 19.7 us -> 23.7 us  [send(): lax.ppermute(x, axis, [(i, i ^ by) for i in range(lax.axis_size(axis))])]
    all_to_all x1, blocking collectives: 10.8 us -> 13.4 us  [on_device(): lax.all_to_all(scores, 'grp', split_axis=0, concat_axis=0, tiled=True)]
  transfers between devices with their start and end apart: 22 -> 22, of which waited for: 11 -> 11; matrix products, arithmetic and copies ran while one was open for 0% -> 0% of each run, Pallas kernels for 13% -> 14%
where the time goes in v6:
time: 107 us
  waiting for transfers between devices  43 us (40%)
  starting transfers between devices  23.7 us (22%)
  Pallas kernels  23.3 us (22%)
  blocking collectives  13.4 us (13%)
  local copies, waits for them, and re-layouts  3.05 us (3%)
    ppermute x22, waiting for transfers between devices, send(): lax.ppermute(x, axis, [(i, i ^ by) for i in range(lax.axis_size(axis))])  43 us
    ppermute x22, starting transfers between devices, send(): lax.ppermute(x, axis, [(i, i ^ by) for i in range(lax.axis_size(axis))])  23.7 us
    pallas_call x3, Pallas kernels, stage(): pl.pallas_call(functools.partial(stage_kernel, n, nb, piece, seen, ds), o...  15 us
    all_to_all x1, blocking collectives, on_device(): lax.all_to_all(scores, 'grp', split_axis=0, concat_axis=0, tiled=True)  13.4 us
    pallas_call x1, Pallas kernels, on_device(): pl.pallas_call(functools.partial(first_kernel, n, piece, rows * nb, early...  3.84 us
    pallas_call x1, Pallas kernels, on_device(): pl.pallas_call(functools.partial(second_kernel, n, piece, late), out_shap...  3.5 us
    unnamed x6, local copies, waits for them, and re-layouts  3.05 us
  transfers between devices with their start and end apart: 22, of which 11 were waited for; matrix products, arithmetic and copies ran while one was open for 0% of the time, Pallas kernels for 14%

profile of v6, /device:TPU:0, one launch (start us, length us, event | category | flops | bytes accessed | tf_op | source)
XLA Modules:
  0.0 106.7 jit_solution(4475327345389030756)
XLA Ops:
  0.1 1.7 %copy-done = bf16[1536,768]{1,0:T(8,128)(2,1)S(1)} copy-done((bf16[1536,768]{1,0:T(8,128)(2,1)S(1)}, bf16[1536,768]{1,0:T(8,128)(2,1)}, u32[]{:S(2)}) %copy-start) | copy-done | bytes 2359320
  1.7 0.7 copy-done.1
  2.4 0.7 copy-done.2
  3.1 3.8 %first.1 = (s32[1,1536]{1,0:T(1,128)S(1)}, s32[1,1536]{1,0:T(1,128)S(1)}, f32[8,8,256]{2,1,0:T(8,128)S(1)}, bf16[1536,768]{1,0:T(8,128)(2,1)S(1)}, bf16[208,768]...) custom-call(s32[2]{0:T(128)S(1)} %pad_add_fusion.here_ref, s32[12,128]{1,0:T(8,128)S(1)} %bitcast.5, ...), custom_call_target="tpu_custom_call" | custom-call | tf_op jit(solution)/shard_map/first/pallas_call | solution.py:259
  7.0 4.1 %collective-permute-start = (bf16[208,768]{1,0:T(8,128)(2,1)S(1)}, bf16[208,768]{1,0:T(8,128)(2,1)S(1)}, u32[]{:S(2)}, u32[]{:S(2)}) collective-permute-start(bf16[208,768]{1,0:T(8,128)(2,1)S(1)} %get-tuple-element.58), channel_id=1, source_target_pairs={{0,16},{4,20},{8,24},{12,28},{16,0},{20,4},{24,8},{28,12},{1,17},{... | collective-permute-start | bytes 958472 | tf_op jit(solution)/shard_map/ppermute | solution.py:233
  11.1 1.6 %collective-permute-start.1 = (bf16[208,768]{1,0:T(8,128)(2,1)S(1)}, bf16[208,768]{1,0:T(8,128)(2,1)S(1)}, u32[]{:S(2)}, u32[]{:S(2)}) collective-permute-start(bf16[208,768]{1,0:T(8,128)(2,1)S(1)} %get-tuple-element.59), channel_id=1, source_target_pairs={{0,8},{4,12},{8,0},{12,4},{16,24},{20,28},{24,16},{28,20},{1,9},{5... | collective-permute-start | bytes 958472 | tf_op jit(solution)/shard_map/ppermute | solution.py:233
  12.7 3.5 %second.1 = (bf16[200,768]{1,0:T(8,128)(2,1)S(1)}, bf16[200,768]{1,0:T(8,128)(2,1)S(1)}, bf16[200,768]{1,0:T(8,128)(2,1)S(1)}, bf16[200,768]{1,0:T(8,128)(2,1)S(...) custom-call(s32[2]{0:T(128)S(1)} %pad_add_fusion.here_ref, ...), custom_call_target="tpu_custom_call" | custom-call | flops 14495514624 | tf_op jit(solution)/shard_map/second/pallas_call | solution.py:269
  16.2 1.6 %collective-permute-start.2 = (bf16[1,200,768]{2,1,0:T(8,128)(2,1)S(1)}, bf16[1,200,768]{2,1,0:T(8,128)(2,1)S(1)}, u32[]{:S(2)}, u32[]{:S(2)}) collective-permute-start(bf16[1,200,768]{2,1,0:T(8,128)(2,1)S(1)} %bitcast.6), channel_id=1, source_target_pairs={{0,2},{1,3},{2,0},{3,1},{4,6},{5,7},{6,4},{7,5},{8,10},{9,11},{10,... | collective-permute-start | bytes 921608 | tf_op jit(solution)/shard_map/ppermute | solution.py:233
  17.7 6.9 %collective-permute-done.2.refs_3_ = bf16[1,200,768]{2,1,0:T(8,128)(2,1)S(1)} collective-permute-done((bf16[1,200,768]{2,1,0:T(8,128)(2,1)S(1)}, bf16[1,200,768]{2,1,0:T(8,128)(2,1)S(1)}, u32[]{:S(2)}, u32[]{:S(2)}) %collective-permute-start.2) | collective-permute-done | bytes 307232 | tf_op jit(solution)/shard_map/ppermute | solution.py:233
  24.7 0.9 collective-permute-done.refs_0_
  25.8 1.6 %collective-permute-start.6 = (bf16[2,200,768]{2,1,0:T(8,128)(2,1)S(1)}, bf16[2,200,768]{2,1,0:T(8,128)(2,1)S(1)}, u32[]{:S(2)}, u32[]{:S(2)}) collective-permute-start(bf16[2,200,768]{2,1,0:T(8,128)(2,1)S(1)} %get-tuple-element.69.rest_4_), channel_id=1, source_target_pairs={{0,2},{1,3},{2,0},{3,1},{4,6},{5,7},{6,4},{7,5},{8,10},{9,11},{10,... | collective-permute-start | bytes 1843208 | tf_op jit(solution)/shard_map/ppermute | solution.py:233
  27.4 2.3 %collective-permute-start.4 = (bf16[200,768]{1,0:T(8,128)(2,1)S(1)}, bf16[200,768]{1,0:T(8,128)(2,1)S(1)}, u32[]{:S(2)}, u32[]{:S(2)}) collective-permute-start(bf16[200,768]{1,0:T(8,128)(2,1)S(1)} %get-tuple-element.66), channel_id=1, source_target_pairs={{0,20},{4,16},{8,28},{12,24},{16,4},{20,0},{24,12},{28,8},{1,21},{... | collective-permute-start | bytes 921608 | tf_op jit(solution)/shard_map/ppermute | solution.py:233
  29.7 2.4 %collective-permute-start.5 = (bf16[200,768]{1,0:T(8,128)(2,1)S(1)}, bf16[200,768]{1,0:T(8,128)(2,1)S(1)}, u32[]{:S(2)}, u32[]{:S(2)}) collective-permute-start(bf16[200,768]{1,0:T(8,128)(2,1)S(1)} %get-tuple-element.67), channel_id=1, source_target_pairs={{0,12},{4,8},{8,4},{12,0},{16,28},{20,24},{24,20},{28,16},{1,13},{... | collective-permute-start | bytes 921608 | tf_op jit(solution)/shard_map/ppermute | solution.py:233
  32.1 13.5 %collective-permute-done.4.refs_0_ = bf16[200,768]{1,0:T(8,128)(2,1)S(1)} collective-permute-done((bf16[200,768]{1,0:T(8,128)(2,1)S(1)}, bf16[200,768]{1,0:T(8,128)(2,1)S(1)}, u32[]{:S(2)}, u32[]{:S(2)}) %collective-permute-start.4) | collective-permute-done | bytes 307232 | tf_op jit(solution)/shard_map/ppermute | solution.py:233
  45.7 0.5 collective-permute-start.11
  46.7 3.5 %collective-permute-start.9 = (bf16[208,768]{1,0:T(8,128)(2,1)S(1)}, bf16[208,768]{1,0:T(8,128)(2,1)S(1)}, u32[]{:S(2)}, u32[]{:S(2)}) collective-permute-start(bf16[208,768]{1,0:T(8,128)(2,1)S(1)} %get-tuple-element.73), channel_id=1, source_target_pairs={{0,24},{4,28},{8,16},{12,20},{16,8},{20,12},{24,0},{28,4},{1,25},{... | collective-permute-start | bytes 958472 | tf_op jit(solution)/shard_map/ppermute | solution.py:233
  50.2 0.6 collective-permute-start.10
  50.7 8.3 %collective-permute-done.10.refs_1_ = bf16[200,768]{1,0:T(8,128)(2,1)S(1)} collective-permute-done((bf16[200,768]{1,0:T(8,128)(2,1)S(1)}, bf16[200,768]{1,0:T(8,128)(2,1)S(1)}, u32[]{:S(2)}, u32[]{:S(2)}) %collective-permute-start.10) | collective-permute-done | bytes 307232 | tf_op jit(solution)/shard_map/ppermute | solution.py:233
  59.1 2.1 %collective-permute-done.11.refs_3_ = bf16[2,200,768]{2,1,0:T(8,128)(2,1)S(1)} collective-permute-done((bf16[2,200,768]{2,1,0:T(8,128)(2,1)S(1)}, bf16[2,200,768]{2,1,0:T(8,128)(2,1)S(1)}, u32[]{:S(2)}, u32[]{:S(2)}) %collective-permute-start.11) | collective-permute-done | bytes 614432 | tf_op jit(solution)/shard_map/ppermute | solution.py:233
  61.3 0.5 collective-permute-start.16
  62.0 3.5 %collective-permute-start.14 = (bf16[200,768]{1,0:T(8,128)(2,1)S(1)}, bf16[200,768]{1,0:T(8,128)(2,1)S(1)}, u32[]{:S(2)}, u32[]{:S(2)}) collective-permute-start(bf16[200,768]{1,0:T(8,128)(2,1)S(1)} %get-tuple-element.79), channel_id=1, source_target_pairs={{0,28},{4,24},{8,20},{12,16},{16,12},{20,8},{24,4},{28,0},{1,29},{... | collective-permute-start | bytes 921608 | tf_op jit(solution)/shard_map/ppermute | solution.py:233
  65.5 6.4 %stage.3 = (f32[8,128]{1,0:T(8,128)S(1)}, bf16[8,4,192,768]{3,2,1,0:T(8,128)(2,1)S(1)}, f32[8,8,192]{2,1,0:T(8,128)S(1)}, f32[32,192,128]{2,1,0:T(8,128)S(1)}, f...) custom-call(s32[2]{0:T(128)S(1)} %pad_add_fusion.here_ref, ...), custom_call_target="tpu_custom_call", output_to_operand_aliasing={{0}: (1, {})} | custom-call | flops 6794772480 | tf_op jit(solution)/shard_map/stage/pallas_call | solution.py:322
  71.9 2.4 %collective-permute-done.14.refs_0_ = bf16[200,768]{1,0:T(8,128)(2,1)S(1)} collective-permute-done((bf16[200,768]{1,0:T(8,128)(2,1)S(1)}, bf16[200,768]{1,0:T(8,128)(2,1)S(1)}, u32[]{:S(2)}, u32[]{:S(2)}) %collective-permute-start.14) | collective-permute-done | bytes 307232 | tf_op jit(solution)/shard_map/ppermute | solution.py:233
  74.3 3.3 %collective-permute-done.16.refs_2_ = bf16[2,200,768]{2,1,0:T(8,128)(2,1)S(1)} collective-permute-done((bf16[2,200,768]{2,1,0:T(8,128)(2,1)S(1)}, bf16[2,200,768]{2,1,0:T(8,128)(2,1)S(1)}, u32[]{:S(2)}, u32[]{:S(2)}) %collective-permute-start.16) | collective-permute-done | bytes 614432 | tf_op jit(solution)/shard_map/ppermute | solution.py:233
  77.7 0.5 collective-permute-start.19
  78.4 1.3 %collective-permute-done.18.rest_3_ = bf16[2,200,768]{2,1,0:T(8,128)(2,1)S(1)} collective-permute-done((bf16[2,200,768]{2,1,0:T(8,128)(2,1)S(1)}, bf16[2,200,768]{2,1,0:T(8,128)(2,1)S(1)}, u32[]{:S(2)}, u32[]{:S(2)}) %collective-permute-start.18) | collective-permute-done | bytes 614432 | tf_op jit(solution)/shard_map/ppermute | solution.py:233
  79.7 5.2 %stage.4 = (f32[8,128]{1,0:T(8,128)S(1)}, bf16[8,4,192,768]{3,2,1,0:T(8,128)(2,1)S(1)}, f32[8,8,192]{2,1,0:T(8,128)S(1)}, f32[32,192,128]{2,1,0:T(8,128)S(1)}, f...) custom-call(s32[2]{0:T(128)S(1)} %pad_add_fusion.here_ref, ...), custom_call_target="tpu_custom_call", output_to_operand_aliasing={{0}: (1, {}), {1}: (6, {}), {2}: (7, {}), {3}: (8, {}), {4}... | custom-call | flops 5888802816 | tf_op jit(solution)/shard_map/stage/pallas_call | solution.py:322
  85.0 2.4 %collective-permute-done.19.refs_1_ = bf16[1,200,768]{2,1,0:T(8,128)(2,1)S(1)} collective-permute-done((bf16[1,200,768]{2,1,0:T(8,128)(2,1)S(1)}, bf16[1,200,768]{2,1,0:T(8,128)(2,1)S(1)}, u32[]{:S(2)}, u32[]{:S(2)}) %collective-permute-start.19) | collective-permute-done | bytes 307232 | tf_op jit(solution)/shard_map/ppermute | solution.py:233
  87.4 1.6 %collective-permute-done.21.rest_3_ = bf16[1,200,768]{2,1,0:T(8,128)(2,1)S(1)} collective-permute-done((bf16[1,200,768]{2,1,0:T(8,128)(2,1)S(1)}, bf16[1,200,768]{2,1,0:T(8,128)(2,1)S(1)}, u32[]{:S(2)}, u32[]{:S(2)}) %collective-permute-start.21) | collective-permute-done | bytes 307232 | tf_op jit(solution)/shard_map/ppermute | solution.py:233
  89.0 3.4 %stage.5 = (f32[8,128]{1,0:T(8,128)S(1)}, f32[8,1,192]{2,1,0:T(1,128)S(1)}, bf16[8,4,192,768]{3,2,1,0:T(8,128)(2,1)S(1)}, f32[8,8,192]{2,1,0:T(8,128)S(1)}, f32[...) custom-call(s32[2]{0:T(128)S(1)} %pad_add_fusion.here_ref, ...), custom_call_target="tpu_custom_call", output_to_operand_aliasing={{0}: (1, {}), {2}: (6, {}), {3}: (7, {}), {4}: (8, {}), {5}... | custom-call | flops 3623878656 | tf_op jit(solution)/shard_map/stage/pallas_call | solution.py:322
  92.4 13.4 %all_to_all.5.score_ref = f32[8,1,192]{2,1,0:T(1,128)S(1)} all-to-all(f32[8,1,192]{2,1,0:T(1,128)S(1)} %get-tuple-element.106), channel_id=1, replica_groups=mesh['grp'=8,'blk'=4] {'grp'}, dimensions={0} | all-to-all | bytes 12288 | tf_op jit(solution)/shard_map/all_to_all | solution.py:362
  105.8 0.8 unpack.1
  (31 shorter events, 1.4 us)
Async XLA Ops:
  0.1 1.7 %copy-start = (bf16[1536,768]{1,0:T(8,128)(2,1)S(1)}, bf16[1536,768]{1,0:T(8,128)(2,1)}, u32[]{:S(2)}) copy-start(bf16[1536,768]{1,0:T(8,128)(2,1)} %emb_ref.1) | copy-start | bytes 7077892
  1.7 0.7 copy-start.1
  2.4 0.7 copy-start.2
  7.0 18.6 %collective-permute-start = (bf16[208,768]{1,0:T(8,128)(2,1)S(1)}, bf16[208,768]{1,0:T(8,128)(2,1)S(1)}, u32[]{:S(2)}, u32[]{:S(2)}) collective-permute-start(bf16[208,768]{1,0:T(8,128)(2,1)S(1)} %get-tuple-element.58), channel_id=1, source_target_pairs={{0,16},{4,20},{8,24},{12,28},{16,0},{20,4},{24,8},{28,12},{1,17},{... | collective-permute-start | bytes 958472 | tf_op jit(solution)/shard_map/ppermute | solution.py:233
  11.1 14.7 %collective-permute-start.1 = (bf16[208,768]{1,0:T(8,128)(2,1)S(1)}, bf16[208,768]{1,0:T(8,128)(2,1)S(1)}, u32[]{:S(2)}, u32[]{:S(2)}) collective-permute-start(bf16[208,768]{1,0:T(8,128)(2,1)S(1)} %get-tuple-element.59), channel_id=1, source_target_pairs={{0,8},{4,12},{8,0},{12,4},{16,24},{20,28},{24,16},{28,20},{1,9},{5... | collective-permute-start | bytes 958472 | tf_op jit(solution)/shard_map/ppermute | solution.py:233
  16.2 8.5 %collective-permute-start.2 = (bf16[1,200,768]{2,1,0:T(8,128)(2,1)S(1)}, bf16[1,200,768]{2,1,0:T(8,128)(2,1)S(1)}, u32[]{:S(2)}, u32[]{:S(2)}) collective-permute-start(bf16[1,200,768]{2,1,0:T(8,128)(2,1)S(1)} %bitcast.6), channel_id=1, source_target_pairs={{0,2},{1,3},{2,0},{3,1},{4,6},{5,7},{6,4},{7,5},{8,10},{9,11},{10,... | collective-permute-start | bytes 921608 | tf_op jit(solution)/shard_map/ppermute | solution.py:233
  17.7 6.9 %collective-permute-start.3 = (bf16[1,200,768]{2,1,0:T(8,128)(2,1)S(1)}, bf16[1,200,768]{2,1,0:T(8,128)(2,1)S(1)}, u32[]{:S(2)}, u32[]{:S(2)}) collective-permute-start(bf16[1,200,768]{2,1,0:T(8,128)(2,1)S(1)} %bitcast.7), channel_id=1, source_target_pairs={{0,1},{1,0},{2,3},{3,2},{4,5},{5,4},{6,7},{7,6},{8,9},{9,8},{10,11... | collective-permute-start | bytes 921608 | tf_op jit(solution)/shard_map/ppermute | solution.py:233
  25.8 19.8 %collective-permute-start.6 = (bf16[2,200,768]{2,1,0:T(8,128)(2,1)S(1)}, bf16[2,200,768]{2,1,0:T(8,128)(2,1)S(1)}, u32[]{:S(2)}, u32[]{:S(2)}) collective-permute-start(bf16[2,200,768]{2,1,0:T(8,128)(2,1)S(1)} %get-tuple-element.69.rest_4_), channel_id=1, source_target_pairs={{0,2},{1,3},{2,0},{3,1},{4,6},{5,7},{6,4},{7,5},{8,10},{9,11},{10,... | collective-permute-start | bytes 1843208 | tf_op jit(solution)/shard_map/ppermute | solution.py:233
  27.4 18.2 %collective-permute-start.7 = (bf16[2,200,768]{2,1,0:T(8,128)(2,1)S(1)}, bf16[2,200,768]{2,1,0:T(8,128)(2,1)S(1)}, u32[]{:S(2)}, u32[]{:S(2)}) collective-permute-start(bf16[2,200,768]{2,1,0:T(8,128)(2,1)S(1)} %get-tuple-element.69.rest_4_), channel_id=1, source_target_pairs={{0,1},{1,0},{2,3},{3,2},{4,5},{5,4},{6,7},{7,6},{8,9},{9,8},{10,11... | collective-permute-start | bytes 1843208 | tf_op jit(solution)/shard_map/ppermute | solution.py:233
  27.4 18.2 %collective-permute-start.4 = (bf16[200,768]{1,0:T(8,128)(2,1)S(1)}, bf16[200,768]{1,0:T(8,128)(2,1)S(1)}, u32[]{:S(2)}, u32[]{:S(2)}) collective-permute-start(bf16[200,768]{1,0:T(8,128)(2,1)S(1)} %get-tuple-element.66), channel_id=1, source_target_pairs={{0,20},{4,16},{8,28},{12,24},{16,4},{20,0},{24,12},{28,8},{1,21},{... | collective-permute-start | bytes 921608 | tf_op jit(solution)/shard_map/ppermute | solution.py:233
  29.7 15.9 %collective-permute-start.5 = (bf16[200,768]{1,0:T(8,128)(2,1)S(1)}, bf16[200,768]{1,0:T(8,128)(2,1)S(1)}, u32[]{:S(2)}, u32[]{:S(2)}) collective-permute-start(bf16[200,768]{1,0:T(8,128)(2,1)S(1)} %get-tuple-element.67), channel_id=1, source_target_pairs={{0,12},{4,8},{8,4},{12,0},{16,28},{20,24},{24,20},{28,16},{1,13},{... | collective-permute-start | bytes 921608 | tf_op jit(solution)/shard_map/ppermute | solution.py:233
  32.1 13.5 %collective-permute-start.8 = (bf16[1,200,768]{2,1,0:T(8,128)(2,1)S(1)}, bf16[1,200,768]{2,1,0:T(8,128)(2,1)S(1)}, u32[]{:S(2)}, u32[]{:S(2)}) collective-permute-start(bf16[1,200,768]{2,1,0:T(8,128)(2,1)S(1)} %get-tuple-element.70.rest_2_), channel_id=1, source_target_pairs={{0,1},{1,0},{2,3},{3,2},{4,5},{5,4},{6,7},{7,6},{8,9},{9,8},{10,11... | collective-permute-start | bytes 921608 | tf_op jit(solution)/shard_map/ppermute | solution.py:233
  45.7 15.5 %collective-permute-start.11 = (bf16[2,200,768]{2,1,0:T(8,128)(2,1)S(1)}, bf16[2,200,768]{2,1,0:T(8,128)(2,1)S(1)}, u32[]{:S(2)}, u32[]{:S(2)}) collective-permute-start(bf16[2,200,768]{2,1,0:T(8,128)(2,1)S(1)} %get-tuple-element.76.rest_8_), channel_id=1, source_target_pairs={{0,2},{1,3},{2,0},{3,1},{4,6},{5,7},{6,4},{7,5},{8,10},{9,11},{10,... | collective-permute-start | bytes 1843208 | tf_op jit(solution)/shard_map/ppermute | solution.py:233
  46.2 15.0 %collective-permute-start.12 = (bf16[2,200,768]{2,1,0:T(8,128)(2,1)S(1)}, bf16[2,200,768]{2,1,0:T(8,128)(2,1)S(1)}, u32[]{:S(2)}, u32[]{:S(2)}) collective-permute-start(bf16[2,200,768]{2,1,0:T(8,128)(2,1)S(1)} %get-tuple-element.76.rest_8_), channel_id=1, source_target_pairs={{0,1},{1,0},{2,3},{3,2},{4,5},{5,4},{6,7},{7,6},{8,9},{9,8},{10,11... | collective-permute-start | bytes 1843208 | tf_op jit(solution)/shard_map/ppermute | solution.py:233
  46.2 15.0 %collective-permute-start.13 = (bf16[2,200,768]{2,1,0:T(8,128)(2,1)S(1)}, bf16[2,200,768]{2,1,0:T(8,128)(2,1)S(1)}, u32[]{:S(2)}, u32[]{:S(2)}) collective-permute-start(bf16[2,200,768]{2,1,0:T(8,128)(2,1)S(1)} %get-tuple-element.77.rest_6_), channel_id=1, source_target_pairs={{0,1},{1,0},{2,3},{3,2},{4,5},{5,4},{6,7},{7,6},{8,9},{9,8},{10,11... | collective-permute-start | bytes 1843208 | tf_op jit(solution)/shard_map/ppermute | solution.py:233
  46.7 12.4 %collective-permute-start.9 = (bf16[208,768]{1,0:T(8,128)(2,1)S(1)}, bf16[208,768]{1,0:T(8,128)(2,1)S(1)}, u32[]{:S(2)}, u32[]{:S(2)}) collective-permute-start(bf16[208,768]{1,0:T(8,128)(2,1)S(1)} %get-tuple-element.73), channel_id=1, source_target_pairs={{0,24},{4,28},{8,16},{12,20},{16,8},{20,12},{24,0},{28,4},{1,25},{... | collective-permute-start | bytes 958472 | tf_op jit(solution)/shard_map/ppermute | solution.py:233
  50.2 8.9 %collective-permute-start.10 = (bf16[200,768]{1,0:T(8,128)(2,1)S(1)}, bf16[200,768]{1,0:T(8,128)(2,1)S(1)}, u32[]{:S(2)}, u32[]{:S(2)}) collective-permute-start(bf16[200,768]{1,0:T(8,128)(2,1)S(1)} %get-tuple-element.74), channel_id=1, source_target_pairs={{0,4},{4,0},{8,12},{12,8},{16,20},{20,16},{24,28},{28,24},{1,5},{5... | collective-permute-start | bytes 921608 | tf_op jit(solution)/shard_map/ppermute | solution.py:233
  61.2 4.3 %collective-permute-start.15 = (bf16[2,200,768]{2,1,0:T(8,128)(2,1)S(1)}, bf16[2,200,768]{2,1,0:T(8,128)(2,1)S(1)}, u32[]{:S(2)}, u32[]{:S(2)}) collective-permute-start(bf16[2,200,768]{2,1,0:T(8,128)(2,1)S(1)} %get-tuple-element.86.rest_10_), channel_id=1, source_target_pairs={{0,1},{1,0},{2,3},{3,2},{4,5},{5,4},{6,7},{7,6},{8,9},{9,8},{10,11... | collective-permute-start | bytes 1843208 | tf_op jit(solution)/shard_map/ppermute | solution.py:233
  61.3 16.3 %collective-permute-start.16 = (bf16[2,200,768]{2,1,0:T(8,128)(2,1)S(1)}, bf16[2,200,768]{2,1,0:T(8,128)(2,1)S(1)}, u32[]{:S(2)}, u32[]{:S(2)}) collective-permute-start(bf16[2,200,768]{2,1,0:T(8,128)(2,1)S(1)} %get-tuple-element.88.rest_0_), channel_id=1, source_target_pairs={{0,2},{1,3},{2,0},{3,1},{4,6},{5,7},{6,4},{7,5},{8,10},{9,11},{10,... | collective-permute-start | bytes 1843208 | tf_op jit(solution)/shard_map/ppermute | solution.py:233
  61.8 15.8 %collective-permute-start.17 = (bf16[2,200,768]{2,1,0:T(8,128)(2,1)S(1)}, bf16[2,200,768]{2,1,0:T(8,128)(2,1)S(1)}, u32[]{:S(2)}, u32[]{:S(2)}) collective-permute-start(bf16[2,200,768]{2,1,0:T(8,128)(2,1)S(1)} %get-tuple-element.88.rest_0_), channel_id=1, source_target_pairs={{0,1},{1,0},{2,3},{3,2},{4,5},{5,4},{6,7},{7,6},{8,9},{9,8},{10,11... | collective-permute-start | bytes 1843208 | tf_op jit(solution)/shard_map/ppermute | solution.py:233
  62.0 12.3 %collective-permute-start.14 = (bf16[200,768]{1,0:T(8,128)(2,1)S(1)}, bf16[200,768]{1,0:T(8,128)(2,1)S(1)}, u32[]{:S(2)}, u32[]{:S(2)}) collective-permute-start(bf16[200,768]{1,0:T(8,128)(2,1)S(1)} %get-tuple-element.79), channel_id=1, source_target_pairs={{0,28},{4,24},{8,20},{12,16},{16,12},{20,8},{24,4},{28,0},{1,29},{... | collective-permute-start | bytes 921608 | tf_op jit(solution)/shard_map/ppermute | solution.py:233
  77.6 2.1 %collective-permute-start.18 = (bf16[2,200,768]{2,1,0:T(8,128)(2,1)S(1)}, bf16[2,200,768]{2,1,0:T(8,128)(2,1)S(1)}, u32[]{:S(2)}, u32[]{:S(2)}) collective-permute-start(bf16[2,200,768]{2,1,0:T(8,128)(2,1)S(1)} %get-tuple-element.91.rest_2_), channel_id=1, source_target_pairs={{0,1},{1,0},{2,3},{3,2},{4,5},{5,4},{6,7},{7,6},{8,9},{9,8},{10,11... | collective-permute-start | bytes 1843208 | tf_op jit(solution)/shard_map/ppermute | solution.py:233
  77.7 9.7 %collective-permute-start.19 = (bf16[1,200,768]{2,1,0:T(8,128)(2,1)S(1)}, bf16[1,200,768]{2,1,0:T(8,128)(2,1)S(1)}, u32[]{:S(2)}, u32[]{:S(2)}) collective-permute-start(bf16[1,200,768]{2,1,0:T(8,128)(2,1)S(1)} %get-tuple-element.98.rest_0_), channel_id=1, source_target_pairs={{0,2},{1,3},{2,0},{3,1},{4,6},{5,7},{6,4},{7,5},{8,10},{9,11},{10,... | collective-permute-start | bytes 921608 | tf_op jit(solution)/shard_map/ppermute | solution.py:233
  78.2 9.2 %collective-permute-start.20 = (bf16[1,200,768]{2,1,0:T(8,128)(2,1)S(1)}, bf16[1,200,768]{2,1,0:T(8,128)(2,1)S(1)}, u32[]{:S(2)}, u32[]{:S(2)}) collective-permute-start(bf16[1,200,768]{2,1,0:T(8,128)(2,1)S(1)} %get-tuple-element.98.rest_0_), channel_id=1, source_target_pairs={{0,1},{1,0},{2,3},{3,2},{4,5},{5,4},{6,7},{7,6},{8,9},{9,8},{10,11... | collective-permute-start | bytes 921608 | tf_op jit(solution)/shard_map/ppermute | solution.py:233
  87.4 1.6 %collective-permute-start.21 = (bf16[1,200,768]{2,1,0:T(8,128)(2,1)S(1)}, bf16[1,200,768]{2,1,0:T(8,128)(2,1)S(1)}, u32[]{:S(2)}, u32[]{:S(2)}) collective-permute-start(bf16[1,200,768]{2,1,0:T(8,128)(2,1)S(1)} %get-tuple-element.100.rest_2_), channel_id=1, source_target_pairs={{0,1},{1,0},{2,3},{3,2},{4,5},{5,4},{6,7},{7,6},{8,9},{9,8},{10,11... | collective-permute-start | bytes 921608 | tf_op jit(solution)/shard_map/ppermute | solution.py:233

commit v7 on v6

--- a/solution.py
+++ b/solution.py
@@ -76,7 +76,7 @@
             out[piece + NOTE:] = jnp.zeros((out.shape[0] - piece - NOTE, width), BF16)
 
 
-def first_kernel(n, piece, family_rows, which, here_ref, route_ref, cluster_ref, emb_ref, *rest):
+def first_kernel(n, piece, family_rows, which, here_ref, route_ref, emb_ref, *rest):
     fam_ref, rank_ref, note_ref, unit_ref = rest[:4]
     outs = rest[4:4 + len(which)]
     rows = emb_ref.shape[0]
@@ -87,12 +87,7 @@
     high, low = [jnp.where(mine, x, 0.0) for x in digits(rel_row)]
     at_rank = one_hot(iota((piece, rows), 0) == rank_row)
     slots = dot_nt(jnp.concatenate([high, low], axis=0).astype(BF16), at_rank)
-    cluster = cluster_ref[...]
-    counts = []
-    for c in range(CLUSTERS - 1):
-        total = jnp.sum(jnp.where(cluster <= c, 1.0, 0.0), axis=1, keepdims=True)
-        counts += digits(jnp.broadcast_to(total, (1, piece)).astype(I32))
-    counts = jnp.concatenate(counts, axis=0)
+    counts = jnp.zeros((NOTE - 2, piece), F32)
     spare = note_ref.shape[-1] - piece
     for f in range(n):
         note = jnp.concatenate([slots[f:f + 1], slots[n + f:n + f + 1], counts], axis=0)
@@ -110,10 +105,19 @@
     pack(n, piece, which, here_ref[0], unit_ref, fam_row, rank_row, note_ref, outs)
 
 
-def second_kernel(n, piece, which, here_ref, fam_ref, rank_ref, note_ref, unit_ref, *rest):
-    *outs, token_ref = rest
+def second_kernel(
+    n, piece, which, here_ref, cluster_ref, fam_ref, rank_ref, note_ref, unit_ref, *rest
+):
+    *outs, token_ref, counted = rest
     token_ref[...] = jnp.zeros(token_ref.shape, F32)
-    pack(n, piece, which, here_ref[0], unit_ref, fam_ref[...], rank_ref[...], note_ref, outs)
+    cluster = cluster_ref[...]
+    counts = [jnp.zeros((2, note_ref.shape[-1]), F32)]
+    for c in range(CLUSTERS - 1):
+        total = jnp.sum(jnp.where(cluster <= c, 1.0, 0.0), axis=1, keepdims=True)
+        counts += digits(jnp.broadcast_to(total, (1, note_ref.shape[-1])).astype(I32))
+    counted[...] = note_ref[...]
+    counted[here_ref[0]] = note_ref[here_ref[0]] + jnp.concatenate(counts, axis=0)
+    pack(n, piece, which, here_ref[0], unit_ref, fam_ref[...], rank_ref[...], counted, outs)
 
 
 def join_kernel(count, *refs):
@@ -122,17 +126,17 @@
         out_ref[i] = refs[i][:out_ref.shape[1]]
 
 
-def stage_kernel(n, nb, piece, old, groups, here_ref, token_ref, *rest):
+def stage_kernel(n, nb, piece, old, groups, side, here_ref, token_ref, *rest):
     new = [d for group in groups for d in group]
+    came = range(nb) if side is None else range(side * nb // 2, (side + 1) * nb // 2)
     pieces = [
-        [rest[i * nb + e].at[j] for e in range(nb)]
+        [rest[i * len(came) + k].at[j] for k in range(len(came))]
         for i, group in enumerate(groups)
         for j in range(len(group))
     ]
     out_ref, keys, best, key_kinds, query_kinds, bounds_ref = rest[-6:]
     grp, blk = here_ref[0], here_ref[1]
     width = keys.shape[-1]
-    span = nb * piece
     wide = -(-piece // LANES) * LANES
 
     def note_of(ref):
@@ -155,7 +159,7 @@
         best[...] = jnp.full(best.shape, -1.0, F32)
     for d, refs in zip(new, pieces):
         column = grp ^ d
-        for e, ref in enumerate(refs):
+        for e, ref in zip(came, refs):
             keys[column, blk ^ e] = ref[:piece]
             note = note_of(ref)[:, :piece]
             slots = note[0:1] * 64.0 + note[1:2]
@@ -172,14 +176,21 @@
             )
 
     def fold(query, key, causal):
-        scores = dot_nt(keys[key].reshape(span, width), keys[query, blk])
-        kinds = key_kinds[pl.ds(key * nb, nb)].reshape(span, LANES)
+        if side is None:
+            count, first_blk = nb, 0
+        else:
+            count = nb // 2
+            first_blk = ((blk // count) ^ side) * count
+        span = count * piece
+        k = keys[key, pl.ds(first_blk, count)].reshape(span, width)
+        scores = dot_nt(k, keys[query, blk])
+        kinds = key_kinds[pl.ds(key * nb + first_blk, count)].reshape(span, LANES)
         parts = []
         for at in range(0, piece, LANES):
             w = min(LANES, piece - at)
             match = kinds[:, :w] == query_kinds[query][:, at:at + w]
             if causal:
-                early = iota((span, w), 0) - iota((span, w), 1) < blk * piece + at
+                early = iota((span, w), 0) - iota((span, w), 1) < (blk - first_blk) * piece + at
                 match = match & early
             part = jnp.where(match, scores[:, at:at + w], -1.0)
             parts.append(jnp.max(part.reshape(span // 8, 8, w), axis=0))
@@ -204,7 +215,7 @@
             def _(b):
                 pair(a, b)
 
-    if len(old) + len(new) == n:
+    if len(old) + len(new) == n and side != 0:
         for f in range(n):
             out_ref[f] = jnp.max(best[f], axis=0, keepdims=True)
 
@@ -261,20 +272,21 @@
         out_shape=[shape(1, rows, kind=I32)] * 2
         + [shape(n, NOTE, wide), shape(rows, width, kind=BF16)]
         + [kind_of[d] for d in early],
-        in_specs=[SMEM, VMEM, VMEM, VMEM],
+        in_specs=[SMEM, VMEM, VMEM],
         out_specs=[VMEM] * (4 + len(early)),
         compiler_params=limit(16),
         name="first",
-    )(here, route.reshape(blocks, LANES), cluster, embeddings)
+    )(here, route.reshape(blocks, LANES), embeddings)
     *others, token = pl.pallas_call(
         functools.partial(second_kernel, n, piece, late),
         out_shape=[kind_of[d] for d in late] + [shape(8, LANES)],
-        in_specs=[SMEM] + [VMEM] * 4,
+        in_specs=[SMEM] + [VMEM] * 5,
         out_specs=[VMEM] * (len(late) + 1),
+        scratch_shapes=[pltpu.VMEM((n, NOTE, wide), F32)],
         compiler_params=limit(16),
         cost_estimate=cost(8 * rows * rows * width),
         name="second",
-    )(here, fam, rank, note, unit)
+    )(here, cluster, fam, rank, note, unit)
     sent = dict(zip(early + late, packed + others))
     own, seen, state = {0: sent[0]}, [], []
 
@@ -299,7 +311,7 @@
         )(*ins, *kept)
         return rest[len(later):] + rest[:len(later)]
 
-    def stage(*groups):
+    def stage(*groups, side=None):
         nonlocal token, seen, state
         kept = [
             shape(n, nb, piece, width, kind=BF16),
@@ -314,13 +326,13 @@
         args += list(state)
         ds = [list(group[0]) for group in groups]
         now = seen + sum(ds, [])
-        outs = [shape(8, LANES)] + ([shape(n, 1, piece)] if len(now) == n else []) + kept
+        outs = [shape(8, LANES)] + ([shape(n, 1, piece)] if len(now) == n and side != 0 else []) + kept
         alias = {1: 0}
         if seen:
             alias |= {len(args) - 5 + i: len(outs) - 5 + i for i in range(5)}
         folds = sum(range(len(seen) + 1, len(now) + 1))
         token, *state = pl.pallas_call(
-            functools.partial(stage_kernel, n, nb, piece, seen, ds),
+            functools.partial(stage_kernel, n, nb, piece, seen, ds, side),
             out_shape=outs,
             in_specs=[SMEM] + [VMEM] * (len(args) - 1),
             out_specs=[VMEM] * len(outs),
@@ -329,7 +341,7 @@
             cost_estimate=cost(folds * 4 * piece * piece * nb * width),
             name="stage",
         )(*args)
-        seen = now
+        seen = seen if side == 0 else now
 
     if n == 8:
         to_columns(4, 2)
@@ -348,8 +360,9 @@
         m4, y3, c3 = join((7,), [y3, c3])
         y4, c4, x3 = send(m4, "blk", 2), send(m4, "blk", 1), send(y3, "blk", 1)
         stage(((6, 1), m3, c3, y3, x3))
+        stage(((7,), m4, c4), side=0)
         (y4,) = join((), [y4])
-        stage(((7,), m4, c4, y4, send(y4, "blk", 1)))
+        stage(((7,), y4, send(y4, "blk", 1)), side=1)
     else:
         to_columns(*range(1, n))
         for lo in range(0, n, 8):

time: 107 us -> 105 us (0.981)
  waiting for transfers between devices: 43 us -> 39.9 us
    ppermute x22, waiting for transfers between devices: 43 us -> 39.9 us  [send(): lax.ppermute(x, axis, [(i, i ^ by) for i in range(lax.axis_size(axis))])]
    pallas_call x3 -> x4, Pallas kernels: 15 us -> 15.9 us  [stage(): pl.pallas_call(functools.partial(stage_kernel, n, nb, piece, seen, ds, si...]
  transfers between devices with their start and end apart: 22 -> 22, of which waited for: 11 -> 11; matrix products, arithmetic and copies ran while one was open for 0% -> 0% of each run, Pallas kernels for 14% -> 17%
where the time goes in v7:
time: 105 us
  waiting for transfers between devices  39.9 us (38%)
  Pallas kernels  24.2 us (23%)
  starting transfers between devices  24 us (23%)
  blocking collectives  13.5 us (13%)
  local copies, waits for them, and re-layouts  3.05 us (3%)
    ppermute x22, waiting for transfers between devices, send(): lax.ppermute(x, axis, [(i, i ^ by) for i in range(lax.axis_size(axis))])  39.9 us
    ppermute x22, starting transfers between devices, send(): lax.ppermute(x, axis, [(i, i ^ by) for i in range(lax.axis_size(axis))])  24 us
    pallas_call x4, Pallas kernels, stage(): pl.pallas_call(functools.partial(stage_kernel, n, nb, piece, seen, ds, si...  15.9 us
    all_to_all x1, blocking collectives, on_device(): lax.all_to_all(scores, 'grp', split_axis=0, concat_axis=0, tiled=True)  13.5 us
    pallas_call x1, Pallas kernels, on_device(): pl.pallas_call(functools.partial(first_kernel, n, piece, rows * nb, early...  3.83 us
    pallas_call x1, Pallas kernels, on_device(): pl.pallas_call(functools.partial(second_kernel, n, piece, late), out_shap...  3.5 us
    unnamed x6, local copies, waits for them, and re-layouts  3.05 us
  transfers between devices with their start and end apart: 22, of which 11 were waited for; matrix products, arithmetic and copies ran while one was open for 0% of the time, Pallas kernels for 17%

profile of v7, /device:TPU:0, one launch (start us, length us, event | category | flops | bytes accessed | tf_op | source)
XLA Modules:
  0.0 104.8 jit_solution(14831177426250318762)
XLA Ops:
  0.1 1.7 %copy-done = bf16[1536,768]{1,0:T(8,128)(2,1)S(1)} copy-done((bf16[1536,768]{1,0:T(8,128)(2,1)S(1)}, bf16[1536,768]{1,0:T(8,128)(2,1)}, u32[]{:S(2)}) %copy-start) | copy-done | bytes 2359320
  1.7 0.7 copy-done.1
  2.4 3.8 %first.1 = (s32[1,1536]{1,0:T(1,128)S(1)}, s32[1,1536]{1,0:T(1,128)S(1)}, f32[8,8,256]{2,1,0:T(8,128)S(1)}, bf16[1536,768]{1,0:T(8,128)(2,1)S(1)}, bf16[208,768]...) custom-call(s32[2]{0:T(128)S(1)} %pad_add_fusion.here_ref, s32[12,128]{1,0:T(8,128)S(1)} %bitcast.5, ...), custom_call_target="tpu_custom_call" | custom-call | tf_op jit(solution)/shard_map/first/pallas_call | solution.py:270
  6.3 4.1 %collective-permute-start = (bf16[208,768]{1,0:T(8,128)(2,1)S(1)}, bf16[208,768]{1,0:T(8,128)(2,1)S(1)}, u32[]{:S(2)}, u32[]{:S(2)}) collective-permute-start(bf16[208,768]{1,0:T(8,128)(2,1)S(1)} %get-tuple-element.64), channel_id=1, source_target_pairs={{0,16},{4,20},{8,24},{12,28},{16,0},{20,4},{24,8},{28,12},{1,17},{... | collective-permute-start | bytes 958472 | tf_op jit(solution)/shard_map/ppermute | solution.py:244
  10.4 1.6 %collective-permute-start.1 = (bf16[208,768]{1,0:T(8,128)(2,1)S(1)}, bf16[208,768]{1,0:T(8,128)(2,1)S(1)}, u32[]{:S(2)}, u32[]{:S(2)}) collective-permute-start(bf16[208,768]{1,0:T(8,128)(2,1)S(1)} %get-tuple-element.65), channel_id=1, source_target_pairs={{0,8},{4,12},{8,0},{12,4},{16,24},{20,28},{24,16},{28,20},{1,9},{5... | collective-permute-start | bytes 958472 | tf_op jit(solution)/shard_map/ppermute | solution.py:244
  12.0 0.7 copy-done.2
  12.7 3.5 %second.1 = (bf16[200,768]{1,0:T(8,128)(2,1)S(1)}, bf16[200,768]{1,0:T(8,128)(2,1)S(1)}, bf16[200,768]{1,0:T(8,128)(2,1)S(1)}, bf16[200,768]{1,0:T(8,128)(2,1)S(...) custom-call(s32[2]{0:T(128)S(1)} %pad_add_fusion.here_ref, ...), custom_call_target="tpu_custom_call" | custom-call | flops 14495514624 | tf_op jit(solution)/shard_map/second/pallas_call | solution.py:280
  16.2 1.6 %collective-permute-start.2 = (bf16[1,200,768]{2,1,0:T(8,128)(2,1)S(1)}, bf16[1,200,768]{2,1,0:T(8,128)(2,1)S(1)}, u32[]{:S(2)}, u32[]{:S(2)}) collective-permute-start(bf16[1,200,768]{2,1,0:T(8,128)(2,1)S(1)} %bitcast.6), channel_id=1, source_target_pairs={{0,2},{1,3},{2,0},{3,1},{4,6},{5,7},{6,4},{7,5},{8,10},{9,11},{10,... | collective-permute-start | bytes 921608 | tf_op jit(solution)/shard_map/ppermute | solution.py:244
  17.8 6.9 %collective-permute-done.2.refs_3_ = bf16[1,200,768]{2,1,0:T(8,128)(2,1)S(1)} collective-permute-done((bf16[1,200,768]{2,1,0:T(8,128)(2,1)S(1)}, bf16[1,200,768]{2,1,0:T(8,128)(2,1)S(1)}, u32[]{:S(2)}, u32[]{:S(2)}) %collective-permute-start.2) | collective-permute-done | bytes 307232 | tf_op jit(solution)/shard_map/ppermute | solution.py:244
  25.1 1.6 %collective-permute-start.6 = (bf16[2,200,768]{2,1,0:T(8,128)(2,1)S(1)}, bf16[2,200,768]{2,1,0:T(8,128)(2,1)S(1)}, u32[]{:S(2)}, u32[]{:S(2)}) collective-permute-start(bf16[2,200,768]{2,1,0:T(8,128)(2,1)S(1)} %get-tuple-element.75.rest_4_), channel_id=1, source_target_pairs={{0,2},{1,3},{2,0},{3,1},{4,6},{5,7},{6,4},{7,5},{8,10},{9,11},{10,... | collective-permute-start | bytes 1843208 | tf_op jit(solution)/shard_map/ppermute | solution.py:244
  26.7 2.2 %collective-permute-start.4 = (bf16[200,768]{1,0:T(8,128)(2,1)S(1)}, bf16[200,768]{1,0:T(8,128)(2,1)S(1)}, u32[]{:S(2)}, u32[]{:S(2)}) collective-permute-start(bf16[200,768]{1,0:T(8,128)(2,1)S(1)} %get-tuple-element.72), channel_id=1, source_target_pairs={{0,20},{4,16},{8,28},{12,24},{16,4},{20,0},{24,12},{28,8},{1,21},{... | collective-permute-start | bytes 921608 | tf_op jit(solution)/shard_map/ppermute | solution.py:244
  29.0 2.4 %collective-permute-start.5 = (bf16[200,768]{1,0:T(8,128)(2,1)S(1)}, bf16[200,768]{1,0:T(8,128)(2,1)S(1)}, u32[]{:S(2)}, u32[]{:S(2)}) collective-permute-start(bf16[200,768]{1,0:T(8,128)(2,1)S(1)} %get-tuple-element.73), channel_id=1, source_target_pairs={{0,12},{4,8},{8,4},{12,0},{16,28},{20,24},{24,20},{28,16},{1,13},{... | collective-permute-start | bytes 921608 | tf_op jit(solution)/shard_map/ppermute | solution.py:244
  31.4 13.5 %collective-permute-done.4.refs_0_ = bf16[200,768]{1,0:T(8,128)(2,1)S(1)} collective-permute-done((bf16[200,768]{1,0:T(8,128)(2,1)S(1)}, bf16[200,768]{1,0:T(8,128)(2,1)S(1)}, u32[]{:S(2)}, u32[]{:S(2)}) %collective-permute-start.4) | collective-permute-done | bytes 307232 | tf_op jit(solution)/shard_map/ppermute | solution.py:244
  45.0 0.5 collective-permute-start.11
  45.5 0.5 collective-permute-start.13
  46.0 3.5 %collective-permute-start.9 = (bf16[208,768]{1,0:T(8,128)(2,1)S(1)}, bf16[208,768]{1,0:T(8,128)(2,1)S(1)}, u32[]{:S(2)}, u32[]{:S(2)}) collective-permute-start(bf16[208,768]{1,0:T(8,128)(2,1)S(1)} %get-tuple-element.79), channel_id=1, source_target_pairs={{0,24},{4,28},{8,16},{12,20},{16,8},{20,12},{24,0},{28,4},{1,25},{... | collective-permute-start | bytes 958472 | tf_op jit(solution)/shard_map/ppermute | solution.py:244
  49.5 0.6 collective-permute-start.10
  50.0 8.3 %collective-permute-done.10.refs_1_ = bf16[200,768]{1,0:T(8,128)(2,1)S(1)} collective-permute-done((bf16[200,768]{1,0:T(8,128)(2,1)S(1)}, bf16[200,768]{1,0:T(8,128)(2,1)S(1)}, u32[]{:S(2)}, u32[]{:S(2)}) %collective-permute-start.10) | collective-permute-done | bytes 307232 | tf_op jit(solution)/shard_map/ppermute | solution.py:244
  58.4 2.1 %collective-permute-done.11.refs_3_ = bf16[2,200,768]{2,1,0:T(8,128)(2,1)S(1)} collective-permute-done((bf16[2,200,768]{2,1,0:T(8,128)(2,1)S(1)}, bf16[2,200,768]{2,1,0:T(8,128)(2,1)S(1)}, u32[]{:S(2)}, u32[]{:S(2)}) %collective-permute-start.11) | collective-permute-done | bytes 614432 | tf_op jit(solution)/shard_map/ppermute | solution.py:244
  60.6 0.5 collective-permute-start.16
  61.3 3.5 %collective-permute-start.14 = (bf16[200,768]{1,0:T(8,128)(2,1)S(1)}, bf16[200,768]{1,0:T(8,128)(2,1)S(1)}, u32[]{:S(2)}, u32[]{:S(2)}) collective-permute-start(bf16[200,768]{1,0:T(8,128)(2,1)S(1)} %get-tuple-element.85), channel_id=1, source_target_pairs={{0,28},{4,24},{8,20},{12,16},{16,12},{20,8},{24,4},{28,0},{1,29},{... | collective-permute-start | bytes 921608 | tf_op jit(solution)/shard_map/ppermute | solution.py:244
  64.9 6.4 %stage.4 = (f32[8,128]{1,0:T(8,128)S(1)}, bf16[8,4,192,768]{3,2,1,0:T(8,128)(2,1)S(1)}, f32[8,8,192]{2,1,0:T(8,128)S(1)}, f32[32,192,128]{2,1,0:T(8,128)S(1)}, f...) custom-call(s32[2]{0:T(128)S(1)} %pad_add_fusion.here_ref, ...), custom_call_target="tpu_custom_call", output_to_operand_aliasing={{0}: (1, {})} | custom-call | flops 6794772480 | tf_op jit(solution)/shard_map/stage/pallas_call | solution.py:334
  71.3 2.4 %collective-permute-done.14.refs_0_ = bf16[200,768]{1,0:T(8,128)(2,1)S(1)} collective-permute-done((bf16[200,768]{1,0:T(8,128)(2,1)S(1)}, bf16[200,768]{1,0:T(8,128)(2,1)S(1)}, u32[]{:S(2)}, u32[]{:S(2)}) %collective-permute-start.14) | collective-permute-done | bytes 307232 | tf_op jit(solution)/shard_map/ppermute | solution.py:244
  73.6 3.3 %collective-permute-done.16.refs_2_ = bf16[2,200,768]{2,1,0:T(8,128)(2,1)S(1)} collective-permute-done((bf16[2,200,768]{2,1,0:T(8,128)(2,1)S(1)}, bf16[2,200,768]{2,1,0:T(8,128)(2,1)S(1)}, u32[]{:S(2)}, u32[]{:S(2)}) %collective-permute-start.16) | collective-permute-done | bytes 614432 | tf_op jit(solution)/shard_map/ppermute | solution.py:244
  77.0 0.5 collective-permute-start.19
  77.9 1.1 %collective-permute-done.18.rest_3_ = bf16[2,200,768]{2,1,0:T(8,128)(2,1)S(1)} collective-permute-done((bf16[2,200,768]{2,1,0:T(8,128)(2,1)S(1)}, bf16[2,200,768]{2,1,0:T(8,128)(2,1)S(1)}, u32[]{:S(2)}, u32[]{:S(2)}) %collective-permute-start.18) | collective-permute-done | bytes 614432 | tf_op jit(solution)/shard_map/ppermute | solution.py:244
  79.0 5.3 %stage.5 = (f32[8,128]{1,0:T(8,128)S(1)}, bf16[8,4,192,768]{3,2,1,0:T(8,128)(2,1)S(1)}, f32[8,8,192]{2,1,0:T(8,128)S(1)}, f32[32,192,128]{2,1,0:T(8,128)S(1)}, f...) custom-call(s32[2]{0:T(128)S(1)} %pad_add_fusion.here_ref, ...), custom_call_target="tpu_custom_call", output_to_operand_aliasing={{0}: (1, {}), {1}: (6, {}), {2}: (7, {}), {3}: (8, {}), {4}... | custom-call | flops 5888802816 | tf_op jit(solution)/shard_map/stage/pallas_call | solution.py:334
  84.3 2.1 %stage.6 = (f32[8,128]{1,0:T(8,128)S(1)}, bf16[8,4,192,768]{3,2,1,0:T(8,128)(2,1)S(1)}, f32[8,8,192]{2,1,0:T(8,128)S(1)}, f32[32,192,128]{2,1,0:T(8,128)S(1)}, f...) custom-call(s32[2]{0:T(128)S(1)} %pad_add_fusion.here_ref, ...), custom_call_target="tpu_custom_call", output_to_operand_aliasing={{0}: (1, {}), {1}: (4, {}), {2}: (5, {}), {3}: (6, {}), {4}... | custom-call | flops 3623878656 | tf_op jit(solution)/shard_map/stage/pallas_call | solution.py:334
  86.7 1.6 %collective-permute-done.21.rest_1_ = bf16[1,200,768]{2,1,0:T(8,128)(2,1)S(1)} collective-permute-done((bf16[1,200,768]{2,1,0:T(8,128)(2,1)S(1)}, bf16[1,200,768]{2,1,0:T(8,128)(2,1)S(1)}, u32[]{:S(2)}, u32[]{:S(2)}) %collective-permute-start.21) | collective-permute-done | bytes 307232 | tf_op jit(solution)/shard_map/ppermute | solution.py:244
  88.3 2.1 %stage.7 = (f32[8,128]{1,0:T(8,128)S(1)}, f32[8,1,192]{2,1,0:T(1,128)S(1)}, bf16[8,4,192,768]{3,2,1,0:T(8,128)(2,1)S(1)}, f32[8,8,192]{2,1,0:T(8,128)S(1)}, f32[...) custom-call(s32[2]{0:T(128)S(1)} %pad_add_fusion.here_ref, ...), custom_call_target="tpu_custom_call", output_to_operand_aliasing={{0}: (1, {}), {2}: (4, {}), {3}: (5, {}), {4}: (6, {}), {5}... | custom-call | flops 3623878656 | tf_op jit(solution)/shard_map/stage/pallas_call | solution.py:334
  90.5 13.5 %all_to_all.5.score_ref = f32[8,1,192]{2,1,0:T(1,128)S(1)} all-to-all(f32[8,1,192]{2,1,0:T(1,128)S(1)} %get-tuple-element.118), channel_id=1, replica_groups=mesh['grp'=8,'blk'=4] {'grp'}, dimensions={0} | all-to-all | bytes 12288 | tf_op jit(solution)/shard_map/all_to_all | solution.py:375
  103.9 0.8 unpack.1
  (32 shorter events, 1.7 us)
Async XLA Ops:
  0.1 1.7 %copy-start = (bf16[1536,768]{1,0:T(8,128)(2,1)S(1)}, bf16[1536,768]{1,0:T(8,128)(2,1)}, u32[]{:S(2)}) copy-start(bf16[1536,768]{1,0:T(8,128)(2,1)} %emb_ref.1) | copy-start | bytes 7077892
  1.7 0.7 copy-start.1
  6.3 18.6 %collective-permute-start = (bf16[208,768]{1,0:T(8,128)(2,1)S(1)}, bf16[208,768]{1,0:T(8,128)(2,1)S(1)}, u32[]{:S(2)}, u32[]{:S(2)}) collective-permute-start(bf16[208,768]{1,0:T(8,128)(2,1)S(1)} %get-tuple-element.64), channel_id=1, source_target_pairs={{0,16},{4,20},{8,24},{12,28},{16,0},{20,4},{24,8},{28,12},{1,17},{... | collective-permute-start | bytes 958472 | tf_op jit(solution)/shard_map/ppermute | solution.py:244
  10.4 14.7 %collective-permute-start.1 = (bf16[208,768]{1,0:T(8,128)(2,1)S(1)}, bf16[208,768]{1,0:T(8,128)(2,1)S(1)}, u32[]{:S(2)}, u32[]{:S(2)}) collective-permute-start(bf16[208,768]{1,0:T(8,128)(2,1)S(1)} %get-tuple-element.65), channel_id=1, source_target_pairs={{0,8},{4,12},{8,0},{12,4},{16,24},{20,28},{24,16},{28,20},{1,9},{5... | collective-permute-start | bytes 958472 | tf_op jit(solution)/shard_map/ppermute | solution.py:244
  12.0 0.7 copy-start.2
  16.2 8.5 %collective-permute-start.2 = (bf16[1,200,768]{2,1,0:T(8,128)(2,1)S(1)}, bf16[1,200,768]{2,1,0:T(8,128)(2,1)S(1)}, u32[]{:S(2)}, u32[]{:S(2)}) collective-permute-start(bf16[1,200,768]{2,1,0:T(8,128)(2,1)S(1)} %bitcast.6), channel_id=1, source_target_pairs={{0,2},{1,3},{2,0},{3,1},{4,6},{5,7},{6,4},{7,5},{8,10},{9,11},{10,... | collective-permute-start | bytes 921608 | tf_op jit(solution)/shard_map/ppermute | solution.py:244
  17.7 6.9 %collective-permute-start.3 = (bf16[1,200,768]{2,1,0:T(8,128)(2,1)S(1)}, bf16[1,200,768]{2,1,0:T(8,128)(2,1)S(1)}, u32[]{:S(2)}, u32[]{:S(2)}) collective-permute-start(bf16[1,200,768]{2,1,0:T(8,128)(2,1)S(1)} %bitcast.7), channel_id=1, source_target_pairs={{0,1},{1,0},{2,3},{3,2},{4,5},{5,4},{6,7},{7,6},{8,9},{9,8},{10,11... | collective-permute-start | bytes 921608 | tf_op jit(solution)/shard_map/ppermute | solution.py:244
  25.1 19.8 %collective-permute-start.6 = (bf16[2,200,768]{2,1,0:T(8,128)(2,1)S(1)}, bf16[2,200,768]{2,1,0:T(8,128)(2,1)S(1)}, u32[]{:S(2)}, u32[]{:S(2)}) collective-permute-start(bf16[2,200,768]{2,1,0:T(8,128)(2,1)S(1)} %get-tuple-element.75.rest_4_), channel_id=1, source_target_pairs={{0,2},{1,3},{2,0},{3,1},{4,6},{5,7},{6,4},{7,5},{8,10},{9,11},{10,... | collective-permute-start | bytes 1843208 | tf_op jit(solution)/shard_map/ppermute | solution.py:244
  26.7 18.2 %collective-permute-start.7 = (bf16[2,200,768]{2,1,0:T(8,128)(2,1)S(1)}, bf16[2,200,768]{2,1,0:T(8,128)(2,1)S(1)}, u32[]{:S(2)}, u32[]{:S(2)}) collective-permute-start(bf16[2,200,768]{2,1,0:T(8,128)(2,1)S(1)} %get-tuple-element.75.rest_4_), channel_id=1, source_target_pairs={{0,1},{1,0},{2,3},{3,2},{4,5},{5,4},{6,7},{7,6},{8,9},{9,8},{10,11... | collective-permute-start | bytes 1843208 | tf_op jit(solution)/shard_map/ppermute | solution.py:244
  26.7 18.2 %collective-permute-start.4 = (bf16[200,768]{1,0:T(8,128)(2,1)S(1)}, bf16[200,768]{1,0:T(8,128)(2,1)S(1)}, u32[]{:S(2)}, u32[]{:S(2)}) collective-permute-start(bf16[200,768]{1,0:T(8,128)(2,1)S(1)} %get-tuple-element.72), channel_id=1, source_target_pairs={{0,20},{4,16},{8,28},{12,24},{16,4},{20,0},{24,12},{28,8},{1,21},{... | collective-permute-start | bytes 921608 | tf_op jit(solution)/shard_map/ppermute | solution.py:244
  29.0 15.9 %collective-permute-start.5 = (bf16[200,768]{1,0:T(8,128)(2,1)S(1)}, bf16[200,768]{1,0:T(8,128)(2,1)S(1)}, u32[]{:S(2)}, u32[]{:S(2)}) collective-permute-start(bf16[200,768]{1,0:T(8,128)(2,1)S(1)} %get-tuple-element.73), channel_id=1, source_target_pairs={{0,12},{4,8},{8,4},{12,0},{16,28},{20,24},{24,20},{28,16},{1,13},{... | collective-permute-start | bytes 921608 | tf_op jit(solution)/shard_map/ppermute | solution.py:244
  31.4 13.5 %collective-permute-start.8 = (bf16[1,200,768]{2,1,0:T(8,128)(2,1)S(1)}, bf16[1,200,768]{2,1,0:T(8,128)(2,1)S(1)}, u32[]{:S(2)}, u32[]{:S(2)}) collective-permute-start(bf16[1,200,768]{2,1,0:T(8,128)(2,1)S(1)} %get-tuple-element.76.rest_2_), channel_id=1, source_target_pairs={{0,1},{1,0},{2,3},{3,2},{4,5},{5,4},{6,7},{7,6},{8,9},{9,8},{10,11... | collective-permute-start | bytes 921608 | tf_op jit(solution)/shard_map/ppermute | solution.py:244
  45.0 15.5 %collective-permute-start.11 = (bf16[2,200,768]{2,1,0:T(8,128)(2,1)S(1)}, bf16[2,200,768]{2,1,0:T(8,128)(2,1)S(1)}, u32[]{:S(2)}, u32[]{:S(2)}) collective-permute-start(bf16[2,200,768]{2,1,0:T(8,128)(2,1)S(1)} %get-tuple-element.82.rest_8_), channel_id=1, source_target_pairs={{0,2},{1,3},{2,0},{3,1},{4,6},{5,7},{6,4},{7,5},{8,10},{9,11},{10,... | collective-permute-start | bytes 1843208 | tf_op jit(solution)/shard_map/ppermute | solution.py:244
  45.5 15.0 %collective-permute-start.12 = (bf16[2,200,768]{2,1,0:T(8,128)(2,1)S(1)}, bf16[2,200,768]{2,1,0:T(8,128)(2,1)S(1)}, u32[]{:S(2)}, u32[]{:S(2)}) collective-permute-start(bf16[2,200,768]{2,1,0:T(8,128)(2,1)S(1)} %get-tuple-element.82.rest_8_), channel_id=1, source_target_pairs={{0,1},{1,0},{2,3},{3,2},{4,5},{5,4},{6,7},{7,6},{8,9},{9,8},{10,11... | collective-permute-start | bytes 1843208 | tf_op jit(solution)/shard_map/ppermute | solution.py:244
  45.5 15.0 %collective-permute-start.13 = (bf16[2,200,768]{2,1,0:T(8,128)(2,1)S(1)}, bf16[2,200,768]{2,1,0:T(8,128)(2,1)S(1)}, u32[]{:S(2)}, u32[]{:S(2)}) collective-permute-start(bf16[2,200,768]{2,1,0:T(8,128)(2,1)S(1)} %get-tuple-element.83.rest_6_), channel_id=1, source_target_pairs={{0,1},{1,0},{2,3},{3,2},{4,5},{5,4},{6,7},{7,6},{8,9},{9,8},{10,11... | collective-permute-start | bytes 1843208 | tf_op jit(solution)/shard_map/ppermute | solution.py:244
  46.0 12.4 %collective-permute-start.9 = (bf16[208,768]{1,0:T(8,128)(2,1)S(1)}, bf16[208,768]{1,0:T(8,128)(2,1)S(1)}, u32[]{:S(2)}, u32[]{:S(2)}) collective-permute-start(bf16[208,768]{1,0:T(8,128)(2,1)S(1)} %get-tuple-element.79), channel_id=1, source_target_pairs={{0,24},{4,28},{8,16},{12,20},{16,8},{20,12},{24,0},{28,4},{1,25},{... | collective-permute-start | bytes 958472 | tf_op jit(solution)/shard_map/ppermute | solution.py:244
  49.5 8.9 %collective-permute-start.10 = (bf16[200,768]{1,0:T(8,128)(2,1)S(1)}, bf16[200,768]{1,0:T(8,128)(2,1)S(1)}, u32[]{:S(2)}, u32[]{:S(2)}) collective-permute-start(bf16[200,768]{1,0:T(8,128)(2,1)S(1)} %get-tuple-element.80), channel_id=1, source_target_pairs={{0,4},{4,0},{8,12},{12,8},{16,20},{20,16},{24,28},{28,24},{1,5},{5... | collective-permute-start | bytes 921608 | tf_op jit(solution)/shard_map/ppermute | solution.py:244
  60.5 4.3 %collective-permute-start.15 = (bf16[2,200,768]{2,1,0:T(8,128)(2,1)S(1)}, bf16[2,200,768]{2,1,0:T(8,128)(2,1)S(1)}, u32[]{:S(2)}, u32[]{:S(2)}) collective-permute-start(bf16[2,200,768]{2,1,0:T(8,128)(2,1)S(1)} %get-tuple-element.92.rest_10_), channel_id=1, source_target_pairs={{0,1},{1,0},{2,3},{3,2},{4,5},{5,4},{6,7},{7,6},{8,9},{9,8},{10,11... | collective-permute-start | bytes 1843208 | tf_op jit(solution)/shard_map/ppermute | solution.py:244
  60.6 16.3 %collective-permute-start.16 = (bf16[2,200,768]{2,1,0:T(8,128)(2,1)S(1)}, bf16[2,200,768]{2,1,0:T(8,128)(2,1)S(1)}, u32[]{:S(2)}, u32[]{:S(2)}) collective-permute-start(bf16[2,200,768]{2,1,0:T(8,128)(2,1)S(1)} %get-tuple-element.94.rest_0_), channel_id=1, source_target_pairs={{0,2},{1,3},{2,0},{3,1},{4,6},{5,7},{6,4},{7,5},{8,10},{9,11},{10,... | collective-permute-start | bytes 1843208 | tf_op jit(solution)/shard_map/ppermute | solution.py:244
  61.1 15.7 %collective-permute-start.17 = (bf16[2,200,768]{2,1,0:T(8,128)(2,1)S(1)}, bf16[2,200,768]{2,1,0:T(8,128)(2,1)S(1)}, u32[]{:S(2)}, u32[]{:S(2)}) collective-permute-start(bf16[2,200,768]{2,1,0:T(8,128)(2,1)S(1)} %get-tuple-element.94.rest_0_), channel_id=1, source_target_pairs={{0,1},{1,0},{2,3},{3,2},{4,5},{5,4},{6,7},{7,6},{8,9},{9,8},{10,11... | collective-permute-start | bytes 1843208 | tf_op jit(solution)/shard_map/ppermute | solution.py:244
  61.3 12.3 %collective-permute-start.14 = (bf16[200,768]{1,0:T(8,128)(2,1)S(1)}, bf16[200,768]{1,0:T(8,128)(2,1)S(1)}, u32[]{:S(2)}, u32[]{:S(2)}) collective-permute-start(bf16[200,768]{1,0:T(8,128)(2,1)S(1)} %get-tuple-element.85), channel_id=1, source_target_pairs={{0,28},{4,24},{8,20},{12,16},{16,12},{20,8},{24,4},{28,0},{1,29},{... | collective-permute-start | bytes 921608 | tf_op jit(solution)/shard_map/ppermute | solution.py:244
  76.9 2.1 %collective-permute-start.18 = (bf16[2,200,768]{2,1,0:T(8,128)(2,1)S(1)}, bf16[2,200,768]{2,1,0:T(8,128)(2,1)S(1)}, u32[]{:S(2)}, u32[]{:S(2)}) collective-permute-start(bf16[2,200,768]{2,1,0:T(8,128)(2,1)S(1)} %get-tuple-element.97.rest_2_), channel_id=1, source_target_pairs={{0,1},{1,0},{2,3},{3,2},{4,5},{5,4},{6,7},{7,6},{8,9},{9,8},{10,11... | collective-permute-start | bytes 1843208 | tf_op jit(solution)/shard_map/ppermute | solution.py:244
  77.0 7.3 %collective-permute-start.19 = (bf16[1,200,768]{2,1,0:T(8,128)(2,1)S(1)}, bf16[1,200,768]{2,1,0:T(8,128)(2,1)S(1)}, u32[]{:S(2)}, u32[]{:S(2)}) collective-permute-start(bf16[1,200,768]{2,1,0:T(8,128)(2,1)S(1)} %get-tuple-element.104.rest_0_), channel_id=1, source_target_pairs={{0,1},{1,0},{2,3},{3,2},{4,5},{5,4},{6,7},{7,6},{8,9},{9,8},{10,11... | collective-permute-start | bytes 921608 | tf_op jit(solution)/shard_map/ppermute | solution.py:244
  77.5 9.3 %collective-permute-start.20 = (bf16[1,200,768]{2,1,0:T(8,128)(2,1)S(1)}, bf16[1,200,768]{2,1,0:T(8,128)(2,1)S(1)}, u32[]{:S(2)}, u32[]{:S(2)}) collective-permute-start(bf16[1,200,768]{2,1,0:T(8,128)(2,1)S(1)} %get-tuple-element.104.rest_0_), channel_id=1, source_target_pairs={{0,2},{1,3},{2,0},{3,1},{4,6},{5,7},{6,4},{7,5},{8,10},{9,11},{10,... | collective-permute-start | bytes 921608 | tf_op jit(solution)/shard_map/ppermute | solution.py:244
  86.7 1.6 %collective-permute-start.21 = (bf16[1,200,768]{2,1,0:T(8,128)(2,1)S(1)}, bf16[1,200,768]{2,1,0:T(8,128)(2,1)S(1)}, u32[]{:S(2)}, u32[]{:S(2)}) collective-permute-start(bf16[1,200,768]{2,1,0:T(8,128)(2,1)S(1)} %get-tuple-element.112.rest_0_), channel_id=1, source_target_pairs={{0,1},{1,0},{2,3},{3,2},{4,5},{5,4},{6,7},{7,6},{8,9},{9,8},{10,11... | collective-permute-start | bytes 921608 | tf_op jit(solution)/shard_map/ppermute | solution.py:244

commit v8 on v7

--- a/solution.py
+++ b/solution.py
@@ -347,19 +347,19 @@
         to_columns(4, 2)
         m0 = own[0].reshape(1, *one_piece.shape)
         y0, c0 = send(m0, "blk", 2), send(m0, "blk", 1)
-        m1, y0, c0, sent[5], sent[3] = join((4, 2), [y0, c0, sent[5], sent[3]])
-        to_columns(5, 3)
+        m1, y0, c0, sent[5], sent[1] = join((4, 2), [y0, c0, sent[5], sent[1]])
+        to_columns(5, 1)
         y1, c1, x0 = send(m1, "blk", 2), send(m1, "blk", 1), send(y0, "blk", 1)
-        m2, y1, c1, x0, sent[6], sent[1] = join((5, 3), [y1, c1, x0, sent[6], sent[1]])
-        to_columns(6, 1)
+        m2, y1, c1, x0, sent[6], sent[3] = join((5, 1), [y1, c1, x0, sent[6], sent[3]])
+        to_columns(6, 3)
         y2, c2, x1 = send(m2, "blk", 2), send(m2, "blk", 1), send(y1, "blk", 1)
-        m3, y2, c2, x1, sent[7] = join((6, 1), [y2, c2, x1, sent[7]])
+        m3, y2, c2, x1, sent[7] = join((6, 3), [y2, c2, x1, sent[7]])
         to_columns(7)
         y3, c3, x2 = send(m3, "blk", 2), send(m3, "blk", 1), send(y2, "blk", 1)
-        stage(((0,), m0, c0, y0, x0), ((4, 2), m1, c1, y1, x1), ((5, 3), m2, c2, y2, x2))
+        stage(((0,), m0, c0, y0, x0), ((4, 2), m1, c1, y1, x1), ((5, 1), m2, c2, y2, x2))
         m4, y3, c3 = join((7,), [y3, c3])
         y4, c4, x3 = send(m4, "blk", 2), send(m4, "blk", 1), send(y3, "blk", 1)
-        stage(((6, 1), m3, c3, y3, x3))
+        stage(((6, 3), m3, c3, y3, x3))
         stage(((7,), m4, c4), side=0)
         (y4,) = join((), [y4])
         stage(((7,), y4, send(y4, "blk", 1)), side=1)

time: 105 us -> 107 us (1.019)
  waiting for transfers between devices: 39.9 us -> 46.3 us
  blocking collectives: 13.5 us -> 10.9 us
  starting transfers between devices: 24 us -> 21.9 us
    ppermute x22, waiting for transfers between devices: 39.9 us -> 46.3 us  [send(): lax.ppermute(x, axis, [(i, i ^ by) for i in range(lax.axis_size(axis))])]
    all_to_all x1, blocking collectives: 13.5 us -> 10.9 us  [on_device(): lax.all_to_all(scores, 'grp', split_axis=0, concat_axis=0, tiled=True)]
    ppermute x22, starting transfers between devices: 24 us -> 21.9 us  [send(): lax.ppermute(x, axis, [(i, i ^ by) for i in range(lax.axis_size(axis))])]
  transfers between devices with their start and end apart: 22 -> 22, of which waited for: 11 -> 9; matrix products, arithmetic and copies ran while one was open for 0% -> 0% of each run, Pallas kernels for 17% -> 16%
where the time goes in v8:
time: 107 us
  waiting for transfers between devices  46.3 us (43%)
  Pallas kernels  24.2 us (23%)
  starting transfers between devices  21.9 us (20%)
  blocking collectives  10.9 us (10%)
  local copies, waits for them, and re-layouts  3.05 us (3%)
    ppermute x22, waiting for transfers between devices, send(): lax.ppermute(x, axis, [(i, i ^ by) for i in range(lax.axis_size(axis))])  46.3 us
    ppermute x22, starting transfers between devices, send(): lax.ppermute(x, axis, [(i, i ^ by) for i in range(lax.axis_size(axis))])  21.9 us
    pallas_call x4, Pallas kernels, stage(): pl.pallas_call(functools.partial(stage_kernel, n, nb, piece, seen, ds, si...  15.9 us
    all_to_all x1, blocking collectives, on_device(): lax.all_to_all(scores, 'grp', split_axis=0, concat_axis=0, tiled=True)  10.9 us
    pallas_call x1, Pallas kernels, on_device(): pl.pallas_call(functools.partial(first_kernel, n, piece, rows * nb, early...  3.83 us
    pallas_call x1, Pallas kernels, on_device(): pl.pallas_call(functools.partial(second_kernel, n, piece, late), out_shap...  3.5 us
    unnamed x6, local copies, waits for them, and re-layouts  3.05 us
  transfers between devices with their start and end apart: 22, of which 9 were waited for; matrix products, arithmetic and copies ran while one was open for 0% of the time, Pallas kernels for 16%

profile of v8, /device:TPU:0, one launch (start us, length us, event | category | flops | bytes accessed | tf_op | source)
XLA Modules:
  0.0 106.6 jit_solution(7707961281314907411)
XLA Ops:
  0.1 1.7 %copy-done = bf16[1536,768]{1,0:T(8,128)(2,1)S(1)} copy-done((bf16[1536,768]{1,0:T(8,128)(2,1)S(1)}, bf16[1536,768]{1,0:T(8,128)(2,1)}, u32[]{:S(2)}) %copy-start) | copy-done | bytes 2359320
  1.7 0.7 copy-done.1
  2.4 3.8 %first.1 = (s32[1,1536]{1,0:T(1,128)S(1)}, s32[1,1536]{1,0:T(1,128)S(1)}, f32[8,8,256]{2,1,0:T(8,128)S(1)}, bf16[1536,768]{1,0:T(8,128)(2,1)S(1)}, bf16[208,768]...) custom-call(s32[2]{0:T(128)S(1)} %pad_add_fusion.here_ref, s32[12,128]{1,0:T(8,128)S(1)} %bitcast.5, ...), custom_call_target="tpu_custom_call" | custom-call | tf_op jit(solution)/shard_map/first/pallas_call | solution.py:270
  6.3 4.1 %collective-permute-start = (bf16[208,768]{1,0:T(8,128)(2,1)S(1)}, bf16[208,768]{1,0:T(8,128)(2,1)S(1)}, u32[]{:S(2)}, u32[]{:S(2)}) collective-permute-start(bf16[208,768]{1,0:T(8,128)(2,1)S(1)} %get-tuple-element.64), channel_id=1, source_target_pairs={{0,16},{4,20},{8,24},{12,28},{16,0},{20,4},{24,8},{28,12},{1,17},{... | collective-permute-start | bytes 958472 | tf_op jit(solution)/shard_map/ppermute | solution.py:244
  10.4 1.6 %collective-permute-start.1 = (bf16[208,768]{1,0:T(8,128)(2,1)S(1)}, bf16[208,768]{1,0:T(8,128)(2,1)S(1)}, u32[]{:S(2)}, u32[]{:S(2)}) collective-permute-start(bf16[208,768]{1,0:T(8,128)(2,1)S(1)} %get-tuple-element.65), channel_id=1, source_target_pairs={{0,8},{4,12},{8,0},{12,4},{16,24},{20,28},{24,16},{28,20},{1,9},{5... | collective-permute-start | bytes 958472 | tf_op jit(solution)/shard_map/ppermute | solution.py:244
  12.0 0.7 copy-done.2
  12.7 3.5 %second.1 = (bf16[200,768]{1,0:T(8,128)(2,1)S(1)}, bf16[200,768]{1,0:T(8,128)(2,1)S(1)}, bf16[200,768]{1,0:T(8,128)(2,1)S(1)}, bf16[200,768]{1,0:T(8,128)(2,1)S(...) custom-call(s32[2]{0:T(128)S(1)} %pad_add_fusion.here_ref, ...), custom_call_target="tpu_custom_call" | custom-call | flops 14495514624 | tf_op jit(solution)/shard_map/second/pallas_call | solution.py:280
  16.2 1.6 %collective-permute-start.2 = (bf16[1,200,768]{2,1,0:T(8,128)(2,1)S(1)}, bf16[1,200,768]{2,1,0:T(8,128)(2,1)S(1)}, u32[]{:S(2)}, u32[]{:S(2)}) collective-permute-start(bf16[1,200,768]{2,1,0:T(8,128)(2,1)S(1)} %bitcast.6), channel_id=1, source_target_pairs={{0,2},{1,3},{2,0},{3,1},{4,6},{5,7},{6,4},{7,5},{8,10},{9,11},{10,... | collective-permute-start | bytes 921608 | tf_op jit(solution)/shard_map/ppermute | solution.py:244
  17.8 6.9 %collective-permute-done.2.refs_3_ = bf16[1,200,768]{2,1,0:T(8,128)(2,1)S(1)} collective-permute-done((bf16[1,200,768]{2,1,0:T(8,128)(2,1)S(1)}, bf16[1,200,768]{2,1,0:T(8,128)(2,1)S(1)}, u32[]{:S(2)}, u32[]{:S(2)}) %collective-permute-start.2) | collective-permute-done | bytes 307232 | tf_op jit(solution)/shard_map/ppermute | solution.py:244
  24.9 0.2 collective-permute-done.1.refs_1_
  25.1 1.6 %collective-permute-start.6 = (bf16[2,200,768]{2,1,0:T(8,128)(2,1)S(1)}, bf16[2,200,768]{2,1,0:T(8,128)(2,1)S(1)}, u32[]{:S(2)}, u32[]{:S(2)}) collective-permute-start(bf16[2,200,768]{2,1,0:T(8,128)(2,1)S(1)} %get-tuple-element.75.rest_4_), channel_id=1, source_target_pairs={{0,2},{1,3},{2,0},{3,1},{4,6},{5,7},{6,4},{7,5},{8,10},{9,11},{10,... | collective-permute-start | bytes 1843208 | tf_op jit(solution)/shard_map/ppermute | solution.py:244
  26.7 2.2 %collective-permute-start.4 = (bf16[200,768]{1,0:T(8,128)(2,1)S(1)}, bf16[200,768]{1,0:T(8,128)(2,1)S(1)}, u32[]{:S(2)}, u32[]{:S(2)}) collective-permute-start(bf16[200,768]{1,0:T(8,128)(2,1)S(1)} %get-tuple-element.72), channel_id=1, source_target_pairs={{0,20},{4,16},{8,28},{12,24},{16,4},{20,0},{24,12},{28,8},{1,21},{... | collective-permute-start | bytes 921608 | tf_op jit(solution)/shard_map/ppermute | solution.py:244
  29.0 0.5 collective-permute-start.5
  29.5 15.3 %collective-permute-done.4.refs_0_ = bf16[200,768]{1,0:T(8,128)(2,1)S(1)} collective-permute-done((bf16[200,768]{1,0:T(8,128)(2,1)S(1)}, bf16[200,768]{1,0:T(8,128)(2,1)S(1)}, u32[]{:S(2)}, u32[]{:S(2)}) %collective-permute-start.4) | collective-permute-done | bytes 307232 | tf_op jit(solution)/shard_map/ppermute | solution.py:244
  44.9 0.5 collective-permute-start.11
  45.4 0.5 collective-permute-start.13
  45.9 2.7 %collective-permute-start.9 = (bf16[208,768]{1,0:T(8,128)(2,1)S(1)}, bf16[208,768]{1,0:T(8,128)(2,1)S(1)}, u32[]{:S(2)}, u32[]{:S(2)}) collective-permute-start(bf16[208,768]{1,0:T(8,128)(2,1)S(1)} %get-tuple-element.79), channel_id=1, source_target_pairs={{0,24},{4,28},{8,16},{12,20},{16,8},{20,12},{24,0},{28,4},{1,25},{... | collective-permute-start | bytes 958472 | tf_op jit(solution)/shard_map/ppermute | solution.py:244
  48.6 16.2 %collective-permute-done.10.refs_1_ = bf16[200,768]{1,0:T(8,128)(2,1)S(1)} collective-permute-done((bf16[200,768]{1,0:T(8,128)(2,1)S(1)}, bf16[200,768]{1,0:T(8,128)(2,1)S(1)}, u32[]{:S(2)}, u32[]{:S(2)}) %collective-permute-start.10) | collective-permute-done | bytes 307232 | tf_op jit(solution)/shard_map/ppermute | solution.py:244
  65.0 1.6 %collective-permute-start.16 = (bf16[2,200,768]{2,1,0:T(8,128)(2,1)S(1)}, bf16[2,200,768]{2,1,0:T(8,128)(2,1)S(1)}, u32[]{:S(2)}, u32[]{:S(2)}) collective-permute-start(bf16[2,200,768]{2,1,0:T(8,128)(2,1)S(1)} %get-tuple-element.94.rest_0_), channel_id=1, source_target_pairs={{0,2},{1,3},{2,0},{3,1},{4,6},{5,7},{6,4},{7,5},{8,10},{9,11},{10,... | collective-permute-start | bytes 1843208 | tf_op jit(solution)/shard_map/ppermute | solution.py:244
  66.7 2.5 %collective-permute-start.14 = (bf16[200,768]{1,0:T(8,128)(2,1)S(1)}, bf16[200,768]{1,0:T(8,128)(2,1)S(1)}, u32[]{:S(2)}, u32[]{:S(2)}) collective-permute-start(bf16[200,768]{1,0:T(8,128)(2,1)S(1)} %get-tuple-element.85), channel_id=1, source_target_pairs={{0,28},{4,24},{8,20},{12,16},{16,12},{20,8},{24,4},{28,0},{1,29},{... | collective-permute-start | bytes 921608 | tf_op jit(solution)/shard_map/ppermute | solution.py:244
  69.3 6.4 %stage.4 = (f32[8,128]{1,0:T(8,128)S(1)}, bf16[8,4,192,768]{3,2,1,0:T(8,128)(2,1)S(1)}, f32[8,8,192]{2,1,0:T(8,128)S(1)}, f32[32,192,128]{2,1,0:T(8,128)S(1)}, f...) custom-call(s32[2]{0:T(128)S(1)} %pad_add_fusion.here_ref, ...), custom_call_target="tpu_custom_call", output_to_operand_aliasing={{0}: (1, {})} | custom-call | flops 6794772480 | tf_op jit(solution)/shard_map/stage/pallas_call | solution.py:334
  75.7 3.4 %collective-permute-done.14.refs_0_ = bf16[200,768]{1,0:T(8,128)(2,1)S(1)} collective-permute-done((bf16[200,768]{1,0:T(8,128)(2,1)S(1)}, bf16[200,768]{1,0:T(8,128)(2,1)S(1)}, u32[]{:S(2)}, u32[]{:S(2)}) %collective-permute-start.14) | collective-permute-done | bytes 307232 | tf_op jit(solution)/shard_map/ppermute | solution.py:244
  79.0 2.2 %collective-permute-done.16.refs_2_ = bf16[2,200,768]{2,1,0:T(8,128)(2,1)S(1)} collective-permute-done((bf16[2,200,768]{2,1,0:T(8,128)(2,1)S(1)}, bf16[2,200,768]{2,1,0:T(8,128)(2,1)S(1)}, u32[]{:S(2)}, u32[]{:S(2)}) %collective-permute-start.16) | collective-permute-done | bytes 614432 | tf_op jit(solution)/shard_map/ppermute | solution.py:244
  81.4 0.5 collective-permute-start.19
  81.9 1.5 %collective-permute-start.20 = (bf16[1,200,768]{2,1,0:T(8,128)(2,1)S(1)}, bf16[1,200,768]{2,1,0:T(8,128)(2,1)S(1)}, u32[]{:S(2)}, u32[]{:S(2)}) collective-permute-start(bf16[1,200,768]{2,1,0:T(8,128)(2,1)S(1)} %get-tuple-element.104.rest_0_), channel_id=1, source_target_pairs={{0,2},{1,3},{2,0},{3,1},{4,6},{5,7},{6,4},{7,5},{8,10},{9,11},{10,... | collective-permute-start | bytes 921608 | tf_op jit(solution)/shard_map/ppermute | solution.py:244
  83.4 5.3 %stage.5 = (f32[8,128]{1,0:T(8,128)S(1)}, bf16[8,4,192,768]{3,2,1,0:T(8,128)(2,1)S(1)}, f32[8,8,192]{2,1,0:T(8,128)S(1)}, f32[32,192,128]{2,1,0:T(8,128)S(1)}, f...) custom-call(s32[2]{0:T(128)S(1)} %pad_add_fusion.here_ref, ...), custom_call_target="tpu_custom_call", output_to_operand_aliasing={{0}: (1, {}), {1}: (6, {}), {2}: (7, {}), {3}: (8, {}), {4}... | custom-call | flops 5888802816 | tf_op jit(solution)/shard_map/stage/pallas_call | solution.py:334
  88.7 2.1 %stage.6 = (f32[8,128]{1,0:T(8,128)S(1)}, bf16[8,4,192,768]{3,2,1,0:T(8,128)(2,1)S(1)}, f32[8,8,192]{2,1,0:T(8,128)S(1)}, f32[32,192,128]{2,1,0:T(8,128)S(1)}, f...) custom-call(s32[2]{0:T(128)S(1)} %pad_add_fusion.here_ref, ...), custom_call_target="tpu_custom_call", output_to_operand_aliasing={{0}: (1, {}), {1}: (4, {}), {2}: (5, {}), {3}: (6, {}), {4}... | custom-call | flops 3623878656 | tf_op jit(solution)/shard_map/stage/pallas_call | solution.py:334
  90.8 0.3 collective-permute-done.20.refs_1_
  91.1 1.6 %collective-permute-done.21.rest_1_ = bf16[1,200,768]{2,1,0:T(8,128)(2,1)S(1)} collective-permute-done((bf16[1,200,768]{2,1,0:T(8,128)(2,1)S(1)}, bf16[1,200,768]{2,1,0:T(8,128)(2,1)S(1)}, u32[]{:S(2)}, u32[]{:S(2)}) %collective-permute-start.21) | collective-permute-done | bytes 307232 | tf_op jit(solution)/shard_map/ppermute | solution.py:244
  92.7 2.1 %stage.7 = (f32[8,128]{1,0:T(8,128)S(1)}, f32[8,1,192]{2,1,0:T(1,128)S(1)}, bf16[8,4,192,768]{3,2,1,0:T(8,128)(2,1)S(1)}, f32[8,8,192]{2,1,0:T(8,128)S(1)}, f32[...) custom-call(s32[2]{0:T(128)S(1)} %pad_add_fusion.here_ref, ...), custom_call_target="tpu_custom_call", output_to_operand_aliasing={{0}: (1, {}), {2}: (4, {}), {3}: (5, {}), {4}: (6, {}), {5}... | custom-call | flops 3623878656 | tf_op jit(solution)/shard_map/stage/pallas_call | solution.py:334
  94.8 10.9 %all_to_all.5.score_ref = f32[8,1,192]{2,1,0:T(1,128)S(1)} all-to-all(f32[8,1,192]{2,1,0:T(1,128)S(1)} %get-tuple-element.118), channel_id=1, replica_groups=mesh['grp'=8,'blk'=4] {'grp'}, dimensions={0} | all-to-all | bytes 12288 | tf_op jit(solution)/shard_map/all_to_all | solution.py:375
  105.7 0.8 unpack.1
  (32 shorter events, 0.8 us)
Async XLA Ops:
  0.1 1.7 %copy-start = (bf16[1536,768]{1,0:T(8,128)(2,1)S(1)}, bf16[1536,768]{1,0:T(8,128)(2,1)}, u32[]{:S(2)}) copy-start(bf16[1536,768]{1,0:T(8,128)(2,1)} %emb_ref.1) | copy-start | bytes 7077892
  1.7 0.7 copy-start.1
  6.3 18.6 %collective-permute-start = (bf16[208,768]{1,0:T(8,128)(2,1)S(1)}, bf16[208,768]{1,0:T(8,128)(2,1)S(1)}, u32[]{:S(2)}, u32[]{:S(2)}) collective-permute-start(bf16[208,768]{1,0:T(8,128)(2,1)S(1)} %get-tuple-element.64), channel_id=1, source_target_pairs={{0,16},{4,20},{8,24},{12,28},{16,0},{20,4},{24,8},{28,12},{1,17},{... | collective-permute-start | bytes 958472 | tf_op jit(solution)/shard_map/ppermute | solution.py:244
  10.4 14.7 %collective-permute-start.1 = (bf16[208,768]{1,0:T(8,128)(2,1)S(1)}, bf16[208,768]{1,0:T(8,128)(2,1)S(1)}, u32[]{:S(2)}, u32[]{:S(2)}) collective-permute-start(bf16[208,768]{1,0:T(8,128)(2,1)S(1)} %get-tuple-element.65), channel_id=1, source_target_pairs={{0,8},{4,12},{8,0},{12,4},{16,24},{20,28},{24,16},{28,20},{1,9},{5... | collective-permute-start | bytes 958472 | tf_op jit(solution)/shard_map/ppermute | solution.py:244
  12.0 0.7 copy-start.2
  16.2 8.5 %collective-permute-start.2 = (bf16[1,200,768]{2,1,0:T(8,128)(2,1)S(1)}, bf16[1,200,768]{2,1,0:T(8,128)(2,1)S(1)}, u32[]{:S(2)}, u32[]{:S(2)}) collective-permute-start(bf16[1,200,768]{2,1,0:T(8,128)(2,1)S(1)} %bitcast.6), channel_id=1, source_target_pairs={{0,2},{1,3},{2,0},{3,1},{4,6},{5,7},{6,4},{7,5},{8,10},{9,11},{10,... | collective-permute-start | bytes 921608 | tf_op jit(solution)/shard_map/ppermute | solution.py:244
  17.7 6.9 %collective-permute-start.3 = (bf16[1,200,768]{2,1,0:T(8,128)(2,1)S(1)}, bf16[1,200,768]{2,1,0:T(8,128)(2,1)S(1)}, u32[]{:S(2)}, u32[]{:S(2)}) collective-permute-start(bf16[1,200,768]{2,1,0:T(8,128)(2,1)S(1)} %bitcast.7), channel_id=1, source_target_pairs={{0,1},{1,0},{2,3},{3,2},{4,5},{5,4},{6,7},{7,6},{8,9},{9,8},{10,11... | collective-permute-start | bytes 921608 | tf_op jit(solution)/shard_map/ppermute | solution.py:244
  25.1 19.7 %collective-permute-start.6 = (bf16[2,200,768]{2,1,0:T(8,128)(2,1)S(1)}, bf16[2,200,768]{2,1,0:T(8,128)(2,1)S(1)}, u32[]{:S(2)}, u32[]{:S(2)}) collective-permute-start(bf16[2,200,768]{2,1,0:T(8,128)(2,1)S(1)} %get-tuple-element.75.rest_4_), channel_id=1, source_target_pairs={{0,2},{1,3},{2,0},{3,1},{4,6},{5,7},{6,4},{7,5},{8,10},{9,11},{10,... | collective-permute-start | bytes 1843208 | tf_op jit(solution)/shard_map/ppermute | solution.py:244
  26.7 18.1 %collective-permute-start.7 = (bf16[2,200,768]{2,1,0:T(8,128)(2,1)S(1)}, bf16[2,200,768]{2,1,0:T(8,128)(2,1)S(1)}, u32[]{:S(2)}, u32[]{:S(2)}) collective-permute-start(bf16[2,200,768]{2,1,0:T(8,128)(2,1)S(1)} %get-tuple-element.75.rest_4_), channel_id=1, source_target_pairs={{0,1},{1,0},{2,3},{3,2},{4,5},{5,4},{6,7},{7,6},{8,9},{9,8},{10,11... | collective-permute-start | bytes 1843208 | tf_op jit(solution)/shard_map/ppermute | solution.py:244
  26.7 18.1 %collective-permute-start.4 = (bf16[200,768]{1,0:T(8,128)(2,1)S(1)}, bf16[200,768]{1,0:T(8,128)(2,1)S(1)}, u32[]{:S(2)}, u32[]{:S(2)}) collective-permute-start(bf16[200,768]{1,0:T(8,128)(2,1)S(1)} %get-tuple-element.72), channel_id=1, source_target_pairs={{0,20},{4,16},{8,28},{12,24},{16,4},{20,0},{24,12},{28,8},{1,21},{... | collective-permute-start | bytes 921608 | tf_op jit(solution)/shard_map/ppermute | solution.py:244
  29.0 15.8 %collective-permute-start.5 = (bf16[200,768]{1,0:T(8,128)(2,1)S(1)}, bf16[200,768]{1,0:T(8,128)(2,1)S(1)}, u32[]{:S(2)}, u32[]{:S(2)}) collective-permute-start(bf16[200,768]{1,0:T(8,128)(2,1)S(1)} %get-tuple-element.73), channel_id=1, source_target_pairs={{0,4},{4,0},{8,12},{12,8},{16,20},{20,16},{24,28},{28,24},{1,5},{5... | collective-permute-start | bytes 921608 | tf_op jit(solution)/shard_map/ppermute | solution.py:244
  29.5 15.3 %collective-permute-start.8 = (bf16[1,200,768]{2,1,0:T(8,128)(2,1)S(1)}, bf16[1,200,768]{2,1,0:T(8,128)(2,1)S(1)}, u32[]{:S(2)}, u32[]{:S(2)}) collective-permute-start(bf16[1,200,768]{2,1,0:T(8,128)(2,1)S(1)} %get-tuple-element.76.rest_2_), channel_id=1, source_target_pairs={{0,1},{1,0},{2,3},{3,2},{4,5},{5,4},{6,7},{7,6},{8,9},{9,8},{10,11... | collective-permute-start | bytes 921608 | tf_op jit(solution)/shard_map/ppermute | solution.py:244
  44.9 19.9 %collective-permute-start.11 = (bf16[2,200,768]{2,1,0:T(8,128)(2,1)S(1)}, bf16[2,200,768]{2,1,0:T(8,128)(2,1)S(1)}, u32[]{:S(2)}, u32[]{:S(2)}) collective-permute-start(bf16[2,200,768]{2,1,0:T(8,128)(2,1)S(1)} %get-tuple-element.82.rest_8_), channel_id=1, source_target_pairs={{0,2},{1,3},{2,0},{3,1},{4,6},{5,7},{6,4},{7,5},{8,10},{9,11},{10,... | collective-permute-start | bytes 1843208 | tf_op jit(solution)/shard_map/ppermute | solution.py:244
  45.4 19.4 %collective-permute-start.12 = (bf16[2,200,768]{2,1,0:T(8,128)(2,1)S(1)}, bf16[2,200,768]{2,1,0:T(8,128)(2,1)S(1)}, u32[]{:S(2)}, u32[]{:S(2)}) collective-permute-start(bf16[2,200,768]{2,1,0:T(8,128)(2,1)S(1)} %get-tuple-element.82.rest_8_), channel_id=1, source_target_pairs={{0,1},{1,0},{2,3},{3,2},{4,5},{5,4},{6,7},{7,6},{8,9},{9,8},{10,11... | collective-permute-start | bytes 1843208 | tf_op jit(solution)/shard_map/ppermute | solution.py:244
  45.4 19.4 %collective-permute-start.13 = (bf16[2,200,768]{2,1,0:T(8,128)(2,1)S(1)}, bf16[2,200,768]{2,1,0:T(8,128)(2,1)S(1)}, u32[]{:S(2)}, u32[]{:S(2)}) collective-permute-start(bf16[2,200,768]{2,1,0:T(8,128)(2,1)S(1)} %get-tuple-element.83.rest_6_), channel_id=1, source_target_pairs={{0,1},{1,0},{2,3},{3,2},{4,5},{5,4},{6,7},{7,6},{8,9},{9,8},{10,11... | collective-permute-start | bytes 1843208 | tf_op jit(solution)/shard_map/ppermute | solution.py:244
  45.9 18.9 %collective-permute-start.9 = (bf16[208,768]{1,0:T(8,128)(2,1)S(1)}, bf16[208,768]{1,0:T(8,128)(2,1)S(1)}, u32[]{:S(2)}, u32[]{:S(2)}) collective-permute-start(bf16[208,768]{1,0:T(8,128)(2,1)S(1)} %get-tuple-element.79), channel_id=1, source_target_pairs={{0,24},{4,28},{8,16},{12,20},{16,8},{20,12},{24,0},{28,4},{1,25},{... | collective-permute-start | bytes 958472 | tf_op jit(solution)/shard_map/ppermute | solution.py:244
  48.6 16.2 %collective-permute-start.10 = (bf16[200,768]{1,0:T(8,128)(2,1)S(1)}, bf16[200,768]{1,0:T(8,128)(2,1)S(1)}, u32[]{:S(2)}, u32[]{:S(2)}) collective-permute-start(bf16[200,768]{1,0:T(8,128)(2,1)S(1)} %get-tuple-element.80), channel_id=1, source_target_pairs={{0,12},{4,8},{8,4},{12,0},{16,28},{20,24},{24,20},{28,16},{1,13},{... | collective-permute-start | bytes 921608 | tf_op jit(solution)/shard_map/ppermute | solution.py:244
  64.9 4.4 %collective-permute-start.15 = (bf16[2,200,768]{2,1,0:T(8,128)(2,1)S(1)}, bf16[2,200,768]{2,1,0:T(8,128)(2,1)S(1)}, u32[]{:S(2)}, u32[]{:S(2)}) collective-permute-start(bf16[2,200,768]{2,1,0:T(8,128)(2,1)S(1)} %get-tuple-element.92.rest_10_), channel_id=1, source_target_pairs={{0,1},{1,0},{2,3},{3,2},{4,5},{5,4},{6,7},{7,6},{8,9},{9,8},{10,11... | collective-permute-start | bytes 1843208 | tf_op jit(solution)/shard_map/ppermute | solution.py:244
  65.0 16.3 %collective-permute-start.16 = (bf16[2,200,768]{2,1,0:T(8,128)(2,1)S(1)}, bf16[2,200,768]{2,1,0:T(8,128)(2,1)S(1)}, u32[]{:S(2)}, u32[]{:S(2)}) collective-permute-start(bf16[2,200,768]{2,1,0:T(8,128)(2,1)S(1)} %get-tuple-element.94.rest_0_), channel_id=1, source_target_pairs={{0,2},{1,3},{2,0},{3,1},{4,6},{5,7},{6,4},{7,5},{8,10},{9,11},{10,... | collective-permute-start | bytes 1843208 | tf_op jit(solution)/shard_map/ppermute | solution.py:244
  66.6 14.7 %collective-permute-start.17 = (bf16[2,200,768]{2,1,0:T(8,128)(2,1)S(1)}, bf16[2,200,768]{2,1,0:T(8,128)(2,1)S(1)}, u32[]{:S(2)}, u32[]{:S(2)}) collective-permute-start(bf16[2,200,768]{2,1,0:T(8,128)(2,1)S(1)} %get-tuple-element.94.rest_0_), channel_id=1, source_target_pairs={{0,1},{1,0},{2,3},{3,2},{4,5},{5,4},{6,7},{7,6},{8,9},{9,8},{10,11... | collective-permute-start | bytes 1843208 | tf_op jit(solution)/shard_map/ppermute | solution.py:244
  66.7 12.3 %collective-permute-start.14 = (bf16[200,768]{1,0:T(8,128)(2,1)S(1)}, bf16[200,768]{1,0:T(8,128)(2,1)S(1)}, u32[]{:S(2)}, u32[]{:S(2)}) collective-permute-start(bf16[200,768]{1,0:T(8,128)(2,1)S(1)} %get-tuple-element.85), channel_id=1, source_target_pairs={{0,28},{4,24},{8,20},{12,16},{16,12},{20,8},{24,4},{28,0},{1,29},{... | collective-permute-start | bytes 921608 | tf_op jit(solution)/shard_map/ppermute | solution.py:244
  81.3 2.1 %collective-permute-start.18 = (bf16[2,200,768]{2,1,0:T(8,128)(2,1)S(1)}, bf16[2,200,768]{2,1,0:T(8,128)(2,1)S(1)}, u32[]{:S(2)}, u32[]{:S(2)}) collective-permute-start(bf16[2,200,768]{2,1,0:T(8,128)(2,1)S(1)} %get-tuple-element.97.rest_2_), channel_id=1, source_target_pairs={{0,1},{1,0},{2,3},{3,2},{4,5},{5,4},{6,7},{7,6},{8,9},{9,8},{10,11... | collective-permute-start | bytes 1843208 | tf_op jit(solution)/shard_map/ppermute | solution.py:244
  81.4 7.3 %collective-permute-start.19 = (bf16[1,200,768]{2,1,0:T(8,128)(2,1)S(1)}, bf16[1,200,768]{2,1,0:T(8,128)(2,1)S(1)}, u32[]{:S(2)}, u32[]{:S(2)}) collective-permute-start(bf16[1,200,768]{2,1,0:T(8,128)(2,1)S(1)} %get-tuple-element.104.rest_0_), channel_id=1, source_target_pairs={{0,1},{1,0},{2,3},{3,2},{4,5},{5,4},{6,7},{7,6},{8,9},{9,8},{10,11... | collective-permute-start | bytes 921608 | tf_op jit(solution)/shard_map/ppermute | solution.py:244
  81.9 9.3 %collective-permute-start.20 = (bf16[1,200,768]{2,1,0:T(8,128)(2,1)S(1)}, bf16[1,200,768]{2,1,0:T(8,128)(2,1)S(1)}, u32[]{:S(2)}, u32[]{:S(2)}) collective-permute-start(bf16[1,200,768]{2,1,0:T(8,128)(2,1)S(1)} %get-tuple-element.104.rest_0_), channel_id=1, source_target_pairs={{0,2},{1,3},{2,0},{3,1},{4,6},{5,7},{6,4},{7,5},{8,10},{9,11},{10,... | collective-permute-start | bytes 921608 | tf_op jit(solution)/shard_map/ppermute | solution.py:244
  91.1 1.6 %collective-permute-start.21 = (bf16[1,200,768]{2,1,0:T(8,128)(2,1)S(1)}, bf16[1,200,768]{2,1,0:T(8,128)(2,1)S(1)}, u32[]{:S(2)}, u32[]{:S(2)}) collective-permute-start(bf16[1,200,768]{2,1,0:T(8,128)(2,1)S(1)} %get-tuple-element.112.rest_0_), channel_id=1, source_target_pairs={{0,1},{1,0},{2,3},{3,2},{4,5},{5,4},{6,7},{7,6},{8,9},{9,8},{10,11... | collective-permute-start | bytes 921608 | tf_op jit(solution)/shard_map/ppermute | solution.py:244
